TPU v7x, 32 devices: a whole 2x2x4 slice. The times are simulated.
32 devices in a mesh: dp: 4 (over z), seq: 8 (over y, x, core).
Axes of the slice: x: 2, y: 2, z: 4, core: 2. Of those that a mesh axis runs over, the one named last changes fastest.
Arguments:
- latents: bfloat16 [13056, 768], P(('dp', 'seq')), may hold values from -6 to 6
- clip_ids: int32 [13056], P('dp'), may hold values from 0 to 31, as said below
- restore: int32 [13056], P('dp'), may hold values from 0 to 2047
- counts: int32 [32], P('dp'), may hold values from 51 to 408, as said below
- embed_weight: bfloat16 [768, 512], replicated, may hold values from -0.21875 to 0.21875
- embed_bias: bfloat16 [512], replicated, may hold values from -3 to 3
- mask_token: bfloat16 [512], replicated, may hold values from -4 to 4
- first_gain: bfloat16 [512], replicated, may hold values from 0.099609375 to 1.8984375
- first_shift: bfloat16 [512], replicated, may hold values from -2 to 2
- joint_weight: bfloat16 [512, 1536], replicated, may hold values from -0.375 to 0.375
- query_bias: bfloat16 [512], replicated, may hold values from -3 to 3
- value_bias: bfloat16 [512], replicated, may hold values from -3 to 3
- output_weight: bfloat16 [512, 512], replicated, may hold values from -1.5 to 1.5
- output_bias: bfloat16 [512], replicated, may hold values from -2 to 2
- second_gain: bfloat16 [512], replicated, may hold values from 0.099609375 to 1.8984375
- second_shift: bfloat16 [512], replicated, may hold values from -2 to 2
- expand_weight: bfloat16 [512, 2048], replicated, may hold values from -0.25 to 0.25
- expand_bias: bfloat16 [2048], replicated, may hold values from -2 to 2
- contract_weight: bfloat16 [2048, 512], replicated, may hold values from -0.125 to 0.125
- contract_bias: bfloat16 [512], replicated, may hold values from -2 to 2
- cotangent: bfloat16 [32, 2048, 512], P('dp', 'seq'), may hold values from -6 to 6
Outputs:
- decoded: bfloat16 [32, 2048, 512], P('dp', 'seq')
- latent_grad: bfloat16 [13056, 768], P(('dp', 'seq'))
- grad_embed_weight: float32 [768, 512], replicated
- grad_embed_bias: float32 [512], replicated
- grad_mask_token: float32 [512], replicated
- grad_first_gain: float32 [512], replicated
- grad_first_shift: float32 [512], replicated
- grad_joint_weight: float32 [512, 1536], replicated
- grad_query_bias: float32 [512], replicated
- grad_value_bias: float32 [512], replicated
- grad_output_weight: float32 [512, 512], replicated
- grad_output_bias: float32 [512], replicated
- grad_second_gain: float32 [512], replicated
- grad_second_shift: float32 [512], replicated
- grad_expand_weight: float32 [512, 2048], replicated
- grad_expand_bias: float32 [2048], replicated
- grad_contract_weight: float32 [2048, 512], replicated
- grad_contract_bias: float32 [512], replicated
Inputs may be any that keep to these rules, and one draw needn't show every extreme that they name: Only the first counts rows of each device's 408 row slots are visible latents; the others are to be ignored. In every dp group some device has exactly 408. `clip_ids`: every row's clip is one of the 8 clips of its dp index, dp index times 8 onward. Over the live rows the pairs (clip, position) are all different, and of one device's live rows at most 51 have restore // 256 equal to one value; this bound is reached on every dp index.
All inputs are finite; a program needn't handle non-finite values.
Results may differ from a plain program's by a relative error of at most 0.018.
Values may be sent and summed in bfloat16 or wider, within the bound.
A program may use at most 320 MiB of HBM per device.

v0:
```python
from functools import partial
import math

import jax
import jax.numpy as jnp
from jax import lax
from jax.sharding import PartitionSpec as P

HEADS = 16
HEAD_DIM = 32


epsilon = 1e-06


def layer_norm(values, gain, shift):
    center = values - jnp.mean(values, axis=-1, keepdims=True)
    spread = jnp.mean(center * center, axis=-1, keepdims=True)
    return center * lax.rsqrt(spread + epsilon) * gain + shift


def sinusoid(places, table_width):
    half_width = table_width // 2
    frequency = jnp.exp(-math.log(10000.0) * jnp.arange(half_width, dtype=jnp.float32) / half_width)
    angles = places.astype(jnp.float32)[:, None] * frequency[None, :]
    return jnp.concatenate([jnp.sin(angles), jnp.cos(angles)], axis=1)


def plain_dot(left, right):
    return jnp.dot(left, right, preferred_element_type=jnp.float32)


def lead_dot(left, right):
    return lax.dot_general(
        left, right, (((0,), (0,)), ((), ())), preferred_element_type=jnp.float32
    )


def trail_dot(left, right):
    return lax.dot_general(
        left, right, (((1,), (1,)), ((), ())), preferred_element_type=jnp.float32
    )


def column_sum(values):
    return jnp.sum(values.astype(jnp.float32), axis=0)


def split_heads(matrix):
    return matrix.reshape(matrix.shape[0], HEADS, HEAD_DIM)


def attend_clip(inputs):
    query_rows, key_rows, value_rows = inputs
    scores = jnp.einsum(
        "qhd,khd->hqk",
        split_heads(query_rows),
        split_heads(key_rows),
        preferred_element_type=jnp.float32,
    ) * HEAD_DIM ** (-0.5)
    highest_score = jnp.max(scores, axis=-1, keepdims=True)
    raised = jnp.exp(scores - highest_score)
    totals = jnp.sum(raised, axis=-1, keepdims=True)
    attention_low = (raised / totals).astype(jnp.bfloat16)
    mixed = jnp.einsum(
        "hqk,khd->qhd", attention_low, split_heads(value_rows), preferred_element_type=jnp.float32
    )
    log_total = (highest_score + jnp.log(totals))[..., 0]
    return (mixed.reshape(query_rows.shape[0], -1).astype(jnp.bfloat16), log_total)


def query_backward(inputs):
    query_rows, key_rows, value_rows, log_total, grad_rows = inputs
    query_heads = split_heads(query_rows)
    key_heads = split_heads(key_rows)
    grad_heads = split_heads(grad_rows)
    scores = jnp.einsum(
        "qhd,khd->hqk", query_heads, key_heads, preferred_element_type=jnp.float32
    ) * HEAD_DIM ** (-0.5)
    attention = jnp.exp(scores - log_total[..., None])
    grad_attention = jnp.einsum(
        "qhd,khd->hqk", grad_heads, split_heads(value_rows), preferred_element_type=jnp.float32
    )
    row_inner = jnp.sum(attention * grad_attention, axis=-1)
    grad_scores = (attention * (grad_attention - row_inner[..., None])).astype(jnp.bfloat16)
    grad_query = jnp.einsum(
        "hqk,khd->qhd", grad_scores, key_heads, preferred_element_type=jnp.float32
    ) * HEAD_DIM ** (-0.5)
    return (grad_query.reshape(query_rows.shape[0], -1), row_inner)


def key_backward(inputs):
    all_query, all_grad, all_log, all_inner, own_key, own_value = inputs
    query_heads = split_heads(all_query)
    grad_heads = split_heads(all_grad)
    scores = jnp.einsum(
        "qhd,khd->hqk", query_heads, split_heads(own_key), preferred_element_type=jnp.float32
    ) * HEAD_DIM ** (-0.5)
    attention = jnp.exp(scores - all_log[..., None])
    grad_attention = jnp.einsum(
        "qhd,khd->hqk", grad_heads, split_heads(own_value), preferred_element_type=jnp.float32
    )
    grad_scores = (attention * (grad_attention - all_inner[..., None])).astype(jnp.bfloat16)
    grad_key = jnp.einsum(
        "hqk,qhd->khd", grad_scores, query_heads, preferred_element_type=jnp.float32
    ) * HEAD_DIM ** (-0.5)
    grad_value = jnp.einsum(
        "hqk,qhd->khd",
        attention.astype(jnp.bfloat16),
        grad_heads,
        preferred_element_type=jnp.float32,
    )
    return (grad_key.reshape(own_key.shape[0], -1), grad_value.reshape(own_key.shape[0], -1))


def body(
    latents,
    clip_ids,
    restore,
    counts,
    embed_weight,
    embed_bias,
    mask_token,
    first_gain,
    first_shift,
    joint_weight,
    query_bias,
    value_bias,
    output_weight,
    output_bias,
    second_gain,
    second_shift,
    expand_weight,
    expand_bias,
    contract_weight,
    contract_bias,
    cotangent,
):
    splits = lax.axis_size("seq")
    seq_index = lax.axis_index("seq")
    capacity = latents.shape[0]
    slot_count = capacity // splits
    clip_count = cotangent.shape[0]
    clip_share = cotangent.shape[1]
    model_width = cotangent.shape[2]
    local_rows = clip_count * clip_share
    slot_total = splits * slot_count
    group_clip = (clip_ids % clip_count).reshape(splits, capacity)
    group_place = restore.reshape(splits, capacity)
    group_live = jnp.arange(capacity, dtype=jnp.int32)[None, :] < counts[:, None]
    group_dest = group_place // clip_share
    arriving = group_live & (group_dest == seq_index)
    arrive_rank = jnp.cumsum(arriving.astype(jnp.int32), axis=1) - 1
    arrive_slot = jnp.arange(splits, dtype=jnp.int32)[:, None] * slot_count + arrive_rank
    arrive_row = group_clip * clip_share + group_place % clip_share
    slot_index = jnp.where(arriving, arrive_slot, slot_total).reshape(-1)
    slot_target = (
        jnp.full((slot_total,), -1, jnp.int32)
        .at[slot_index]
        .set(arrive_row.reshape(-1), mode="drop")
    )
    restore_map = (jnp.arange(local_rows, dtype=jnp.int32)[:, None] == slot_target[None, :]).astype(
        jnp.bfloat16
    )
    own_live = lax.dynamic_index_in_dim(group_live, seq_index, 0, keepdims=False)
    own_dest = lax.dynamic_index_in_dim(group_dest, seq_index, 0, keepdims=False)
    peer_index = jnp.arange(splits, dtype=jnp.int32)
    to_peer = own_live[:, None] & (own_dest[:, None] == peer_index[None, :])
    peer_rank = jnp.cumsum(to_peer.astype(jnp.int32), axis=0) - 1
    own_slot = jnp.sum(jnp.where(to_peer, peer_index[None, :] * slot_count + peer_rank, 0), axis=1)
    send_map = (
        (jnp.arange(slot_total, dtype=jnp.int32)[:, None] == own_slot[None, :]) & own_live[None, :]
    ).astype(jnp.bfloat16)
    embedded = (plain_dot(latents, embed_weight) + embed_bias.astype(jnp.float32)).astype(
        jnp.bfloat16
    )
    outgoing = (
        plain_dot(send_map, embedded).astype(jnp.bfloat16).reshape(splits, slot_count, model_width)
    )
    incoming = lax.all_to_all(outgoing, "seq", split_axis=0, concat_axis=0, tiled=True)
    placed = plain_dot(restore_map, incoming.reshape(slot_total, model_width))
    visible_mask = jnp.sum(restore_map, axis=1, dtype=jnp.float32)
    places = seq_index * clip_share + jnp.arange(local_rows, dtype=jnp.int32) % clip_share
    stream = (
        placed
        + (1.0 - visible_mask)[:, None] * mask_token.astype(jnp.float32)[None, :]
        + sinusoid(places, model_width)
    )
    first_normed, first_back = jax.vjp(
        layer_norm, stream, first_gain.astype(jnp.float32), first_shift.astype(jnp.float32)
    )
    first_low = first_normed.astype(jnp.bfloat16)
    joint = plain_dot(first_low, joint_weight)
    query_rows = (joint[:, :model_width] + query_bias.astype(jnp.float32)).astype(jnp.bfloat16)
    key_rows = joint[:, model_width : 2 * model_width].astype(jnp.bfloat16)
    value_rows = (joint[:, 2 * model_width :] + value_bias.astype(jnp.float32)).astype(jnp.bfloat16)
    query_clips = query_rows.reshape(clip_count, clip_share, model_width)
    key_clips = key_rows.reshape(clip_count, clip_share, model_width)
    value_clips = value_rows.reshape(clip_count, clip_share, model_width)
    key_all, value_all = (
        lax.all_gather(key_clips, "seq", axis=1, tiled=True),
        lax.all_gather(value_clips, "seq", axis=1, tiled=True),
    )
    attended_clips, log_total = lax.map(attend_clip, (query_clips, key_all, value_all))
    attended = attended_clips.reshape(local_rows, model_width)
    middle = stream + plain_dot(attended, output_weight) + output_bias.astype(jnp.float32)
    second_normed, second_back = jax.vjp(
        layer_norm, middle, second_gain.astype(jnp.float32), second_shift.astype(jnp.float32)
    )
    second_low = second_normed.astype(jnp.bfloat16)
    hidden = plain_dot(second_low, expand_weight) + expand_bias.astype(jnp.float32)
    active, gelu_back = jax.vjp(partial(jax.nn.gelu, approximate=False), hidden)
    active_low = active.astype(jnp.bfloat16)
    output_rows = (
        middle + plain_dot(active_low, contract_weight) + contract_bias.astype(jnp.float32)
    )
    decoded = output_rows.astype(jnp.bfloat16).reshape(clip_count, clip_share, model_width)
    grad_output = cotangent.reshape(local_rows, model_width)
    grad_contract = lead_dot(active_low, grad_output)
    grad_contract_bias = column_sum(grad_output)
    grad_hidden = gelu_back(trail_dot(grad_output, contract_weight))[0].astype(jnp.bfloat16)
    grad_expand = lead_dot(second_low, grad_hidden)
    grad_expand_bias = column_sum(grad_hidden)
    grad_middle_norm, grad_second_gain, grad_second_shift = second_back(
        trail_dot(grad_hidden, expand_weight)
    )
    grad_middle = grad_output.astype(jnp.float32) + grad_middle_norm
    grad_branch = grad_middle.astype(jnp.bfloat16)
    grad_output_weight = lead_dot(attended, grad_branch)
    grad_output_bias = column_sum(grad_branch)
    grad_attended = trail_dot(grad_branch, output_weight).astype(jnp.bfloat16)
    grad_clips = grad_attended.reshape(clip_count, clip_share, model_width)
    grad_query_clips, row_inner = lax.map(
        query_backward, (query_clips, key_all, value_all, log_total, grad_clips)
    )
    part_key, part_value = lax.map(
        key_backward, (query_clips, grad_clips, log_total, row_inner, key_all, value_all)
    )
    owned = (
        lax.psum_scatter(
            jnp.concatenate([part_key, part_value], axis=2).transpose(1, 0, 2).astype(jnp.bfloat16),
            "seq",
            scatter_dimension=0,
            tiled=True,
        )
        .astype(jnp.float32)
        .transpose(1, 0, 2)
    )
    grad_key_own = owned[:, :, :model_width]
    grad_value_own = owned[:, :, model_width:]
    grad_joint = jnp.concatenate(
        [
            grad_query_clips.reshape(local_rows, model_width).astype(jnp.bfloat16),
            grad_key_own.reshape(local_rows, model_width).astype(jnp.bfloat16),
            grad_value_own.reshape(local_rows, model_width).astype(jnp.bfloat16),
        ],
        axis=1,
    )
    grad_joint_weight = lead_dot(first_low, grad_joint)
    grad_query_bias = column_sum(grad_joint[:, :model_width])
    grad_value_bias = column_sum(grad_joint[:, 2 * model_width :])
    grad_stream_norm, grad_first_gain, grad_first_shift = first_back(
        trail_dot(grad_joint, joint_weight)
    )
    grad_stream = grad_middle + grad_stream_norm
    grad_mask = jnp.sum((1.0 - visible_mask)[:, None] * grad_stream, axis=0)
    back_rows = lead_dot(restore_map, grad_stream.astype(jnp.bfloat16)).astype(jnp.bfloat16)
    back_rows = back_rows.reshape(splits, slot_count, model_width)
    returned = lax.all_to_all(back_rows, "seq", split_axis=0, concat_axis=0, tiled=True)
    grad_embedded = lead_dot(send_map, returned.reshape(slot_total, model_width)).astype(
        jnp.bfloat16
    )
    latent_grad = trail_dot(grad_embedded, embed_weight).astype(jnp.bfloat16)
    grad_embed_weight = lead_dot(latents, grad_embedded)
    grad_embed_bias = column_sum(grad_embedded)
    summed = lax.psum(
        (
            grad_embed_weight,
            grad_embed_bias,
            grad_mask,
            grad_first_gain,
            grad_first_shift,
            grad_joint_weight,
            grad_query_bias,
            grad_value_bias,
            grad_output_weight,
            grad_output_bias,
            grad_second_gain,
            grad_second_shift,
            grad_expand,
            grad_expand_bias,
            grad_contract,
            grad_contract_bias,
        ),
        ("dp", "seq"),
    )
    return (decoded, latent_grad) + tuple(summed)


def solution(mesh):
    placed = (
        P(("dp", "seq"), None),
        P("dp"),
        P("dp"),
        P("dp"),
        P(),
        P(),
        P(),
        P(),
        P(),
        P(),
        P(),
        P(),
        P(),
        P(),
        P(),
        P(),
        P(),
        P(),
        P(),
        P(),
        P("dp", "seq", None),
    )
    return jax.shard_map(
        body,
        mesh=mesh,
        in_specs=placed,
        out_specs=(
            P("dp", "seq", None),
            P(("dp", "seq"), None),
            P(),
            P(),
            P(),
            P(),
            P(),
            P(),
            P(),
            P(),
            P(),
            P(),
            P(),
            P(),
            P(),
            P(),
            P(),
            P(),
        ),
        check_vma=False,
    )
```

profile of v0, /device:TPU:0, one launch (start us, length us, event | category | flops | bytes accessed | tf_op | source)
XLA Modules:
  0.0 2252.3 jit_solution(9829885538139009058)
XLA Ops:
  81.2 80.3 %all-gather.3.cloned.1.call-done = bf16[8,2048,512]{1,2,0:T(8,128)(2,1)} async-done(((bf16[8,256,512]{1,2,0:T(8,128)(2,1)}), bf16[8,2048,512]{1,2,0:T(8,128)(2,1)}) %all-gather.3.cloned.1.call-update) | async-done | bytes 16777232 | tf_op jit(solution)/shard_map/all_gather | solution.py:202
  161.6 95.0 %all-gather.5.cloned.1.call-done = bf16[8,2048,512]{1,2,0:T(8,128)(2,1)} async-done(((bf16[8,256,512]{1,2,0:T(8,128)(2,1)}), bf16[8,2048,512]{1,2,0:T(8,128)(2,1)}) %all-gather.5.cloned.1.call-update) | async-done | bytes 16777232 | tf_op jit(solution)/shard_map/all_gather | solution.py:201
  256.6 380.6 %while.36 = (s32[]{:T(128)}, bf16[8,256,512]{2,1,0:T(8,128)(2,1)}, f32[8,16,256]{2,1,0:T(8,128)S(1)}, bf16[8,2048,512]{1,2,0:T(8,128)(2,1)}, bf16[8,256,512]{1,2...) while((s32[]{:T(128)}, bf16[8,256,512]{2,1,0:T(8,128)(2,1)}, f32[8,16,256]{2,1,0:T(8,128)S(1)}, ...), condition=%wide.region_12.13_spmd, body=%wide.region_9.12_spmd.sunk | while | flops 1149366272 | bytes 115475024 | solution.py:204
  642.6 44.1 %multiply_convert_fusion.5 = (bf16[2048,2048]{1,0:T(8,128)(2,1)}, f32[2048,2048]{1,0:T(8,128)}, f32[2048,2048]{1,0:T(8,128)}) fusion(f32[2048]{0:T(1024)S(1)} %copy-done.46, bf16[512,2048]{1,0:T(8,128)(2,1)S(1)} %copy-done, f32[2048,512]{1,0:T(8,128)S(1)} %get-tuple-element.377, f32[512]{0:T(512)S(1)} %copy-done.62, f32[512]{0:T(512)S(1)} %copy-done.50, ...), kind=kOutput, calls=%fused_computation.49 | convolution fusion | flops 4577034240 | bytes 48263168 | tf_op jit(solution)/shard_map/dot_general | solution.py:30
  686.7 22.3 convert_reduce_fusion
  727.9 508.4 %while.37 = (s32[]{:T(128)}, bf16[8,256,512]{2,1,0:T(8,128)(2,1)}, f32[8,16,256]{2,1,0:T(8,128)S(1)}, bf16[8,2048,512]{1,2,0:T(8,128)(2,1)}, bf16[8,256,512]{1,2...) while((s32[]{:T(128)}, bf16[8,256,512]{2,1,0:T(8,128)(2,1)}, ...), condition=%wide.region_19.20_spmd, body=%wide.region_17.19_spmd.sunk | while | flops 1686368256 | bytes 185467504 | solution.py:233
  745.7 22.6 %multiply_reduce_fusion.12 = (f32[16,256]{1,0:T(8,128)S(1)}, f32[16,256,2048]{2,1,0:T(8,128)}) fusion(f32[16,256,2048]{2,1,0:T(8,128)} %fusion.157, f32[16,256]{1,0:T(8,128)S(1)} %dynamic-slice_bitcast_fusion.5, bf16[256,16,32]{0,2,1:T(8,128)(2,1)S(1)} %bitcast.184, bf16[2048,16,32]{0,2,1:T(8,128)(2,1)S(1)} %bitcast.174), kind=kOutput, calls=%fused_computation.14.clone.1 | convolution fusion | flops 570421248 | bytes 69500928 | tf_op jit(solution)/shard_map/while/body/eval_jaxpr/qhd,khd->hqk/dot_general | solution.py:81
  768.2 22.5 fusion.158
  809.2 22.6 %multiply_reduce_fusion.12 = (f32[16,256]{1,0:T(8,128)S(1)}, f32[16,256,2048]{2,1,0:T(8,128)}) fusion(f32[16,256,2048]{2,1,0:T(8,128)} %fusion.157, f32[16,256]{1,0:T(8,128)S(1)} %dynamic-slice_bitcast_fusion.5, bf16[256,16,32]{0,2,1:T(8,128)(2,1)S(1)} %bitcast.184, bf16[2048,16,32]{0,2,1:T(8,128)(2,1)S(1)} %bitcast.174), kind=kOutput, calls=%fused_computation.14.clone.1 | convolution fusion | flops 570421248 | bytes 69500928 | tf_op jit(solution)/shard_map/while/body/eval_jaxpr/qhd,khd->hqk/dot_general | solution.py:81
  831.8 22.5 fusion.158
  872.7 22.6 %multiply_reduce_fusion.12 = (f32[16,256]{1,0:T(8,128)S(1)}, f32[16,256,2048]{2,1,0:T(8,128)}) fusion(f32[16,256,2048]{2,1,0:T(8,128)} %fusion.157, f32[16,256]{1,0:T(8,128)S(1)} %dynamic-slice_bitcast_fusion.5, bf16[256,16,32]{0,2,1:T(8,128)(2,1)S(1)} %bitcast.184, bf16[2048,16,32]{0,2,1:T(8,128)(2,1)S(1)} %bitcast.174), kind=kOutput, calls=%fused_computation.14.clone.1 | convolution fusion | flops 570421248 | bytes 69500928 | tf_op jit(solution)/shard_map/while/body/eval_jaxpr/qhd,khd->hqk/dot_general | solution.py:81
  895.3 22.5 fusion.158
  936.3 22.6 %multiply_reduce_fusion.12 = (f32[16,256]{1,0:T(8,128)S(1)}, f32[16,256,2048]{2,1,0:T(8,128)}) fusion(f32[16,256,2048]{2,1,0:T(8,128)} %fusion.157, f32[16,256]{1,0:T(8,128)S(1)} %dynamic-slice_bitcast_fusion.5, bf16[256,16,32]{0,2,1:T(8,128)(2,1)S(1)} %bitcast.184, bf16[2048,16,32]{0,2,1:T(8,128)(2,1)S(1)} %bitcast.174), kind=kOutput, calls=%fused_computation.14.clone.1 | convolution fusion | flops 570421248 | bytes 69500928 | tf_op jit(solution)/shard_map/while/body/eval_jaxpr/qhd,khd->hqk/dot_general | solution.py:81
  958.9 22.5 fusion.158
  999.8 22.6 %multiply_reduce_fusion.12 = (f32[16,256]{1,0:T(8,128)S(1)}, f32[16,256,2048]{2,1,0:T(8,128)}) fusion(f32[16,256,2048]{2,1,0:T(8,128)} %fusion.157, f32[16,256]{1,0:T(8,128)S(1)} %dynamic-slice_bitcast_fusion.5, bf16[256,16,32]{0,2,1:T(8,128)(2,1)S(1)} %bitcast.184, bf16[2048,16,32]{0,2,1:T(8,128)(2,1)S(1)} %bitcast.174), kind=kOutput, calls=%fused_computation.14.clone.1 | convolution fusion | flops 570421248 | bytes 69500928 | tf_op jit(solution)/shard_map/while/body/eval_jaxpr/qhd,khd->hqk/dot_general | solution.py:81
  1022.4 22.5 fusion.158
  1063.3 22.6 %multiply_reduce_fusion.12 = (f32[16,256]{1,0:T(8,128)S(1)}, f32[16,256,2048]{2,1,0:T(8,128)}) fusion(f32[16,256,2048]{2,1,0:T(8,128)} %fusion.157, f32[16,256]{1,0:T(8,128)S(1)} %dynamic-slice_bitcast_fusion.5, bf16[256,16,32]{0,2,1:T(8,128)(2,1)S(1)} %bitcast.184, bf16[2048,16,32]{0,2,1:T(8,128)(2,1)S(1)} %bitcast.174), kind=kOutput, calls=%fused_computation.14.clone.1 | convolution fusion | flops 570421248 | bytes 69500928 | tf_op jit(solution)/shard_map/while/body/eval_jaxpr/qhd,khd->hqk/dot_general | solution.py:81
  1085.9 22.5 fusion.158
  1126.8 22.6 %multiply_reduce_fusion.12 = (f32[16,256]{1,0:T(8,128)S(1)}, f32[16,256,2048]{2,1,0:T(8,128)}) fusion(f32[16,256,2048]{2,1,0:T(8,128)} %fusion.157, f32[16,256]{1,0:T(8,128)S(1)} %dynamic-slice_bitcast_fusion.5, bf16[256,16,32]{0,2,1:T(8,128)(2,1)S(1)} %bitcast.184, bf16[2048,16,32]{0,2,1:T(8,128)(2,1)S(1)} %bitcast.174), kind=kOutput, calls=%fused_computation.14.clone.1 | convolution fusion | flops 570421248 | bytes 69500928 | tf_op jit(solution)/shard_map/while/body/eval_jaxpr/qhd,khd->hqk/dot_general | solution.py:81
  1149.4 22.5 fusion.158
  1190.4 22.6 %multiply_reduce_fusion.12 = (f32[16,256]{1,0:T(8,128)S(1)}, f32[16,256,2048]{2,1,0:T(8,128)}) fusion(f32[16,256,2048]{2,1,0:T(8,128)} %fusion.157, f32[16,256]{1,0:T(8,128)S(1)} %dynamic-slice_bitcast_fusion.5, bf16[256,16,32]{0,2,1:T(8,128)(2,1)S(1)} %bitcast.184, bf16[2048,16,32]{0,2,1:T(8,128)(2,1)S(1)} %bitcast.174), kind=kOutput, calls=%fused_computation.14.clone.1 | convolution fusion | flops 570421248 | bytes 69500928 | tf_op jit(solution)/shard_map/while/body/eval_jaxpr/qhd,khd->hqk/dot_general | solution.py:81
  1212.9 22.5 fusion.158
  1236.3 480.7 %while.38 = (s32[]{:T(128)}, bf16[8,2048,512]{2,1,0:T(8,128)(2,1)}, bf16[8,2048,512]{2,1,0:T(8,128)(2,1)}, bf16[8,256,512]{1,2,0:T(8,128)(2,1)}, bf16[8,2048,512...) while((s32[]{:T(128)}, bf16[8,2048,512]{2,1,0:T(8,128)(2,1)}, ...), condition=%wide.region_21.22_spmd, body=%wide.region_20.21_spmd.sunk | while | flops 2216689664 | bytes 144819344 | solution.py:236
  1335.6 16.7 fusion.167
  1455.7 16.7 fusion.167
  1515.8 16.7 fusion.167
  1575.8 16.7 fusion.167
  1635.9 16.7 fusion.167
  1717.0 22.6 %maximum_bitcast_fusion = bf16[2048,8,1024]{2,0,1:T(8,128)(2,1)} fusion(bf16[8,2048,512]{2,1,0:T(8,128)(2,1)} %get-tuple-element.147, bf16[8,2048,512]{2,1,0:T(8,128)(2,1)} %get-tuple-element.146), kind=kLoop, calls=%fused_computation.44 | loop fusion | flops 67108864 | bytes 67108864 | tf_op jit(solution)/shard_map/convert_element_type | solution.py:241
  1763.1 181.9 %reduce-scatter.2.cloned.1.call-done = bf16[256,8,1024]{2,0,1:T(8,128)(2,1)} async-done(((bf16[2048,8,1024]{2,0,1:T(8,128)(2,1)}), bf16[256,8,1024]{2,0,1:T(8,128)(2,1)}) %reduce-scatter.2.cloned.1.call-update) | async-done | bytes 4194320 | tf_op jit(solution)/shard_map/reduce_scatter | solution.py:240
  1993.0 42.9 %all-reduce.2 = (f32[512]{0:T(512)}, f32[512]{0:T(512)}, f32[512]{0:T(512)}, f32[512]{0:T(512)}, f32[512]{0:T(512)}, /*index=5*/f32[512]{0:T(512)}, f32[512]{0:T...) all-reduce(f32[512]{0:T(512)S(1)} %get-tuple-element.381, ...), channel_id=1, replica_groups=mesh['dp'=4,'seq'=8] {'dp','seq'}, use_global_device_ids=true, to_apply=%region_27.28 | all-reduce | flops 7168 | bytes 57344 | tf_op jit(solution)/shard_map/psum | solution.py:276
  2037.2 194.4 %all-reduce.6.cloned.1.call-done = (f32[768,512]{0,1:T(8,128)}, f32[512,1536]{1,0:T(8,128)}, f32[512,512]{1,0:T(8,128)}, f32[512,2048]{1,0:T(8,128)}, f32[2048,512]{1,0:T(8,128)}) async-done(((f32[768,512]{0,1:T(8,128)}, f32[512,1536]{1,0:T(8,128)}, f32[512,512]{1,0:T(8,128)}, f32[512,2048]{1,0:T(8,128)}, f32[2048,512]{1,0:T(8,128)}), (f32[768,512]{0,1:T(8,128)}, f32[512,1536]{1,0:T(8,128)}, ...) | async-done | bytes 14155792 | tf_op jit(solution)/shard_map/psum | solution.py:276
  (474 shorter events, 1108.1 us)
Async XLA Ops:
  7.2 635.3 %copy-start = (bf16[512,2048]{1,0:T(8,128)(2,1)S(1)}, bf16[512,2048]{1,0:T(8,128)(2,1)}, u32[]{:S(2)}) copy-start(bf16[512,2048]{1,0:T(8,128)(2,1)} %param.43) | copy-start | bytes 6291460
  7.2 14.1 copy-start.37
  7.2 14.1 copy-start.44
  7.2 14.2 copy-start.66
  7.2 14.2 copy-start.67
  7.3 14.2 copy-start.68
  7.3 14.2 copy-start.69
  7.3 14.2 copy-start.70
  14.4 32.3 %all-to-all-start = ((bf16[8,51,512]{2,1,0:T(8,128)(2,1)}), bf16[8,51,512]{2,1,0:T(8,128)(2,1)S(1)}, u32[]{:S(2)}, u32[]{:S(2)}) async-start(bf16[8,51,512]{2,1,0:T(8,128)(2,1)} %reshape.338), calls=%async_computation | async-start | bytes 917504 | tf_op jit(solution)/shard_map/all_to_all | solution.py:180
  19.5 142.0 %all-gather.3.cloned.1.call-start = ((), (), s32[]{:S(2)}) async-start(), calls=%async_computation.3 | async-start | bytes 18874368 | tf_op jit(solution)/shard_map/all_gather | solution.py:202
  21.4 30.7 %copy-start.48 = (f32[512]{0:T(512)}, f32[512]{0:T(512)S(1)}, u32[]{:S(2)}) copy-start(f32[512]{0:T(512)S(1)} %convert_element_type.176) | copy-start | bytes 6148
  21.5 30.7 %copy-start.60 = (f32[512]{0:T(512)}, f32[512]{0:T(512)S(1)}, u32[]{:S(2)}) copy-start(f32[512]{0:T(512)S(1)} %convert_element_type.177) | copy-start | bytes 6148
  66.6 190.0 %all-gather.5.cloned.1.call-start = ((), (), s32[]{:S(2)}) async-start(), calls=%async_computation.4 | async-start | bytes 18874368 | tf_op jit(solution)/shard_map/all_gather | solution.py:201
  74.7 1870.3 %reduce-scatter.2.cloned.1.call-start = ((), (), s32[]{:S(2)}) async-start(), calls=%async_computation.5 | async-start | bytes 37748736 | tf_op jit(solution)/shard_map/reduce_scatter | solution.py:240
  256.6 380.6 %copy-start.25 = (bf16[512,512]{1,0:T(8,128)(2,1)S(1)}, bf16[512,512]{1,0:T(8,128)(2,1)}, u32[]{:S(2)}) copy-start(bf16[512,512]{1,0:T(8,128)(2,1)} %param.39) | copy-start | bytes 1572868
  256.6 380.6 %copy-start.52 = (f32[512]{0:T(512)S(1)}, f32[512]{0:T(512)}, u32[]{:S(2)}) copy-start(f32[512]{0:T(512)} %convert_element_type.183) | copy-start | bytes 6148
  641.6 45.1 %copy-start.7 = (f32[2048,512]{1,0:T(8,128)}, f32[2048,512]{1,0:T(8,128)S(1)}, u32[]{:S(2)}) copy-start(f32[2048,512]{1,0:T(8,128)S(1)} %get-tuple-element.377) | copy-start | bytes 12582916
  641.6 78.7 %copy-start.35 = (f32[2048]{0:T(1024)}, f32[2048]{0:T(1024)S(1)}, u32[]{:S(2)}) copy-start(f32[2048]{0:T(1024)S(1)} %broadcast_multiply_fusion) | copy-start | bytes 24580
  642.5 44.2 %copy-start.29 = (f32[2048]{0:T(1024)}, f32[2048]{0:T(1024)S(1)}, u32[]{:S(2)}) copy-start(f32[2048]{0:T(1024)S(1)} %multiply_reduce_fusion.7) | copy-start | bytes 24580
  642.5 77.8 %copy-start.42 = (f32[2048]{0:T(1024)}, f32[2048]{0:T(1024)S(1)}, u32[]{:S(2)}) copy-start(f32[2048]{0:T(1024)S(1)} %fusion.65) | copy-start | bytes 24580
  709.0 11.3 copy-start.8
  1739.7 16.3 slice-start
  1744.3 11.6 copy-start.9
  1744.3 11.6 copy-start.36
  1744.3 11.7 copy-start.43
  1744.3 11.7 copy-start.51
  1744.3 11.7 copy-start.63
  1744.3 11.7 slice-start.1
  1961.2 13.0 all-to-all-start.1
  1964.7 11.9 copy-start.24
  1964.7 266.9 %all-reduce.6.cloned.1.call-start = ((), (), s32[]{:S(2)}) async-start(), calls=%async_computation.6 | async-start | bytes 28311552 | tf_op jit(solution)/shard_map/psum | solution.py:276
  1981.9 54.0 %copy-start.22 = (bf16[768,512]{1,0:T(8,128)(2,1)S(1)}, bf16[768,512]{1,0:T(8,128)(2,1)}, u32[]{:S(2)}) copy-start(bf16[768,512]{1,0:T(8,128)(2,1)} %param.31) | copy-start | bytes 2359300
  (60 other events, 276.6 us)
Sparse Core Ops, SparseCore 0:
  66.7 94.7 all-gather.2
  163.4 93.1 all-gather.4
  1739.8 205.2 reduce-scatter.1
  1978.5 253.1 all-reduce.5
where the time goes:
time: 2260 us; the launch traced here: 2250 us
  matrix products  1190 us (53%)
  waiting for transfers between devices  552 us (24%)
  local copies, waits for them, and re-layouts  281 us (12%)
  other arithmetic  166 us (7%)
  blocking collectives  42.9 us (2%)
    psum x1, waiting for transfers between devices, body(): lax.psum((grad_embed_weight, grad_embed_bias, grad_mask, grad_first_gain,...  194 us
    reduce_scatter x1, waiting for transfers between devices, body(): lax.psum_scatter(jnp.concatenate([part_key, part_value], axis=2).transpos...  182 us
    dot_general x8, matrix products, query_backward(): jnp.einsum('qhd,khd->hqk', grad_heads, split_heads(value_rows), preferred...  181 us
    dot_general x8, matrix products, query_backward(): jnp.einsum('hqk,khd->qhd', grad_scores, key_heads, preferred_element_type...  180 us
    dot_general x8, matrix products, key_backward(): jnp.einsum('hqk,qhd->khd', grad_scores, query_heads, preferred_element_ty...  134 us
    dot_general x8, matrix products, attend_clip(): jnp.einsum('hqk,khd->qhd', attention_low, split_heads(value_rows), prefer...  116 us
    dot_general x8, matrix products, key_backward(): jnp.einsum('hqk,qhd->khd', attention.astype(jnp.bfloat16), grad_heads, pr...  114 us
    reduce_sum x8, other arithmetic, attend_clip(): totals = jnp.sum(raised, axis=-1, keepdims=True)  112 us
  transfers between devices with their start and end apart: 6, of which 4 were waited for; matrix products, arithmetic and copies ran while one was open for 4% of the time, Pallas kernels for 0%

commit v1 on v0

v1 whole, which is shorter than its diff:
```python
from functools import partial
import math

import jax
import jax.numpy as jnp
from jax import lax
from jax.experimental import pallas as pl
from jax.experimental.pallas import tpu as pltpu
from jax.sharding import PartitionSpec as P

HEADS = 16
HEAD_DIM = 32
PACK = 128 // HEAD_DIM
VMEM_LIMIT = 56 * 1024 * 1024
LOG2E = math.log2(math.e)
QUERY_SCALE = LOG2E * HEAD_DIM ** (-0.5)


epsilon = 1e-06


def layer_norm(values, gain, shift):
    center = values - jnp.mean(values, axis=-1, keepdims=True)
    spread = jnp.mean(center * center, axis=-1, keepdims=True)
    return center * lax.rsqrt(spread + epsilon) * gain + shift


def sinusoid(places, table_width):
    half_width = table_width // 2
    frequency = jnp.exp(-math.log(10000.0) * jnp.arange(half_width, dtype=jnp.float32) / half_width)
    angles = places.astype(jnp.float32)[:, None] * frequency[None, :]
    return jnp.concatenate([jnp.sin(angles), jnp.cos(angles)], axis=1)


def plain_dot(left, right):
    return jnp.dot(left, right, preferred_element_type=jnp.float32)


def lead_dot(left, right):
    return lax.dot_general(
        left, right, (((0,), (0,)), ((), ())), preferred_element_type=jnp.float32
    )


def trail_dot(left, right):
    return lax.dot_general(
        left, right, (((1,), (1,)), ((), ())), preferred_element_type=jnp.float32
    )


def column_sum(values):
    return jnp.sum(values.astype(jnp.float32), axis=0)


def attend_kernel(key_ref, query_ref, value_ref, mixed_ref, total_ref, raised_ref):
    query = query_ref[...]
    head_row = lax.broadcasted_iota(jnp.int32, query.shape, 0) // HEAD_DIM
    ones = jnp.ones((16, value_ref.shape[1]), jnp.bfloat16)
    totals = []
    for head in range(PACK):
        rows = slice(head * HEAD_DIM, (head + 1) * HEAD_DIM)
        own_query = jnp.where(head_row == head, query, jnp.zeros_like(query))
        scores = jnp.dot(key_ref[...], own_query, preferred_element_type=jnp.float32)
        highest = jnp.max(scores, axis=0, keepdims=True)
        raised = jnp.exp2(scores - highest).astype(jnp.bfloat16)
        raised_ref[head] = raised
        widened = jnp.concatenate([value_ref[rows, :], ones], axis=0)
        mixed = jnp.dot(widened, raised, preferred_element_type=jnp.float32)
        total = mixed[HEAD_DIM : HEAD_DIM + 1]
        totals.append(total)
        mixed_ref[rows, :] = (mixed[:HEAD_DIM] / total).astype(jnp.bfloat16)
    total_ref[0, 0:PACK] = jnp.concatenate(totals, axis=0)


def attend(keys, query_t, value_t):
    width, rows = query_t.shape
    span = keys.shape[0]
    block = min(256, rows)
    groups = width // 128
    return pl.pallas_call(
        attend_kernel,
        grid=(groups, rows // block),
        in_specs=[
            pl.BlockSpec((span, 128), lambda g, i: (0, g)),
            pl.BlockSpec((128, block), lambda g, i: (g, i)),
            pl.BlockSpec((128, span), lambda g, i: (g, 0)),
        ],
        out_specs=[
            pl.BlockSpec((128, block), lambda g, i: (g, i)),
            pl.BlockSpec((1, 8, block), lambda g, i: (g, 0, i)),
            pl.BlockSpec((PACK, span, block), lambda g, i: (g, 0, i)),
        ],
        out_shape=[
            jax.ShapeDtypeStruct((width, rows), jnp.bfloat16),
            jax.ShapeDtypeStruct((groups, 8, rows), jnp.float32),
            jax.ShapeDtypeStruct((HEADS, span, rows), jnp.bfloat16),
        ],
        compiler_params=pltpu.CompilerParams(vmem_limit_bytes=VMEM_LIMIT),
        cost_estimate=pl.CostEstimate(
            flops=HEADS * span * rows * 512,
            bytes_accessed=2 * HEADS * span * rows,
            transcendentals=HEADS * span * rows,
        ),
        name="attend",
    )(keys, query_t, value_t)


def attend_back_kernel(
    raised_ref, total_ref, value_ref, key_ref, query_ref, mixed_ref, grad_ref, grad_query_ref, grad_key_ref, grad_value_ref
):
    @pl.when(pl.program_id(1) == 0)
    def _():
        grad_key_ref[...] = jnp.zeros_like(grad_key_ref)
        grad_value_ref[...] = jnp.zeros_like(grad_value_ref)

    block = query_ref.shape[1]
    head_row = lax.broadcasted_iota(jnp.int32, (128, block), 0) // HEAD_DIM
    head_col = lax.broadcasted_iota(jnp.int32, (block, 128), 1) // HEAD_DIM
    inverse = 1.0 / total_ref[0, 0:PACK]
    inverse = jnp.concatenate(
        [jnp.broadcast_to(inverse[h : h + 1], (HEAD_DIM, block)) for h in range(PACK)], axis=0
    )
    grad = grad_ref[...].astype(jnp.float32) * inverse
    inner = grad * mixed_ref[...].astype(jnp.float32)
    grad_low = grad.astype(jnp.bfloat16)
    grad_turned = grad.T.astype(jnp.bfloat16)
    query_turned = query_ref[...].astype(jnp.float32).T.astype(jnp.bfloat16)
    for head in range(PACK):
        rows = slice(head * HEAD_DIM, (head + 1) * HEAD_DIM)
        own_grad = jnp.where(head_row == head, grad_low, jnp.zeros_like(grad_low))
        grad_weight = jnp.dot(value_ref[...], own_grad, preferred_element_type=jnp.float32)
        row_inner = jnp.sum(inner[rows], axis=0, keepdims=True)
        raised = raised_ref[head]
        grad_scores = raised * (grad_weight - row_inner).astype(jnp.bfloat16)
        grad_value_ref[...] += jnp.dot(
            raised,
            jnp.where(head_col == head, grad_turned, jnp.zeros_like(grad_turned)),
            preferred_element_type=jnp.float32,
        )
        grad_key_ref[...] += jnp.dot(
            grad_scores,
            jnp.where(head_col == head, query_turned, jnp.zeros_like(query_turned)),
            preferred_element_type=jnp.float32,
        )
        grad_query_ref[rows, :] = (
            jnp.dot(key_ref[rows, :], grad_scores, preferred_element_type=jnp.float32)
            * HEAD_DIM ** (-0.5)
        ).astype(jnp.bfloat16)


def attend_back(raised, total, values, key_t, query_t, mixed_t, grad_t):
    width, rows = query_t.shape
    span = values.shape[0]
    block = min(256, rows)
    groups = width // 128
    lane_block = pl.BlockSpec((128, block), lambda g, i: (g, i))
    return pl.pallas_call(
        attend_back_kernel,
        grid=(groups, rows // block),
        in_specs=[
            pl.BlockSpec((PACK, span, block), lambda g, i: (g, 0, i)),
            pl.BlockSpec((1, 8, block), lambda g, i: (g, 0, i)),
            pl.BlockSpec((span, 128), lambda g, i: (0, g)),
            pl.BlockSpec((128, span), lambda g, i: (g, 0)),
            lane_block,
            lane_block,
            lane_block,
        ],
        out_specs=[
            lane_block,
            pl.BlockSpec((span, 128), lambda g, i: (0, g)),
            pl.BlockSpec((span, 128), lambda g, i: (0, g)),
        ],
        out_shape=[
            jax.ShapeDtypeStruct((width, rows), jnp.bfloat16),
            jax.ShapeDtypeStruct((span, width), jnp.float32),
            jax.ShapeDtypeStruct((span, width), jnp.float32),
        ],
        compiler_params=pltpu.CompilerParams(vmem_limit_bytes=VMEM_LIMIT),
        cost_estimate=pl.CostEstimate(
            flops=HEADS * span * rows * 1024,
            bytes_accessed=2 * HEADS * span * rows,
            transcendentals=0,
        ),
        name="attend_back",
    )(raised, total, values, key_t, query_t, mixed_t, grad_t)


def body(
    latents,
    clip_ids,
    restore,
    counts,
    embed_weight,
    embed_bias,
    mask_token,
    first_gain,
    first_shift,
    joint_weight,
    query_bias,
    value_bias,
    output_weight,
    output_bias,
    second_gain,
    second_shift,
    expand_weight,
    expand_bias,
    contract_weight,
    contract_bias,
    cotangent,
):
    splits = lax.axis_size("seq")
    seq_index = lax.axis_index("seq")
    capacity = latents.shape[0]
    clip_count, clip_share, model_width = cotangent.shape
    sharers = splits // clip_count
    rows = clip_count * clip_share
    own_clip = seq_index % clip_count
    first_place = (seq_index // clip_count) * rows
    exchange_groups = [[s * clip_count + c for c in range(clip_count)] for s in range(sharers)]
    clip_groups = [[s * clip_count + c for s in range(sharers)] for c in range(clip_count)]

    def to_clips(blocks):
        return lax.all_to_all(
            blocks,
            "seq",
            split_axis=0,
            concat_axis=0,
            tiled=True,
            axis_index_groups=exchange_groups if sharers > 1 else None,
        )

    def flatten(parts):
        return jnp.concatenate(
            [part.reshape(-1, model_width).astype(jnp.bfloat16) for part in parts], axis=0
        )

    def sum_flat(flat, parts):
        flat = lax.psum(flat, ("dp", "seq")).astype(jnp.float32)
        out, at = [], 0
        for part in parts:
            size = part.size // model_width
            out.append(flat[at : at + size].reshape(part.shape))
            at += size
        return out

    slot = jnp.arange(splits * capacity, dtype=jnp.int32)
    live = (slot % capacity) < jnp.repeat(counts, capacity)
    mine = live & (clip_ids % clip_count == own_clip)
    slot_place = jnp.where(mine, restore - first_place, -1)
    places = jnp.arange(rows, dtype=jnp.int32)
    restore_map = (places[:, None] == slot_place[None, :]).astype(jnp.bfloat16)

    embedded = (plain_dot(latents, embed_weight) + embed_bias.astype(jnp.float32)).astype(
        jnp.bfloat16
    )
    embedded_all = lax.all_gather(embedded, "seq", axis=0, tiled=True)
    grad_output = to_clips(cotangent).reshape(rows, model_width)

    placed = plain_dot(restore_map, embedded_all)
    visible_mask = jnp.sum(restore_map, axis=1, dtype=jnp.float32)
    stream = (
        placed
        + (1.0 - visible_mask)[:, None] * mask_token.astype(jnp.float32)[None, :]
        + sinusoid(first_place + places, model_width)
    )
    first_normed, first_back = jax.vjp(
        layer_norm, stream, first_gain.astype(jnp.float32), first_shift.astype(jnp.float32)
    )
    first_low = first_normed.astype(jnp.bfloat16)
    joint = plain_dot(first_low, joint_weight)
    query_t = (
        ((joint[:, :model_width] + query_bias.astype(jnp.float32)) * QUERY_SCALE)
        .astype(jnp.bfloat16)
        .T
    )
    keys = joint[:, model_width : 2 * model_width].astype(jnp.bfloat16)
    values = (joint[:, 2 * model_width :] + value_bias.astype(jnp.float32)).astype(jnp.bfloat16)
    if sharers > 1:
        keys = lax.all_gather(keys, "seq", axis=0, tiled=True, axis_index_groups=clip_groups)
        values = lax.all_gather(values, "seq", axis=0, tiled=True, axis_index_groups=clip_groups)
    mixed_t, total, raised = attend(keys, query_t, values.T)
    attended = mixed_t.T
    middle = stream + plain_dot(attended, output_weight) + output_bias.astype(jnp.float32)
    second_normed, second_back = jax.vjp(
        layer_norm, middle, second_gain.astype(jnp.float32), second_shift.astype(jnp.float32)
    )
    second_low = second_normed.astype(jnp.bfloat16)
    hidden = plain_dot(second_low, expand_weight) + expand_bias.astype(jnp.float32)
    active, gelu_back = jax.vjp(partial(jax.nn.gelu, approximate=False), hidden)
    active_low = active.astype(jnp.bfloat16)
    output_rows = (
        middle + plain_dot(active_low, contract_weight) + contract_bias.astype(jnp.float32)
    )
    decoded = to_clips(
        output_rows.astype(jnp.bfloat16).reshape(clip_count, clip_share, model_width)
    )
    grad_contract = lead_dot(active_low, grad_output)
    grad_contract_bias = column_sum(grad_output)
    grad_hidden = gelu_back(trail_dot(grad_output, contract_weight))[0].astype(jnp.bfloat16)
    grad_expand = lead_dot(second_low, grad_hidden)
    grad_expand_bias = column_sum(grad_hidden)
    grad_middle_norm, grad_second_gain, grad_second_shift = second_back(
        trail_dot(grad_hidden, expand_weight)
    )
    grad_middle = grad_output.astype(jnp.float32) + grad_middle_norm
    grad_branch = grad_middle.astype(jnp.bfloat16)
    grad_output_weight = lead_dot(attended, grad_branch)
    grad_output_bias = column_sum(grad_branch)
    grad_attended_t = trail_dot(output_weight, grad_branch).astype(jnp.bfloat16)
    early = [
        grad_expand,
        grad_contract,
        grad_output_weight,
        grad_output_bias,
        grad_second_gain,
        grad_second_shift,
        grad_expand_bias,
        grad_contract_bias,
    ]
    early_flat, grad_attended_t = lax.optimization_barrier((flatten(early), grad_attended_t))
    (
        grad_expand,
        grad_contract,
        grad_output_weight,
        grad_output_bias,
        grad_second_gain,
        grad_second_shift,
        grad_expand_bias,
        grad_contract_bias,
    ) = sum_flat(early_flat, early)
    grad_query_t, grad_key, grad_value = attend_back(
        raised, total, values, keys.T, query_t, mixed_t, grad_attended_t
    )
    grad_sides = [(grad_key * (1.0 / LOG2E)).astype(jnp.bfloat16), grad_value.astype(jnp.bfloat16)]
    if sharers > 1:
        grad_sides = [
            lax.psum_scatter(
                side, "seq", scatter_dimension=0, tiled=True, axis_index_groups=clip_groups
            )
            for side in grad_sides
        ]
    grad_joint = jnp.concatenate([grad_query_t.T] + grad_sides, axis=1)
    grad_joint_weight = lead_dot(first_low, grad_joint)
    grad_query_bias = column_sum(grad_joint[:, :model_width])
    grad_value_bias = column_sum(grad_joint[:, 2 * model_width :])
    grad_stream_norm, grad_first_gain, grad_first_shift = first_back(
        trail_dot(grad_joint, joint_weight)
    )
    grad_stream = grad_middle + grad_stream_norm
    grad_mask = jnp.sum((1.0 - visible_mask)[:, None] * grad_stream, axis=0)
    back_rows = lead_dot(restore_map, grad_stream.astype(jnp.bfloat16)).astype(jnp.bfloat16)
    grad_embedded = lax.psum_scatter(back_rows, "seq", scatter_dimension=0, tiled=True)
    latent_grad = trail_dot(grad_embedded, embed_weight).astype(jnp.bfloat16)
    grad_embed_weight = lead_dot(latents, grad_embedded)
    grad_embed_bias = column_sum(grad_embedded)

    def sum_small(parts):
        flat = jnp.concatenate([part.reshape(-1, 128) for part in parts], axis=0)
        flat = lax.psum(flat, ("dp", "seq"))
        out, at = [], 0
        for part in parts:
            size = part.size // 128
            out.append(flat[at : at + size].reshape(part.shape))
            at += size
        return out

    late = [
        grad_joint_weight,
        grad_embed_weight,
        grad_embed_bias,
        grad_mask,
        grad_first_gain,
        grad_first_shift,
        grad_query_bias,
        grad_value_bias,
    ]
    late_flat, grad_output_weight = lax.optimization_barrier((flatten(late), grad_output_weight))
    (
        grad_joint_weight,
        grad_embed_weight,
        grad_embed_bias,
        grad_mask,
        grad_first_gain,
        grad_first_shift,
        grad_query_bias,
        grad_value_bias,
    ) = sum_flat(late_flat, late)
    return (
        decoded,
        latent_grad,
        grad_embed_weight,
        grad_embed_bias,
        grad_mask,
        grad_first_gain,
        grad_first_shift,
        grad_joint_weight,
        grad_query_bias,
        grad_value_bias,
        grad_output_weight,
        grad_output_bias,
        grad_second_gain,
        grad_second_shift,
        grad_expand,
        grad_expand_bias,
        grad_contract,
        grad_contract_bias,
    )


def solution(mesh):
    placed = (
        (P(("dp", "seq"), None),) + (P("dp"),) * 3 + (P(),) * 16 + (P("dp", "seq", None),)
    )
    return jax.shard_map(
        body,
        mesh=mesh,
        in_specs=placed,
        out_specs=(P("dp", "seq", None), P(("dp", "seq"), None)) + (P(),) * 16,
        check_vma=False,
    )
```

time: 2260 us -> 930 us (0.41)
  matrix products: 1190 us -> 159 us
  Pallas kernels: 0 us -> 303 us
  waiting for transfers between devices: 552 us -> 296 us
  local copies, waits for them, and re-layouts: 281 us -> 91.6 us
  other arithmetic: 166 us -> 51.2 us
  blocking collectives: 42.9 us -> 0 us
    dot_general x64 -> x0, matrix products: 1040 us -> none  [the longest x8 181 us: query_backward(): jnp.einsum('qhd,khd->hqk', grad_heads, split_heads(value_rows), preferred...]
    pallas_call x0 -> x2, Pallas kernels: none -> 303 us  [the longest x1 167 us: attend(): pl.pallas_call(attend_kernel, grid=(groups, rows // block), in_specs=[pl....]
    all_gather x2 -> x1, waiting for transfers between devices: 175 us -> 7.96 us  [body(): embedded_all = lax.all_gather(embedded, 'seq', axis=0, tiled=True)]
    reduce_scatter x1, waiting for transfers between devices: 182 us -> 47.9 us  [body(): lax.psum_scatter(back_rows, 'seq', scatter_dimension=0, tiled=True)]
    reduce_sum x9 -> x0, other arithmetic: 112 us -> none  [the longest x8 112 us: attend_clip(): totals = jnp.sum(raised, axis=-1, keepdims=True)]
    dynamic_slice x50 -> x0, local copies, waits for them, and re-layouts: 111 us -> none  [the longest x48 111 us: body(): lax.map(attend_clip, (query_clips, key_all, value_all))]
    dynamic_update_slice x72 -> x0, local copies, waits for them, and re-layouts: 94.5 us -> none  [the longest x32 80.6 us: body(): lax.map(key_backward, (query_clips, grad_clips, log_total, row_inner, key...]
    psum x1 -> x0, blocking collectives: 42.9 us -> none  [body(): lax.psum((grad_embed_weight, grad_embed_bias, grad_mask, grad_first_gain,...]
  transfers between devices with their start and end apart: 6 -> 6, of which waited for: 4 -> 6; matrix products, arithmetic and copies ran while one was open for 4% -> 9% of each run, Pallas kernels for 0% -> 0%
where the time goes in v1:
time: 930 us; the launch traced here: 924 us
  Pallas kernels  303 us (33%)
  waiting for transfers between devices  296 us (32%)
  matrix products  159 us (17%)
  local copies, waits for them, and re-layouts  91.6 us (10%)
  other arithmetic  51.2 us (6%)
  between operations  14.9 us (2%)
    psum x2, waiting for transfers between devices, sum_flat(): flat = lax.psum(flat, ('dp', 'seq')).astype(jnp.float32)  206 us
    pallas_call x1, Pallas kernels, attend(): pl.pallas_call(attend_kernel, grid=(groups, rows // block), in_specs=[pl....  167 us
    pallas_call x1, Pallas kernels, attend_back(): pl.pallas_call(attend_back_kernel, grid=(groups, rows // block), in_specs...  136 us
    dot_general x6, matrix products, plain_dot(): return jnp.dot(left, right, preferred_element_type=jnp.float32)  77.2 us
    reduce_scatter x1, waiting for transfers between devices, body(): lax.psum_scatter(back_rows, 'seq', scatter_dimension=0, tiled=True)  47.9 us
    dot_general x5, matrix products, trail_dot(): lax.dot_general(left, right, (((1,), (1,)), ((), ())), preferred_element_...  43.9 us
    dot_general x6, matrix products, lead_dot(): lax.dot_general(left, right, (((0,), (0,)), ((), ())), preferred_element_...  38.1 us
    all_to_all x2, waiting for transfers between devices, to_clips(): lax.all_to_all(blocks, 'seq', split_axis=0, concat_axis=0, tiled=True, ax...  33.7 us
  transfers between devices with their start and end apart: 6, of which 6 were waited for; matrix products, arithmetic and copies ran while one was open for 9% of the time, Pallas kernels for 0%

profile of v1, /device:TPU:0, one launch (start us, length us, event | category | flops | bytes accessed | tf_op | source)
XLA Modules:
  0.0 924.5 jit_solution(649508700619227677)
XLA Ops:
  10.8 5.2 all-to-all-start.1
  19.5 9.0 multiply_sine_fusion
  28.5 18.7 %all-to-all-done.1 = bf16[8,256,512]{2,1,0:T(8,128)(2,1)} async-done(((bf16[8,256,512]{2,1,0:T(8,128)(2,1)}), bf16[8,256,512]{2,1,0:T(8,128)(2,1)}, u32[]{:S(2)}, u32[]{:S(2)}) %all-to-all-start.1) | async-done | bytes 2097184 | tf_op jit(solution)/shard_map/all_to_all | solution.py:224
  49.7 8.0 all-gather.2.cloned.1.call-done
  57.7 12.3 %fusion.42 = (f32[2048]{0:T(1024)S(1)}, f32[2048,512]{1,0:T(8,128)S(1)}) fusion(f32[2048,256]{1,0:T(8,128)} %get-tuple-element.71, f32[2048,256]{1,0:T(8,128)} %get-tuple-element.70, f32[512]{0:T(512)S(1)} %convert_element_type.273, f32[2048]{0:T(1024)S(1)} %broadcast_subtract_fusion, bf16[3264,512]{1,0:T(8,128)(2,1)} %all-gather.2.cloned.1.call-done, ...), kind=kOutput, calls=%fused_computation.101 | convolution fusion | flops 6857029632 | bytes 11762432 | tf_op jit(solution)/shard_map/dot_general | solution.py:36
  81.7 5.5 copy.55
  87.1 3.9 copy.49.value_ref
  91.1 3.9 copy.54
  95.0 3.9 copy.48.key_ref
  98.9 3.9 fusion.16.query_ref
  102.8 166.9 %attend.1 = (bf16[512,2048]{1,0:T(8,128)(2,1)}, f32[4,8,2048]{2,1,0:T(8,128)}, bf16[16,2048,2048]{2,1,0:T(8,128)(2,1)}) custom-call(bf16[2048,512]{1,0:T(8,128)(2,1)} %copy.48.key_ref, bf16[512,2048]{1,0:T(8,128)(2,1)} %fusion.16.query_ref, bf16[512,2048]{1,0:T(8,128)(2,1)} %copy.49.value_ref), custom_call_target="tpu_custom_call" | custom-call | flops 34359738368 | bytes 134217728 | tf_op jit(solution)/shard_map/attend/pallas_call | solution.py:80
  273.7 44.2 %multiply_convert_fusion = (bf16[2048,2048]{1,0:T(8,128)(2,1)}, f32[2048,2048]{1,0:T(8,128)}, f32[2048,2048]{1,0:T(8,128)}) fusion(f32[2048]{0:T(1024)S(1)} %convert_element_type.286, bf16[512,2048]{1,0:T(8,128)(2,1)S(1)} %copy-done, f32[2048,512]{1,0:T(8,128)S(1)} %get-tuple-element.75, f32[512]{0:T(512)S(1)} %convert_element_type.284, ...), kind=kOutput, calls=%fused_computation.8 | convolution fusion | flops 4577034240 | bytes 48263168 | tf_op jit(solution)/shard_map/dot_general | solution.py:36
  317.9 21.8 %fusion.44 = (bf16[2048]{0:T(1024)(128)(2,1)S(1)}, bf16[2048,2048]{1,0:T(8,128)(2,1)}) fusion(f32[2048,2048]{1,0:T(8,128)} %get-tuple-element.55, bf16[2048,512]{1,0:T(8,128)(2,1)} %bitcast.3, bf16[2048,512]{1,0:T(8,128)(2,1)} %param.39, f32[2048,2048]{1,0:T(8,128)} %get-tuple-element.76, f32[2048]{0:T(1024)S(1)} %convert_element_type.286), kind=kOutput, calls=%fused_computation.103 | convolution fusion | flops 4362074112 | bytes 46149632 | tf_op jit(solution)/shard_map/dot_general | solution.py:46
  339.7 10.7 %multiply_reduce_fusion.3 = (bf16[512]{0:T(512)(128)(2,1)S(1)}, f32[2048]{0:T(1024)S(1)}, bf16[512]{0:T(512)(128)(2,1)S(1)}, f32[2048,512]{1,0:T(8,128)S(1)}) fusion(f32[2048,512]{1,0:T(8,128)} %copy-done.5, f32[2048]{0:T(1024)S(1)} %fusion.28, f32[2048]{0:T(1024)S(1)} %broadcast_multiply_fusion, f32[512]{0:T(512)S(1)} %convert_element_type.283, ...), kind=kOutput, calls=%fused_computation.36 | convolution fusion | flops 4303352832 | bytes 18903040 | tf_op jit(solution)/shard_map/dot_general | solution.py:46
  350.4 6.3 convolution_convert_fusion.3
  369.7 9.9 %convolution_convert_fusion.2 = bf16[2048,512]{1,0:T(8,128)(2,1)} fusion(bf16[2048,2048]{1,0:T(8,128)(2,1)} %get-tuple-element.54, bf16[2048,512]{1,0:T(8,128)(2,1)} %bitcast.3), kind=kOutput, calls=%fused_computation.50 | convolution fusion | flops 4296015872 | bytes 12582912 | tf_op jit(solution)/shard_map/dot_general | solution.py:40
  379.7 16.9 %concatenate.13 = bf16[4616,512]{1,0:T(8,128)(2,1)} concatenate(bf16[2048,512]{1,0:T(8,128)(2,1)S(1)} %convert_element_type.293, bf16[2048,512]{1,0:T(8,128)(2,1)} %convolution_convert_fusion.2, bf16[512,512]{1,0:T(8,128)(2,1)S(1)} %convolution_convert_fusion.6, bf16[1,512]{1,0:T(2,128)(2,1)S(1)} %convert_element_type.297, bf16[1,512]{1,0:T(2,128)(2,1)S(1)} %convert_element_type.299, ...), dimensions={0} | concatenate | bytes 9453568 | tf_op jit(solution)/shard_map/concatenate | solution.py:234
  396.6 135.7 %attend_back.1 = (bf16[512,2048]{1,0:T(8,128)(2,1)}, f32[2048,512]{1,0:T(8,128)}, f32[2048,512]{1,0:T(8,128)}) custom-call(bf16[16,2048,2048]{2,1,0:T(8,128)(2,1)} %get-tuple-element.29.raised_ref, f32[4,8,2048]{2,1,0:T(8,128)} %get-tuple-element.30.total_ref, bf16[2048,512]{1,0:T(8,128)(2,1)} %get-tuple-element.56.value_ref, bf16[512,2048]{1,0:T(8,128)(2,1)} %bitcast.54, ...), custom_call_target="tpu_custom_call" | custom-call | flops 68719476736 | bytes 134217728 | tf_op jit(solution)/shard_map/attend_back/pallas_call | solution.py:157
  532.3 4.2 fusion.33
  543.5 7.4 multiply_reduce_fusion
  551.0 4.9 fusion.34
  558.6 9.3 %fusion.11 = bf16[3264,512]{1,0:T(8,128)(2,1)} fusion(s32[3264]{0:T(1024)S(1)} %copy-done.32, bf16[2048,512]{1,0:T(8,128)(2,1)S(1)} %get-tuple-element.47), kind=kOutput, calls=%fused_computation.27 | convolution fusion | flops 6853459968 | bytes 5452544 | tf_op jit(solution)/shard_map/dot_general | solution.py:40
  567.9 11.3 %add_convert_fusion.1 = bf16[2048,512]{1,0:T(8,128)(2,1)} fusion(f32[2048,512]{1,0:T(8,128)} %copy-done.5, bf16[2048,2048]{1,0:T(8,128)(2,1)} %get-tuple-element.54, bf16[2048,512]{1,0:T(8,128)(2,1)} %param.39, f32[512]{0:T(512)S(1)} %convert_element_type.288), kind=kOutput, calls=%fused_computation.39 | convolution fusion | flops 4298113024 | bytes 16779264 | tf_op jit(solution)/shard_map/dot_general | solution.py:36
  585.2 8.9 convolution_convert_fusion
  597.9 15.0 %all-to-all-done = bf16[8,256,512]{2,1,0:T(8,128)(2,1)S(1)} async-done(((bf16[8,256,512]{2,1,0:T(8,128)(2,1)}), bf16[8,256,512]{2,1,0:T(8,128)(2,1)S(1)}, u32[]{:S(2)}, u32[]{:S(2)}) %all-to-all-start) | async-done | bytes 2097184 | tf_op jit(solution)/shard_map/all_to_all | solution.py:224
  613.0 90.7 %all-reduce.3.cloned.1.call-done = bf16[4616,512]{1,0:T(8,128)(2,1)} async-done(((bf16[4616,512]{1,0:T(8,128)(2,1)}), bf16[4616,512]{1,0:T(8,128)(2,1)}) %all-reduce.3.cloned.1.call-update) | async-done | bytes 4726800 | tf_op jit(solution)/shard_map/psum | solution.py:239
  705.8 47.9 %reduce-scatter.2.cloned.1.call-done = bf16[408,512]{1,0:T(8,128)(2,1)} async-done(((bf16[3264,512]{1,0:T(8,128)(2,1)}), bf16[408,512]{1,0:T(8,128)(2,1)}) %reduce-scatter.2.cloned.1.call-update) | async-done | bytes 417808 | tf_op jit(solution)/shard_map/reduce_scatter | solution.py:353
  758.7 10.1 %concatenate.15 = bf16[2310,512]{1,0:T(8,128)(2,1)} concatenate(bf16[1536,512]{1,0:T(8,128)(2,1)} %convert_element_type.312, bf16[768,512]{1,0:T(8,128)(2,1)S(1)} %copy.52, bf16[1,512]{1,0:T(2,128)(2,1)S(1)} %convert_element_type.315, bf16[1,512]{1,0:T(2,128)(2,1)S(1)} %convert_element_type.317, bf16[1,512]{1,0:T(2,128)(2,1)S(1)} %convert_element_type.319, ...), dimensions={0} | concatenate | bytes 4730880 | tf_op jit(solution)/shard_map/concatenate | solution.py:234
  768.8 6.8 fusion.40
  775.6 5.6 reshape.288
  788.4 115.3 %all-reduce.5.cloned.1.call-done = bf16[2310,512]{1,0:T(8,128)(2,1)} async-done(((bf16[2310,512]{1,0:T(8,128)(2,1)}), bf16[2310,512]{1,0:T(8,128)(2,1)}) %all-reduce.5.cloned.1.call-update) | async-done | bytes 2365456 | tf_op jit(solution)/shard_map/psum | solution.py:239
  907.2 5.0 reshape.282
  (181 shorter events, 80.6 us)
Async XLA Ops:
  7.2 266.5 %copy-start = (bf16[512,2048]{1,0:T(8,128)(2,1)S(1)}, bf16[512,2048]{1,0:T(8,128)(2,1)}, u32[]{:S(2)}) copy-start(bf16[512,2048]{1,0:T(8,128)(2,1)} %param.37) | copy-start | bytes 6291460
  7.2 9.0 copy-start.40
  7.2 9.0 copy-start.41
  7.3 9.0 copy-start.42
  7.3 9.1 copy-start.43
  7.3 9.1 copy-start.44
  7.3 9.1 copy-start.45
  7.3 9.1 copy-start.36
  7.3 9.1 copy-start.46
  7.3 9.2 copy-start.30
  7.3 9.2 copy-start.29
  7.3 50.4 %all-gather.2.cloned.1.call-start = ((), (), s32[]{:S(2)}) async-start(), calls=%async_computation.3 | async-start | bytes 3760128 | tf_op jit(solution)/shard_map/all_gather | solution.py:257
  10.8 36.4 %all-to-all-start.1 = ((bf16[8,256,512]{2,1,0:T(8,128)(2,1)}), bf16[8,256,512]{2,1,0:T(8,128)(2,1)}, u32[]{:S(2)}, u32[]{:S(2)}) async-start(bf16[8,256,512]{2,1,0:T(8,128)(2,1)} %param.41), calls=%async_computation.1 | async-start | bytes 4194304 | tf_op jit(solution)/shard_map/all_to_all | solution.py:224
  16.0 687.7 %all-reduce.3.cloned.1.call-start = ((), (), s32[]{:S(2)}) async-start(), calls=%async_computation.5 | async-start | bytes 9453568 | tf_op jit(solution)/shard_map/psum | solution.py:239
  16.3 55.2 %copy-start.34 = (f32[512]{0:T(512)}, f32[512]{0:T(512)S(1)}, u32[]{:S(2)}) copy-start(f32[512]{0:T(512)S(1)} %convert_element_type.275) | copy-start | bytes 6148
  16.3 55.2 %copy-start.37 = (f32[512]{0:T(512)}, f32[512]{0:T(512)S(1)}, u32[]{:S(2)}) copy-start(f32[512]{0:T(512)S(1)} %convert_element_type.276) | copy-start | bytes 6148
  16.5 53.5 %copy-start.31 = (s32[3264]{0:T(1024)}, s32[3264]{0:T(1024)S(1)}, u32[]{:S(2)}) copy-start(s32[3264]{0:T(1024)S(1)} %subtract_select_fusion.1) | copy-start | bytes 39172
  19.5 50.5 %copy-start.27 = (f32[2048]{0:T(1024)}, f32[2048]{0:T(1024)S(1)}, u32[]{:S(2)}) copy-start(f32[2048]{0:T(1024)S(1)} %broadcast_subtract_fusion) | copy-start | bytes 24580
  102.8 166.9 %copy-start.3 = (f32[2048,512]{1,0:T(8,128)S(1)}, f32[2048,512]{1,0:T(8,128)}, u32[]{:S(2)}) copy-start(f32[2048,512]{1,0:T(8,128)} %copy-done.2) | copy-start | bytes 12582916
  102.8 166.9 %copy-start.17 = (bf16[512,512]{1,0:T(8,128)(2,1)S(1)}, bf16[512,512]{1,0:T(8,128)(2,1)}, u32[]{:S(2)}) copy-start(bf16[512,512]{1,0:T(8,128)(2,1)} %param.33) | copy-start | bytes 1572868
  272.8 45.1 %copy-start.5 = (f32[2048,512]{1,0:T(8,128)}, f32[2048,512]{1,0:T(8,128)S(1)}, u32[]{:S(2)}) copy-start(f32[2048,512]{1,0:T(8,128)S(1)} %get-tuple-element.75) | copy-start | bytes 12582916
  273.7 44.2 %copy-start.21 = (f32[2048]{0:T(1024)}, f32[2048]{0:T(1024)S(1)}, u32[]{:S(2)}) copy-start(f32[2048]{0:T(1024)S(1)} %multiply_reduce_fusion.5) | copy-start | bytes 24580
  339.7 10.8 %copy-start.6 = (f32[2048,512]{1,0:T(8,128)S(1)}, f32[2048,512]{1,0:T(8,128)}, u32[]{:S(2)}) copy-start(f32[2048,512]{1,0:T(8,128)} %copy-done.5) | copy-start | bytes 12582916
  339.7 10.8 %copy-start.51 = (bf16[2048,2048]{1,0:T(8,128)(2,1)S(1)}, bf16[2048,2048]{1,0:T(8,128)(2,1)}, u32[]{:S(2)}) copy-start(bf16[2048,2048]{1,0:T(8,128)(2,1)} %get-tuple-element.79) | copy-start | bytes 25165828
  369.7 9.9 %copy-start.33 = (bf16[1,512]{1,0:T(2,128)(2,1)S(1)}, bf16[1,512]{1,0:T(2,128)(2,1)}, u32[]{:S(2)}) copy-start(bf16[1,512]{1,0:T(2,128)(2,1)} %convert_element_type.303) | copy-start | bytes 3076
  550.9 202.8 %reduce-scatter.2.cloned.1.call-start = ((), (), s32[]{:S(2)}) async-start(), calls=%async_computation.4 | async-start | bytes 3760128 | tf_op jit(solution)/shard_map/reduce_scatter | solution.py:353
  558.6 9.3 %copy-start.47 = (bf16[512]{0:T(512)(128)(2,1)S(1)}, bf16[512]{0:T(512)(128)(2,1)}, u32[]{:S(2)}) copy-start(bf16[512]{0:T(512)(128)(2,1)} %param.40) | copy-start | bytes 3076
  579.3 33.7 %all-to-all-start = ((bf16[8,256,512]{2,1,0:T(8,128)(2,1)}), bf16[8,256,512]{2,1,0:T(8,128)(2,1)S(1)}, u32[]{:S(2)}, u32[]{:S(2)}) async-start(bf16[8,256,512]{2,1,0:T(8,128)(2,1)} %bitcast.58), calls=%async_computation | async-start | bytes 4194304 | tf_op jit(solution)/shard_map/all_to_all | solution.py:224
  583.0 320.7 %all-reduce.5.cloned.1.call-start = ((), (), s32[]{:S(2)}) async-start(), calls=%async_computation.6 | async-start | bytes 4734976 | tf_op jit(solution)/shard_map/psum | solution.py:239
  594.1 159.6 %copy-start.50 = (bf16[408,768]{1,0:T(8,128)(2,1)S(1)}, bf16[408,768]{1,0:T(8,128)(2,1)}, u32[]{:S(2)}) copy-start(bf16[408,768]{1,0:T(8,128)(2,1)} %param.21) | copy-start | bytes 1880068
  613.0 155.8 %copy-start.9 = (bf16[8,256,512]{2,1,0:T(8,128)(2,1)}, bf16[8,256,512]{2,1,0:T(8,128)(2,1)S(1)}, u32[]{:S(2)}) copy-start(bf16[8,256,512]{2,1,0:T(8,128)(2,1)S(1)} %all-to-all-done) | copy-start | bytes 6291460
  907.2 10.5 %copy-start.1 = (bf16[512,2048]{1,0:T(8,128)(2,1)S(1)}, bf16[512,2048]{1,0:T(8,128)(2,1)}, u32[]{:S(2)}) copy-start(bf16[512,2048]{1,0:T(8,128)(2,1)} %param.37) | copy-start | bytes 6291460
  (26 other events, 131.4 us)
Sparse Core Ops, SparseCore 0:
  10.9 46.7 all-gather.1
  551.0 152.5 all-reduce.2
  707.1 46.5 reduce-scatter.1
  768.9 134.7 all-reduce.4

commit v2 on v1

v2 whole, which is shorter than its diff:
```python
from functools import partial
import math

import jax
import jax.numpy as jnp
from jax import lax
from jax.experimental import pallas as pl
from jax.experimental.pallas import tpu as pltpu
from jax.sharding import PartitionSpec as P

HEADS = 16
HEAD_DIM = 32
PACK = 128 // HEAD_DIM
VMEM_LIMIT = 56 * 1024 * 1024
MESH = pl.DeviceIdType.MESH
LOG2E = math.log2(math.e)
QUERY_SCALE = LOG2E * HEAD_DIM ** (-0.5)


epsilon = 1e-06


def whole(shape):
    return pl.BlockSpec(shape, lambda *_: (0,) * len(shape))


def turned(values):
    return values.astype(jnp.float32).T.astype(values.dtype)


def sinusoid(places, table_width):
    half_width = table_width // 2
    frequency = jnp.exp(-math.log(10000.0) * jnp.arange(half_width, dtype=jnp.float32) / half_width)
    angles = places.astype(jnp.float32)[:, None] * frequency[None, :]
    return jnp.concatenate([jnp.sin(angles), jnp.cos(angles)], axis=1)


def plain_dot(left, right):
    return jnp.dot(left, right, preferred_element_type=jnp.float32)


def lead_dot(left, right):
    return lax.dot_general(
        left, right, (((0,), (0,)), ((), ())), preferred_element_type=jnp.float32
    )


def trail_dot(left, right):
    return lax.dot_general(
        left, right, (((1,), (1,)), ((), ())), preferred_element_type=jnp.float32
    )


def column_sum(values):
    return jnp.sum(values.astype(jnp.float32), axis=0, keepdims=True)


def row_mean(values):
    return jnp.mean(values, axis=-1, keepdims=True)


def normalize(values):
    center = values - row_mean(values)
    scale = lax.rsqrt(row_mean(center * center) + epsilon)
    return center * scale, scale


def normalize_back(grad, normed, scale):
    return scale * (grad - row_mean(grad) - normed * row_mean(grad * normed))


class Spot:
    def __init__(self):
        self.layers, self.splits = lax.axis_size("dp"), lax.axis_size("seq")
        self.half = self.splits // 2
        self.layer, self.index = lax.axis_index("dp"), lax.axis_index("seq")
        self.core, self.chip = self.index % 2, self.index // 2

    def sibling(self):
        return (self.layer, self.chip * 2 + (1 - self.core))

    def chip_at(self, step):
        return (self.chip + step) % self.half

    def layer_at(self, step):
        return (self.layer + step) % self.layers

    def peer(self, step):
        return (self.layer, self.chip_at(step) * 2 + self.core)

    def above(self, step):
        return (self.layer_at(step), self.index)

    def meet(self, others):
        barrier = pltpu.get_barrier_semaphore()
        for other in others:
            pl.semaphore_signal(barrier, inc=1, device_id=other, device_id_type=MESH)
        return len(others)

    def tree(self, layers=True):
        others = [self.sibling()] + [self.peer(step) for step in range(1, self.half)]
        if layers:
            others += [self.above(step) for step in range(1, self.layers)]
        return others


def padded(rows, unit):
    return -(-rows // unit) * unit


def span_of(start, size):
    return pl.ds(pl.multiple_of(start, 16), size)


def send(source, target, sems, at, device):
    return pltpu.make_async_remote_copy(
        src_ref=source,
        dst_ref=target,
        send_sem=sems.at[0, at],
        recv_sem=sems.at[1, at],
        device_id=device,
        device_id_type=MESH,
    )


class TreeSum:
    def __init__(self, spot, source, result, refs, scatter):
        (
            self.near,
            self.near_sum,
            self.far,
            self.far_sum,
            self.deep,
            self.done,
            self.sems,
            self.local,
        ) = refs
        self.spot, self.source, self.result, self.scatter = spot, source, result, scatter
        self.part = self.far_sum.shape[0]
        self.piece = self.done.shape[0]

    @staticmethod
    def scratch(rows, width, scatter, splits, layers):
        half = splits // 2
        part = rows // splits
        piece = part // layers if scatter else part
        low = jnp.bfloat16
        return [
            pltpu.VMEM((half * part, width), low),
            pltpu.VMEM((half * part, width), low),
            pltpu.VMEM((max(half - 1, 1) * part, width), low),
            pltpu.VMEM((part, width), low),
            pltpu.VMEM((layers * piece, width), low),
            pltpu.VMEM((piece, width), low),
            pltpu.SemaphoreType.DMA((2, 2 + 2 * half + 2 * layers)),
            pltpu.SemaphoreType.DMA((2,)),
        ]

    def near_copy(self):
        spot = self.spot
        rows = spot.half * self.part
        return send(
            self.source.at[span_of((1 - spot.core) * rows, rows)],
            self.near,
            self.sems,
            0,
            spot.sibling(),
        )

    def own_copy(self):
        rows = self.spot.half * self.part
        return pltpu.make_async_copy(
            self.source.at[span_of(self.spot.core * rows, rows)], self.near_sum, self.local.at[0]
        )

    def far_copy(self, step):
        return send(
            self.near_sum.at[span_of(self.spot.chip_at(step) * self.part, self.part)],
            self.far.at[span_of((step - 1) * self.part, self.part)],
            self.sems,
            1 + step,
            self.spot.peer(step),
        )

    def deep_copy(self, step):
        spot = self.spot
        if self.scatter:
            source = self.far_sum.at[span_of(spot.layer_at(step) * self.piece, self.piece)]
        else:
            source = self.far_sum
        return send(
            source,
            self.deep.at[span_of(spot.layer * self.piece, self.piece)],
            self.sems,
            1 + spot.half + step,
            spot.above(step),
        )

    def place(self, core, chip, layer=None):
        spot = self.spot
        start = (core * spot.half + chip) * self.part
        if layer is None:
            return span_of(start, self.part)
        return span_of(start + layer * self.piece, self.piece)

    def done_copy(self):
        spot = self.spot
        layer = spot.layer if self.scatter else None
        return pltpu.make_async_copy(
            self.done, self.result.at[self.place(spot.core, spot.chip, layer)], self.local.at[1]
        )

    def layer_copy(self, step, arriving):
        spot = self.spot
        layer = spot.layer_at(-step) if arriving else spot.layer
        return send(
            self.done,
            self.result.at[self.place(spot.core, spot.chip, layer)],
            self.sems,
            1 + spot.half + spot.layers + step,
            spot.above(step),
        )

    def part_copy(self, step, arriving):
        spot = self.spot
        place = self.place(spot.core, spot.chip_at(-step) if arriving else spot.chip)
        return send(
            self.result.at[place] if self.scatter else self.done,
            self.result.at[place],
            self.sems,
            1 + spot.half + 2 * spot.layers + step,
            spot.peer(step),
        )

    def half_copy(self, arriving):
        spot = self.spot
        rows = spot.half * self.part
        core = 1 - spot.core if arriving else spot.core
        place = span_of(core * rows, rows)
        return send(
            self.result.at[place], self.result.at[place], self.sems, 1, spot.sibling()
        )

    def start(self):
        self.own_copy().start()
        self.near_copy().start()

    def near_to_far(self):
        self.own_copy().wait()
        self.near_copy().wait()
        unit = self.part
        while unit > 160 and unit % 32 == 0:
            unit //= 2

        def add(at, _):
            rows = span_of(at * unit, unit)
            self.near_sum[rows, :] = (
                self.near_sum[rows, :].astype(jnp.float32) + self.near[rows, :].astype(jnp.float32)
            ).astype(jnp.bfloat16)
            return 0

        lax.fori_loop(0, self.spot.half * (self.part // unit), add, 0)
        for step in range(1, self.spot.half):
            self.far_copy(step).start()

    def far_to_deep(self):
        spot = self.spot
        for step in range(1, spot.half):
            self.far_copy(step).wait()
        unit = self.part
        while unit > 160 and unit % 32 == 0:
            unit //= 2

        def add(at, _):
            start = at * unit
            total = self.near_sum[span_of(spot.chip * self.part + start, unit), :].astype(
                jnp.float32
            )
            for step in range(1, spot.half):
                total = total + self.far[span_of((step - 1) * self.part + start, unit), :].astype(
                    jnp.float32
                )
            self.far_sum[span_of(start, unit), :] = total.astype(jnp.bfloat16)
            return 0

        lax.fori_loop(0, self.part // unit, add, 0)
        for step in range(1, spot.layers):
            self.deep_copy(step).start()
        own = self.far_sum[...]
        if self.scatter:
            own = self.far_sum[span_of(spot.layer * self.piece, self.piece), :]
        self.deep[span_of(spot.layer * self.piece, self.piece), :] = own

    def deep_to_layer(self):
        spot = self.spot
        for step in range(1, spot.layers):
            self.deep_copy(step).wait_send()
        for step in range(1, spot.layers):
            send(
                self.done,
                self.deep.at[span_of(spot.layer_at(-step) * self.piece, self.piece)],
                self.sems,
                1 + spot.half + step,
                spot.above(step),
            ).wait_recv()
        total = self.deep[: self.piece, :].astype(jnp.float32)
        for layer in range(1, spot.layers):
            total = total + self.deep[layer * self.piece : (layer + 1) * self.piece, :].astype(
                jnp.float32
            )
        self.done[...] = total.astype(jnp.bfloat16)
        self.done_copy().start()
        if self.scatter:
            for step in range(1, spot.layers):
                self.layer_copy(step, False).start()
        else:
            for step in range(1, spot.half):
                self.part_copy(step, False).start()

    def layer_to_part(self):
        spot = self.spot
        if not self.scatter:
            return
        self.done_copy().wait()
        for step in range(1, spot.layers):
            self.layer_copy(step, False).wait_send()
        for step in range(1, spot.layers):
            self.layer_copy(step, True).wait_recv()
        for step in range(1, spot.half):
            self.part_copy(step, False).start()

    def part_to_half(self):
        spot = self.spot
        if not self.scatter:
            self.done_copy().wait()
        for step in range(1, spot.half):
            self.part_copy(step, False).wait_send()
        for step in range(1, spot.half):
            self.part_copy(step, True).wait_recv()
        self.half_copy(False).start()

    def finish(self):
        self.half_copy(False).wait_send()
        self.half_copy(True).wait_recv()


def enter_kernel(
    embedded_ref,
    slot_ref,
    table_ref,
    mask_ref,
    gain_ref,
    shift_ref,
    joint_ref,
    query_bias_ref,
    value_bias_ref,
    stream_ref,
    empty_ref,
    normed_ref,
    query_t_ref,
    key_ref,
    key_t_ref,
    value_ref,
    value_t_ref,
):
    block, width = stream_ref.shape
    place = lax.broadcasted_iota(jnp.int32, (block, 1), 0) + pl.program_id(0) * block
    fills = (place == slot_ref[...]).astype(jnp.float32)
    empty = 1.0 - jnp.sum(fills, axis=1, keepdims=True)
    placed = plain_dot(fills.astype(jnp.bfloat16), embedded_ref[...])
    stream = placed + empty * mask_ref[...].astype(jnp.float32) + table_ref[...]
    stream_ref[...] = stream
    empty_ref[...] = empty
    normed, _ = normalize(stream)
    low = (normed * gain_ref[...].astype(jnp.float32) + shift_ref[...].astype(jnp.float32)).astype(
        jnp.bfloat16
    )
    normed_ref[...] = low
    query = plain_dot(low, joint_ref[:, :width]) + query_bias_ref[...].astype(jnp.float32)
    query_t_ref[...] = (query * QUERY_SCALE).T.astype(jnp.bfloat16)
    keys = plain_dot(low, joint_ref[:, width : 2 * width])
    key_ref[...] = keys.astype(jnp.bfloat16)
    key_t_ref[...] = keys.T.astype(jnp.bfloat16)
    values = plain_dot(low, joint_ref[:, 2 * width :]) + value_bias_ref[...].astype(jnp.float32)
    value_ref[...] = values.astype(jnp.bfloat16)
    value_t_ref[...] = values.T.astype(jnp.bfloat16)


def enter(embedded_all, slot_place, table, mask_token, gain, shift, joint_weight, query_bias, value_bias):
    rows, width = table.shape
    slots = embedded_all.shape[0]
    block = min(256, rows)
    row_block = pl.BlockSpec((block, width), lambda i: (i, 0))
    lane_block = pl.BlockSpec((width, block), lambda i: (0, i))
    vector = whole((1, width))
    low = jax.ShapeDtypeStruct((rows, width), jnp.bfloat16)
    low_t = jax.ShapeDtypeStruct((width, rows), jnp.bfloat16)
    return pl.pallas_call(
        enter_kernel,
        grid=(rows // block,),
        in_specs=[
            whole((slots, width)),
            whole((1, slots)),
            row_block,
            vector,
            vector,
            vector,
            whole((width, 3 * width)),
            vector,
            vector,
        ],
        out_specs=[
            row_block,
            pl.BlockSpec((block, 1), lambda i: (i, 0)),
            row_block,
            lane_block,
            row_block,
            lane_block,
            row_block,
            lane_block,
        ],
        out_shape=[
            jax.ShapeDtypeStruct((rows, width), jnp.float32),
            jax.ShapeDtypeStruct((rows, 1), jnp.float32),
            low,
            low_t,
            low,
            low_t,
            low,
            low_t,
        ],
        compiler_params=pltpu.CompilerParams(vmem_limit_bytes=VMEM_LIMIT),
        cost_estimate=pl.CostEstimate(
            flops=2 * rows * width * (slots + 3 * width),
            bytes_accessed=20 * rows * width,
            transcendentals=0,
        ),
        name="enter",
    )(
        embedded_all,
        slot_place[None, :],
        table,
        mask_token[None, :],
        gain[None, :],
        shift[None, :],
        joint_weight,
        query_bias[None, :],
        value_bias[None, :],
    )


def attend_kernel(
    key_ref, query_ref, value_ref, mixed_ref, exact_ref, total_ref, raised_ref, scores_ref
):
    span = key_ref.shape[0]
    block = query_ref.shape[1]
    slice_rows = min(256, span)
    query = query_ref[...]
    head_row = lax.broadcasted_iota(jnp.int32, query.shape, 0) // HEAD_DIM
    ones = jnp.ones((16, slice_rows), jnp.bfloat16)
    highest = None
    for step in range(PACK + 1):
        if step < PACK:
            own_query = jnp.where(head_row == step, query, jnp.zeros_like(query))
            partial_highest = jnp.full((8, block), -jnp.inf, jnp.float32)
        if step > 0:
            head = step - 1
            rows = slice(head * HEAD_DIM, (head + 1) * HEAD_DIM)
            mixed = jnp.zeros((HEAD_DIM + 16, block), jnp.float32)
        for at in range(0, span, slice_rows):
            part = slice(at, at + slice_rows)
            if step < PACK:
                scores = plain_dot(key_ref[part, :], own_query)
                scores_ref[step % 2, part, :] = scores
                partial_highest = jnp.maximum(
                    partial_highest, jnp.max(scores.reshape(slice_rows // 8, 8, block), axis=0)
                )
            if step > 0:
                raised = jnp.exp2(scores_ref[(step - 1) % 2, part, :] - highest).astype(
                    jnp.bfloat16
                )
                raised_ref[head, part, :] = raised
                mixed = mixed + plain_dot(
                    jnp.concatenate([value_ref[rows, part], ones], axis=0), raised
                )
        if step > 0:
            total = mixed[HEAD_DIM : HEAD_DIM + 1]
            total_ref[0, head : head + 1, :] = total
            mixed = mixed[:HEAD_DIM] / total
            exact_ref[rows, :] = mixed
            mixed_ref[rows, :] = mixed.astype(jnp.bfloat16)
        if step < PACK:
            highest = jnp.max(partial_highest, axis=0, keepdims=True)


def attend(keys, query_t, value_t):
    width, rows = query_t.shape
    span = keys.shape[0]
    block = min(512, rows)
    groups = width // 128
    lane_block = pl.BlockSpec((128, block), lambda g, i: (g, i))
    return pl.pallas_call(
        attend_kernel,
        grid=(groups, rows // block),
        in_specs=[
            pl.BlockSpec((span, 128), lambda g, i: (0, g)),
            lane_block,
            pl.BlockSpec((128, span), lambda g, i: (g, 0)),
        ],
        out_specs=[
            lane_block,
            lane_block,
            pl.BlockSpec((1, 8, block), lambda g, i: (g, 0, i)),
            pl.BlockSpec((PACK, span, block), lambda g, i: (g, 0, i)),
        ],
        out_shape=[
            jax.ShapeDtypeStruct((width, rows), jnp.bfloat16),
            jax.ShapeDtypeStruct((width, rows), jnp.float32),
            jax.ShapeDtypeStruct((groups, 8, rows), jnp.float32),
            jax.ShapeDtypeStruct((HEADS, span, rows), jnp.bfloat16),
        ],
        scratch_shapes=[pltpu.VMEM((2, span, block), jnp.float32)],
        compiler_params=pltpu.CompilerParams(vmem_limit_bytes=VMEM_LIMIT),
        cost_estimate=pl.CostEstimate(
            flops=HEADS * span * rows * 512,
            bytes_accessed=2 * HEADS * span * rows,
            transcendentals=HEADS * span * rows,
        ),
        name="attend",
    )(keys, query_t, value_t)


def middle_kernel(
    stream_ref,
    mixed_ref,
    cotangent_ref,
    output_ref,
    output_bias_ref,
    gain_ref,
    shift_ref,
    expand_ref,
    expand_bias_ref,
    contract_ref,
    contract_bias_ref,
    decoded_ref,
    grad_middle_ref,
    grad_attended_ref,
    flat_ref,
    small_ref,
    expand_sum,
    contract_sum,
    output_sum,
    small_sum,
):
    width = stream_ref.shape[1]
    chunks = expand_ref.shape[1] // width

    @pl.when(pl.program_id(0) == 0)
    def _():
        expand_sum[...] = jnp.zeros_like(expand_sum)
        contract_sum[...] = jnp.zeros_like(contract_sum)
        output_sum[...] = jnp.zeros_like(output_sum)
        small_sum[...] = jnp.zeros_like(small_sum)

    mixed_t = mixed_ref[...]
    cotangent = cotangent_ref[...]
    middle = (
        stream_ref[...]
        + plain_dot(turned(mixed_t), output_ref[...])
        + output_bias_ref[...].astype(jnp.float32)
    )
    normed, scale = normalize(middle)
    gain = gain_ref[...].astype(jnp.float32)
    low = (normed * gain + shift_ref[...].astype(jnp.float32)).astype(jnp.bfloat16)
    low_t = turned(low)
    output = middle + contract_bias_ref[...].astype(jnp.float32)
    grad_normed = jnp.zeros_like(middle)
    for chunk in range(chunks):
        part = slice(chunk * width, (chunk + 1) * width)
        hidden = plain_dot(low, expand_ref[:, part]) + expand_bias_ref[:, part].astype(jnp.float32)
        below = 0.5 + 0.5 * lax.erf(hidden * math.sqrt(0.5))
        slope = below + hidden * jnp.exp(-0.5 * hidden * hidden) * (1.0 / math.sqrt(2 * math.pi))
        active = (hidden * below).astype(jnp.bfloat16)
        grad_hidden = (trail_dot(cotangent, contract_ref[part, :]) * slope).astype(jnp.bfloat16)
        output = output + plain_dot(active, contract_ref[part, :])
        grad_normed = grad_normed + trail_dot(grad_hidden, expand_ref[:, part])
        contract_sum[part, :] += plain_dot(turned(active), cotangent)
        expand_sum[part, :] += plain_dot(low_t, grad_hidden)
        small_sum[chunk : chunk + 1, :] += column_sum(grad_hidden)
    decoded_ref[...] = output.astype(jnp.bfloat16)
    grad_middle = cotangent.astype(jnp.float32) + normalize_back(grad_normed * gain, normed, scale)
    grad_middle_ref[...] = grad_middle
    branch = grad_middle.astype(jnp.bfloat16)
    grad_attended_ref[...] = trail_dot(output_ref[...], branch).astype(jnp.bfloat16)
    output_sum[...] += plain_dot(mixed_t, branch)
    small_sum[chunks : chunks + 1, :] += column_sum(cotangent)
    small_sum[chunks + 1 : chunks + 2, :] += column_sum(branch)
    small_sum[chunks + 2 : chunks + 3, :] += column_sum(grad_normed * normed)
    small_sum[chunks + 3 : chunks + 4, :] += column_sum(grad_normed)

    @pl.when(pl.program_id(0) == pl.num_programs(0) - 1)
    def _():
        at = 0
        for total in (expand_sum, contract_sum, output_sum):
            flat_ref[at : at + total.shape[0], :] = total[...].astype(flat_ref.dtype)
            at += total.shape[0]
        if at < flat_ref.shape[0]:
            flat_ref[at:, :] = jnp.zeros((flat_ref.shape[0] - at, width), flat_ref.dtype)
        small_ref[...] = small_sum[...]


def middle_block(
    stream,
    mixed_t,
    cotangent,
    output_weight,
    output_bias,
    gain,
    shift,
    expand_weight,
    expand_bias,
    contract_weight,
    contract_bias,
    flat_rows,
):
    rows, width = stream.shape
    hidden = expand_weight.shape[1]
    block = min(256, rows)
    row_block = pl.BlockSpec((block, width), lambda i: (i, 0))
    lane_block = pl.BlockSpec((width, block), lambda i: (0, i))
    vector = whole((1, width))
    small_rows = hidden // width + 4
    return pl.pallas_call(
        middle_kernel,
        grid=(rows // block,),
        in_specs=[
            row_block,
            lane_block,
            row_block,
            whole((width, width)),
            vector,
            vector,
            vector,
            whole((width, hidden)),
            whole((1, hidden)),
            whole((hidden, width)),
            vector,
        ],
        out_specs=[
            row_block,
            row_block,
            lane_block,
            whole((flat_rows, width)),
            whole((small_rows, width)),
        ],
        out_shape=[
            jax.ShapeDtypeStruct((rows, width), jnp.bfloat16),
            jax.ShapeDtypeStruct((rows, width), jnp.float32),
            jax.ShapeDtypeStruct((width, rows), jnp.bfloat16),
            jax.ShapeDtypeStruct((flat_rows, width), jnp.bfloat16),
            jax.ShapeDtypeStruct((small_rows, width), jnp.float32),
        ],
        scratch_shapes=[
            pltpu.VMEM((hidden, width), jnp.float32),
            pltpu.VMEM((hidden, width), jnp.float32),
            pltpu.VMEM((width, width), jnp.float32),
            pltpu.VMEM((small_rows, width), jnp.float32),
        ],
        compiler_params=pltpu.CompilerParams(vmem_limit_bytes=VMEM_LIMIT),
        cost_estimate=pl.CostEstimate(
            flops=2 * rows * width * (6 * hidden + 3 * width),
            bytes_accessed=16 * rows * width,
            transcendentals=2 * rows * hidden,
        ),
        name="middle",
    )(
        stream,
        mixed_t,
        cotangent,
        output_weight,
        output_bias[None, :],
        gain[None, :],
        shift[None, :],
        expand_weight,
        expand_bias[None, :],
        contract_weight,
        contract_bias[None, :],
    )


def attend_back_kernel(
    steps,
    raised_ref,
    total_ref,
    value_ref,
    key_ref,
    query_ref,
    exact_ref,
    grad_ref,
    flat_ref,
    rows_ref,
    grad_query_ref,
    grad_key_ref,
    grad_value_ref,
    summed_ref,
    decoded_ref,
    key_sum,
    value_sum,
    exchange_sems,
    exchange_local,
    *sum_refs,
):
    spot = Spot()
    tree = TreeSum(spot, flat_ref, summed_ref, sum_refs, True)
    clips, share = decoded_ref.shape[0], decoded_ref.shape[1]
    mine, part = spot.index % clips, spot.index // clips

    def member(step):
        return (mine + step) % clips

    def exchange(step):
        return send(
            rows_ref.at[span_of(member(step) * share, share)],
            decoded_ref.at[mine],
            exchange_sems,
            step,
            (spot.layer, part * clips + member(step)),
        )

    def own_rows():
        return pltpu.make_async_copy(
            rows_ref.at[span_of(mine * share, share)], decoded_ref.at[mine], exchange_local
        )

    step_now = pl.program_id(0) * pl.num_programs(1) + pl.program_id(1)

    def at_step(fraction):
        return pl.when(step_now == fraction * steps // 32)

    @at_step(0)
    def _():
        others = spot.tree() + [
            (spot.layer, part * clips + member(step)) for step in range(1, clips)
        ]
        count = spot.meet(others)
        pl.semaphore_wait(pltpu.get_barrier_semaphore(), count)
        tree.start()

    @at_step(2)
    def _():
        tree.near_to_far()

    @at_step(9)
    def _():
        tree.far_to_deep()
        own_rows().start()
        for step in range(1, clips):
            exchange(step).start()

    @at_step(13)
    def _():
        tree.deep_to_layer()

    @at_step(17)
    def _():
        tree.layer_to_part()

    @at_step(25)
    def _():
        tree.part_to_half()

    @at_step(31)
    def _():
        tree.finish()
        own_rows().wait()
        for step in range(1, clips):
            exchange(step).wait_send()
        for step in range(1, clips):
            send(
                rows_ref.at[span_of(mine * share, share)],
                decoded_ref.at[member(-step)],
                exchange_sems,
                step,
                (spot.layer, part * clips + member(step)),
            ).wait_recv()

    @pl.when(pl.program_id(1) == 0)
    def _():
        key_sum[...] = jnp.zeros_like(key_sum)
        value_sum[...] = jnp.zeros_like(value_sum)

    block = query_ref.shape[1]
    head_row = lax.broadcasted_iota(jnp.int32, (128, block), 0) // HEAD_DIM
    head_col = lax.broadcasted_iota(jnp.int32, (block, 128), 1) // HEAD_DIM
    inverse = 1.0 / total_ref[0, 0:PACK]
    inverse = jnp.concatenate(
        [jnp.broadcast_to(inverse[h : h + 1], (HEAD_DIM, block)) for h in range(PACK)], axis=0
    )
    grad_low = (grad_ref[...].astype(jnp.float32) * inverse).astype(jnp.bfloat16)
    grad = grad_low.astype(jnp.float32)
    inner = grad * exact_ref[...]
    grad_turned = grad.T.astype(jnp.bfloat16)
    query_turned = turned(query_ref[...])
    for head in range(PACK):
        rows = slice(head * HEAD_DIM, (head + 1) * HEAD_DIM)
        own_grad = jnp.where(head_row == head, grad_low, jnp.zeros_like(grad_low))
        grad_weight = plain_dot(value_ref[...], own_grad)
        row_inner = jnp.sum(inner[rows], axis=0, keepdims=True)
        raised = raised_ref[head]
        grad_scores = raised * (grad_weight - row_inner).astype(jnp.bfloat16)
        value_sum[...] += plain_dot(
            raised, jnp.where(head_col == head, grad_turned, jnp.zeros_like(grad_turned))
        )
        key_sum[...] += plain_dot(
            grad_scores, jnp.where(head_col == head, query_turned, jnp.zeros_like(query_turned))
        )
        grad_query_ref[rows, :] = (
            plain_dot(key_ref[rows, :], grad_scores) * HEAD_DIM ** (-0.5)
        ).astype(jnp.bfloat16)

    @pl.when(pl.program_id(1) == pl.num_programs(1) - 1)
    def _():
        grad_key_ref[...] = (key_sum[...] * (1.0 / LOG2E)).astype(jnp.bfloat16)
        grad_value_ref[...] = value_sum[...].astype(jnp.bfloat16)


def attend_back(raised, total, values, key_t, query_t, exact_t, grad_t, flat, decoded_rows):
    splits, layers = lax.axis_size("seq"), lax.axis_size("dp")
    clips, share, _ = decoded_rows.shape
    width, rows = query_t.shape
    span = values.shape[0]
    block = min(256, rows)
    groups = width // 128
    lane_block = pl.BlockSpec((128, block), lambda g, i: (g, i))
    return pl.pallas_call(
        partial(attend_back_kernel, groups * (rows // block)),
        grid=(groups, rows // block),
        in_specs=[
            pl.BlockSpec((PACK, span, block), lambda g, i: (g, 0, i)),
            pl.BlockSpec((1, 8, block), lambda g, i: (g, 0, i)),
            pl.BlockSpec((span, 128), lambda g, i: (0, g)),
            pl.BlockSpec((128, span), lambda g, i: (g, 0)),
            lane_block,
            lane_block,
            lane_block,
            pl.BlockSpec(memory_space=pl.ANY),
            pl.BlockSpec(memory_space=pl.ANY),
        ],
        out_specs=[
            lane_block,
            pl.BlockSpec((span, 128), lambda g, i: (0, g)),
            pl.BlockSpec((span, 128), lambda g, i: (0, g)),
            pl.BlockSpec(memory_space=pl.ANY),
            pl.BlockSpec(memory_space=pl.ANY),
        ],
        out_shape=[
            jax.ShapeDtypeStruct((width, rows), jnp.bfloat16),
            jax.ShapeDtypeStruct((span, width), jnp.bfloat16),
            jax.ShapeDtypeStruct((span, width), jnp.bfloat16),
            jax.ShapeDtypeStruct(flat.shape, flat.dtype),
            jax.ShapeDtypeStruct(decoded_rows.shape, decoded_rows.dtype),
        ],
        scratch_shapes=[
            pltpu.VMEM((span, 128), jnp.float32),
            pltpu.VMEM((span, 128), jnp.float32),
            pltpu.SemaphoreType.DMA((2, clips)),
            pltpu.SemaphoreType.DMA,
        ]
        + TreeSum.scratch(flat.shape[0], flat.shape[1], True, splits, layers),
        compiler_params=pltpu.CompilerParams(
            vmem_limit_bytes=VMEM_LIMIT, collective_id=1, has_side_effects=True
        ),
        cost_estimate=pl.CostEstimate(
            flops=HEADS * span * rows * 1024,
            bytes_accessed=2 * HEADS * span * rows,
            transcendentals=0,
        ),
        name="attend_back",
    )(raised, total, values, key_t, query_t, exact_t, grad_t, flat, decoded_rows.reshape(clips * share, width))


def leave_kernel(
    grad_query_ref,
    grad_key_ref,
    grad_value_ref,
    stream_ref,
    empty_ref,
    low_ref,
    grad_middle_ref,
    gain_ref,
    joint_ref,
    slot_ref,
    back_ref,
    grad_joint_ref,
    small_ref,
    joint_sum,
    small_sum,
    grad_all,
):
    block, width = stream_ref.shape
    step = pl.program_id(0)

    @pl.when(step == 0)
    def _():
        joint_sum[...] = jnp.zeros_like(joint_sum)
        small_sum[...] = jnp.zeros_like(small_sum)

    normed, scale = normalize(stream_ref[...])
    low_t = turned(low_ref[...])
    sides = [turned(grad_query_ref[...]), grad_key_ref[...], grad_value_ref[...]]
    grad_normed = jnp.zeros_like(normed)
    for at, side in enumerate(sides):
        grad_normed = grad_normed + trail_dot(side, joint_ref[:, at * width : (at + 1) * width])
        joint_sum[at * width : (at + 1) * width, :] += plain_dot(low_t, side)
    grad_stream = grad_middle_ref[...] + normalize_back(
        grad_normed * gain_ref[...].astype(jnp.float32), normed, scale
    )
    grad_all[pl.ds(pl.multiple_of(step * block, block), block), :] = grad_stream.astype(jnp.bfloat16)
    small_sum[0:1, :] += column_sum(empty_ref[...] * grad_stream)
    small_sum[1:2, :] += column_sum(grad_normed * normed)
    small_sum[2:3, :] += column_sum(grad_normed)
    small_sum[3:4, :] += column_sum(sides[0])
    small_sum[4:5, :] += column_sum(sides[2])

    @pl.when(step == pl.num_programs(0) - 1)
    def _():
        grad_joint_ref[...] = joint_sum[...].astype(grad_joint_ref.dtype)
        small_ref[...] = small_sum[...]
        slots = back_ref.shape[0]
        place = lax.broadcasted_iota(jnp.int32, (1, grad_all.shape[0]), 1)
        part = slots // 8
        for at in range(0, slots, part):
            takes = (slot_ref[at : at + part, :] == place).astype(jnp.float32).astype(jnp.bfloat16)
            back_ref[at : at + part, :] = plain_dot(takes, grad_all[...]).astype(jnp.bfloat16)


def leave(grad_query_t, grad_key, grad_value, stream, empty, low, grad_middle, gain, joint_weight, slot_place):
    rows, width = stream.shape
    slots = slot_place.shape[0]
    block = min(256, rows)
    row_block = pl.BlockSpec((block, width), lambda i: (i, 0))
    lane_block = pl.BlockSpec((width, block), lambda i: (0, i))
    return pl.pallas_call(
        leave_kernel,
        grid=(rows // block,),
        in_specs=[
            lane_block,
            row_block,
            row_block,
            row_block,
            pl.BlockSpec((block, 1), lambda i: (i, 0)),
            row_block,
            row_block,
            whole((1, width)),
            whole((width, 3 * width)),
            whole((slots, 1)),
        ],
        out_specs=[whole((slots, width)), whole((3 * width, width)), whole((8, width))],
        out_shape=[
            jax.ShapeDtypeStruct((slots, width), jnp.bfloat16),
            jax.ShapeDtypeStruct((3 * width, width), jnp.bfloat16),
            jax.ShapeDtypeStruct((8, width), jnp.float32),
        ],
        scratch_shapes=[
            pltpu.VMEM((3 * width, width), jnp.float32),
            pltpu.VMEM((8, width), jnp.float32),
            pltpu.VMEM((rows, width), jnp.bfloat16),
        ],
        compiler_params=pltpu.CompilerParams(vmem_limit_bytes=VMEM_LIMIT),
        cost_estimate=pl.CostEstimate(
            flops=2 * rows * width * (slots + 6 * width),
            bytes_accessed=20 * rows * width,
            transcendentals=0,
        ),
        name="leave",
    )(
        grad_query_t,
        grad_key,
        grad_value,
        stream,
        empty,
        low,
        grad_middle,
        gain[None, :],
        joint_weight,
        slot_place[:, None],
    )


def body(
    latents,
    clip_ids,
    restore,
    counts,
    embed_weight,
    embed_bias,
    mask_token,
    first_gain,
    first_shift,
    joint_weight,
    query_bias,
    value_bias,
    output_weight,
    output_bias,
    second_gain,
    second_shift,
    expand_weight,
    expand_bias,
    contract_weight,
    contract_bias,
    cotangent,
):
    splits = lax.axis_size("seq")
    seq_index = lax.axis_index("seq")
    capacity = latents.shape[0]
    clip_count, clip_share, model_width = cotangent.shape
    sharers = splits // clip_count
    rows = clip_count * clip_share
    own_clip = seq_index % clip_count
    first_place = (seq_index // clip_count) * rows
    exchange_groups = [[s * clip_count + c for c in range(clip_count)] for s in range(sharers)]
    clip_groups = [[s * clip_count + c for s in range(sharers)] for c in range(clip_count)]

    def to_clips(blocks):
        return lax.all_to_all(
            blocks,
            "seq",
            split_axis=0,
            concat_axis=0,
            tiled=True,
            axis_index_groups=exchange_groups if sharers > 1 else None,
        )

    slot = jnp.arange(splits * capacity, dtype=jnp.int32)
    live = (slot % capacity) < jnp.repeat(counts, capacity)
    mine = live & (clip_ids % clip_count == own_clip)
    slot_place = jnp.where(mine, restore - first_place, -1)
    table = sinusoid(first_place + jnp.arange(rows, dtype=jnp.int32), model_width)

    embedded = (plain_dot(latents, embed_weight) + embed_bias.astype(jnp.float32)).astype(
        jnp.bfloat16
    )
    embedded_all = lax.all_gather(embedded, "seq", axis=0, tiled=True)
    grad_output = to_clips(cotangent).reshape(rows, model_width)

    stream, empty, first_low, query_t, keys, key_t, values, value_t = enter(
        embedded_all,
        slot_place,
        table,
        mask_token,
        first_gain,
        first_shift,
        joint_weight,
        query_bias,
        value_bias,
    )
    if sharers > 1:
        keys = lax.all_gather(keys, "seq", axis=0, tiled=True, axis_index_groups=clip_groups)
        values = lax.all_gather(values, "seq", axis=0, tiled=True, axis_index_groups=clip_groups)
        key_t, value_t = keys.T, values.T
    mixed_t, exact_t, total, raised = attend(keys, query_t, value_t)
    (
        decoded_rows,
        grad_middle,
        grad_attended_t,
        early_flat,
        early_small,
    ) = middle_block(
        stream,
        mixed_t,
        grad_output,
        output_weight,
        output_bias,
        second_gain,
        second_shift,
        expand_weight,
        expand_bias,
        contract_weight,
        contract_bias,
        padded(2 * expand_weight.shape[1] + model_width, splits * lax.axis_size("dp") * 16),
    )
    grad_query_t, grad_key, grad_value, early_sum, decoded = attend_back(
        raised,
        total,
        values,
        key_t,
        query_t,
        exact_t,
        grad_attended_t,
        early_flat,
        decoded_rows.reshape(clip_count, clip_share, model_width),
    )
    if sharers > 1:
        grad_key, grad_value = (
            lax.psum_scatter(
                side, "seq", scatter_dimension=0, tiled=True, axis_index_groups=clip_groups
            )
            for side in (grad_key, grad_value)
        )
    back_rows, grad_joint, late_small = leave(
        grad_query_t,
        grad_key,
        grad_value,
        stream,
        empty,
        first_low,
        grad_middle,
        first_gain,
        joint_weight,
        slot_place,
    )
    grad_embedded = lax.psum_scatter(back_rows, "seq", scatter_dimension=0, tiled=True)
    latent_grad = trail_dot(grad_embedded, embed_weight).astype(jnp.bfloat16)
    grad_embed_weight = lead_dot(latents, grad_embedded)
    grad_embed_bias = column_sum(grad_embedded)
    late_flat = jnp.concatenate(
        [
            grad_joint.astype(jnp.float32),
            grad_embed_weight,
            early_small,
            late_small,
            grad_embed_bias,
        ],
        axis=0,
    )
    late_sum = lax.psum(late_flat, ("dp", "seq"))

    def columns(stack):
        return jnp.concatenate(jnp.split(stack, stack.shape[0] // model_width, axis=0), axis=1)

    hidden_width = expand_weight.shape[1]
    chunks = hidden_width // model_width
    grad_expand = columns(early_sum[:hidden_width])
    grad_contract = early_sum[hidden_width : 2 * hidden_width]
    grad_output_weight = early_sum[2 * hidden_width : 2 * hidden_width + model_width]
    grad_expand, grad_contract, grad_output_weight = (
        summed.astype(jnp.float32) for summed in (grad_expand, grad_contract, grad_output_weight)
    )
    grad_joint_weight = columns(late_sum[: 3 * model_width])
    at = 3 * model_width + embed_weight.shape[0]
    grad_embed_weight = late_sum[3 * model_width : at]
    grad_expand_bias = late_sum[at : at + chunks].reshape(-1)
    at += chunks
    grad_contract_bias, grad_output_bias, grad_second_gain, grad_second_shift = late_sum[at : at + 4]
    at += 4
    (
        grad_mask,
        grad_first_gain,
        grad_first_shift,
        grad_query_bias,
        grad_value_bias,
    ) = late_sum[at : at + 5]
    grad_embed_bias = late_sum[at + 8]
    return (
        decoded,
        latent_grad,
        grad_embed_weight,
        grad_embed_bias,
        grad_mask,
        grad_first_gain,
        grad_first_shift,
        grad_joint_weight,
        grad_query_bias,
        grad_value_bias,
        grad_output_weight,
        grad_output_bias,
        grad_second_gain,
        grad_second_shift,
        grad_expand,
        grad_expand_bias,
        grad_contract,
        grad_contract_bias,
    )


def solution(mesh):
    placed = (
        (P(("dp", "seq"), None),) + (P("dp"),) * 3 + (P(),) * 16 + (P("dp", "seq", None),)
    )
    return jax.shard_map(
        body,
        mesh=mesh,
        in_specs=placed,
        out_specs=(P("dp", "seq", None), P(("dp", "seq"), None)) + (P(),) * 16,
        check_vma=False,
    )
```

time: 930 us -> 622 us (0.67)
  matrix products: 159 us -> 6.56 us
  waiting for transfers between devices: 296 us -> 199 us
  local copies, waits for them, and re-layouts: 91.6 us -> 23.5 us
  Pallas kernels: 303 us -> 339 us
  other arithmetic: 51.2 us -> 25.6 us
    pallas_call x1 -> x4, Pallas kernels: 136 us -> 235 us  [the longest x1 146 us: attend_back(): pl.pallas_call(partial(attend_back_kernel, groups * (rows // block)), gri...]
    dot_general x6 -> x1, matrix products: 77.2 us -> 2.35 us  [plain_dot(): return jnp.dot(left, right, preferred_element_type=jnp.float32)]
    psum x2 -> x1, waiting for transfers between devices: 206 us -> 134 us  [body(): late_sum = lax.psum(late_flat, ('dp', 'seq'))]
    pallas_call x1, Pallas kernels: 167 us -> 104 us  [attend(): pl.pallas_call(attend_kernel, grid=(groups, rows // block), in_specs=[pl....]
    dot_general x5 -> x1, matrix products: 43.9 us -> 1.35 us  [trail_dot(): lax.dot_general(left, right, (((1,), (1,)), ((), ())), preferred_element_...]
    dot_general x6 -> x1, matrix products: 38.1 us -> 2.86 us  [lead_dot(): lax.dot_general(left, right, (((0,), (0,)), ((), ())), preferred_element_...]
    all_to_all x2 -> x1, waiting for transfers between devices: 33.7 us -> 0.01 us  [to_clips(): lax.all_to_all(blocks, 'seq', split_axis=0, concat_axis=0, tiled=True, ax...]
    reduce_sum x11 -> x1, other arithmetic: 27 us -> 1.1 us  [column_sum(): return jnp.sum(values.astype(jnp.float32), axis=0, keepdims=True)]
  transfers between devices with their start and end apart: 6 -> 4, of which waited for: 6 -> 3; matrix products, arithmetic and copies ran while one was open for 9% -> 5% of each run, Pallas kernels for 0% -> 20%
where the time goes in v2:
time: 622 us; the launch traced here: 613 us
  Pallas kernels  339 us (55%)
  waiting for transfers between devices  199 us (32%)
  other arithmetic  25.6 us (4%)
  local copies, waits for them, and re-layouts  23.5 us (4%)
  between operations  14.4 us (2%)
  matrix products  6.56 us (1%)
    pallas_call x1, Pallas kernels, attend_back(): pl.pallas_call(partial(attend_back_kernel, groups * (rows // block)), gri...  146 us
    psum x1, waiting for transfers between devices, body(): late_sum = lax.psum(late_flat, ('dp', 'seq'))  134 us
    pallas_call x1, Pallas kernels, attend(): pl.pallas_call(attend_kernel, grid=(groups, rows // block), in_specs=[pl....  104 us
    pallas_call x1, Pallas kernels, middle_block(): pl.pallas_call(middle_kernel, grid=(rows // block,), in_specs=[row_block,...  46.1 us
    reduce_scatter x1, waiting for transfers between devices, body(): lax.psum_scatter(back_rows, 'seq', scatter_dimension=0, tiled=True)  42 us
    pallas_call x1, Pallas kernels, leave(): pl.pallas_call(leave_kernel, grid=(rows // block,), in_specs=[lane_block,...  24.1 us
    all_gather x1, waiting for transfers between devices, body(): embedded_all = lax.all_gather(embedded, 'seq', axis=0, tiled=True)  22.7 us
    pallas_call x1, Pallas kernels, enter(): pl.pallas_call(enter_kernel, grid=(rows // block,), in_specs=[whole((slot...  18.8 us
  transfers between devices with their start and end apart: 4, of which 3 were waited for; matrix products, arithmetic and copies ran while one was open for 5% of the time, Pallas kernels for 20%

profile of v2, /device:TPU:0, one launch (start us, length us, event | category | flops | bytes accessed | tf_op | source)
XLA Modules:
  0.0 613.2 jit_solution(407886967077973010)
XLA Ops:
  7.2 0.7 convert_element_type.31
  8.4 2.3 fusion
  10.8 5.3 all-to-all-start
  16.4 0.6 broadcast_in_dim.52.slot_ref
  17.0 2.3 broadcast_in_dim.65.slot_ref
  22.3 0.6 broadcast_in_dim.61.expand_bias_ref
  25.2 7.3 %multiply_sine_fusion = (f32[2048,256]{1,0:T(8,128)S(1)}, f32[2048,256]{1,0:T(8,128)S(1)}) fusion(f32[256]{0:T(256)S(1)} %multiply_exponential_fusion, f32[2048]{0:T(1024)S(1)} %add_convert_fusion), kind=kLoop, calls=%fused_computation.4 | loop fusion | flops 524288 | bytes 4203520 | tf_op jit(solution)/shard_map/sin | solution.py:35
  32.6 2.5 pad_maximum_fusion.table_ref
  35.1 22.7 %all-gather.2.cloned.1.call-done.embedded_ref = bf16[3264,512]{1,0:T(8,128)(2,1)} async-done(((bf16[408,512]{1,0:T(8,128)(2,1)}), bf16[3264,512]{1,0:T(8,128)(2,1)}) %all-gather.2.cloned.1.call-update) | async-done | bytes 3342352 | tf_op jit(solution)/shard_map/all_gather | solution.py:1043
  57.8 18.8 %enter.1 = (f32[2048,512]{1,0:T(8,128)}, f32[2048,1]{1,0:T(8,128)}, bf16[2048,512]{1,0:T(8,128)(2,1)}, bf16[512,2048]{1,0:T(8,128)(2,1)}, bf16[2048,512]{1,0:T(8...) custom-call(bf16[3264,512]{1,0:T(8,128)(2,1)} %all-gather.2.cloned.1.call-done.embedded_, ...), custom_call_target="tpu_custom_call" | custom-call | flops 10066329600 | bytes 20971520 | tf_op jit(solution)/shard_map/enter/pallas_call | solution.py:398
  76.6 104.1 %attend.1 = (bf16[512,2048]{1,0:T(8,128)(2,1)}, f32[512,2048]{1,0:T(8,128)}, f32[4,8,2048]{2,1,0:T(8,128)}, bf16[16,2048,2048]{2,1,0:T(8,128)(2,1)}) custom-call(bf16[2048,512]{1,0:T(8,128)(2,1)} %get-tuple-element.43.key_ref, bf16[512,2048]{1,0:T(8,128)(2,1)} %get-tuple-element.44.query_ref, bf16[512,2048]{1,0:T(8,128)(2,1)} %get-tuple-element.45.value_ref), custom_call_target="tpu_custom_call" | custom-call | flops 34359738368 | bytes 134217728 | tf_op jit(solution)/shard_map/attend/pallas_call | solution.py:502
  180.7 1.3 copy-done.2
  182.1 46.1 %middle.1 = (bf16[2048,512]{1,0:T(8,128)(2,1)}, f32[2048,512]{1,0:T(8,128)}, bf16[512,2048]{1,0:T(8,128)(2,1)}, bf16[4608,512]{1,0:T(8,128)(2,1)}, f32[8,512]{1,0:T(8,128)}) custom-call(f32[2048,512]{1,0:T(8,128)} %get-tuple-element.51.stream_ref, bf16[512,2048]{1,0:T(8,128)(2,1)} %get-tuple-element.52.mixed_ref, bf16[2048,512]{1,0:T(8,128)(2,1)} %bitcast.23, ...), custom_call_target="tpu_custom_call" | custom-call | flops 28991029248 | bytes 16777216 | tf_op jit(solution)/shard_map/middle/pallas_call | solution.py:633
  228.1 145.7 %attend_back.1 = (bf16[512,2048]{1,0:T(8,128)(2,1)}, bf16[2048,512]{1,0:T(8,128)(2,1)}, bf16[2048,512]{1,0:T(8,128)(2,1)}, bf16[4608,512]{1,0:T(8,128)(2,1)}, bf16[8,256,512]{2,1,0:T(8,128)(2,1)}) custom-call(bf16[16,2048,2048]{2,1,0:T(8,128)(2,1)} %get-tuple-element.46.raised_ref, f32[4,8,2048]{2,1,0:T(8,128)} %get-tuple-element.47.total_ref, ...), custom_call_target="tpu_custom_call" | custom-call | flops 68719476736 | bytes 134217728 | tf_op jit(solution)/shard_map/attend_back/pallas_call | solution.py:835
  373.9 24.1 %leave.1 = (bf16[3264,512]{1,0:T(8,128)(2,1)}, bf16[1536,512]{1,0:T(8,128)(2,1)}, f32[8,512]{1,0:T(8,128)}) custom-call(bf16[512,2048]{1,0:T(8,128)(2,1)} %get-tuple-element.57.grad_query_ref, bf16[2048,512]{1,0:T(8,128)(2,1)} %get-tuple-element.58.grad_key_ref, bf16[2048,512]{1,0:T(8,128)(2,1)} %get-tuple-element.59.grad_value_ref, ...), custom_call_target="tpu_custom_call" | custom-call | flops 13287555072 | bytes 20971520 | tf_op jit(solution)/shard_map/leave/pallas_call | solution.py:943
  398.3 1.1 copy-done.4
  399.4 2.1 convert_dynamic-update-slice_fusion
  401.5 42.0 %reduce-scatter.2.cloned.1.call-done = bf16[408,512]{1,0:T(8,128)(2,1)} async-done(((bf16[3264,512]{1,0:T(8,128)(2,1)}), bf16[408,512]{1,0:T(8,128)(2,1)}) %reduce-scatter.2.cloned.1.call-update) | async-done | bytes 417808 | tf_op jit(solution)/shard_map/reduce_scatter | solution.py:1112
  443.5 2.9 bitcast_dynamic-update-slice_fusion
  447.6 1.1 convert_reduce_fusion
  448.7 1.3 dynamic-update-slice.4
  450.0 3.0 fusion.10
  453.0 2.6 maximum_convert_fusion
  455.5 4.4 slice_convert_fusion
  459.9 1.4 convolution_convert_fusion
  461.3 133.8 %all-reduce.2.cloned.1.call-done = f32[2321,512]{1,0:T(8,128)} async-done(((f32[2321,512]{1,0:T(8,128)}), f32[2321,512]{1,0:T(8,128)}) %all-reduce.2.cloned.1.call-update) | async-done | bytes 4753424 | tf_op jit(solution)/shard_map/psum | solution.py:1126
  595.1 0.7 slice_bitcast_fusion
  596.4 2.2 fusion.9
  598.6 1.9 pad_maximum_fusion.1
  600.4 2.8 slice.40
  603.3 1.6 fusion.8
  604.9 1.3 copy.50
  (64 shorter events, 8.1 us)
Async XLA Ops:
  7.2 1.2 copy-start
  7.2 50.6 %all-gather.2.cloned.1.call-start = ((), (), s32[]{:S(2)}) async-start(), calls=%async_computation.2 | async-start | bytes 3760128 | tf_op jit(solution)/shard_map/all_gather | solution.py:1043
  8.3 7.8 %copy-start.20 = (s32[8]{0:T(128)S(1)}, s32[8]{0:T(128)}, u32[]{:S(2)}) copy-start(s32[8]{0:T(128)} %param.24) | copy-start | bytes 100
  8.3 8.0 %copy-start.8 = (s32[3264]{0:T(1024)S(1)}, s32[3264]{0:T(1024)}, u32[]{:S(2)}) copy-start(s32[3264]{0:T(1024)} %param.23) | copy-start | bytes 39172
  8.3 8.0 %copy-start.9 = (s32[3264]{0:T(1024)S(1)}, s32[3264]{0:T(1024)}, u32[]{:S(2)}) copy-start(s32[3264]{0:T(1024)} %param.22) | copy-start | bytes 39172
  10.7 8.7 %copy-start.11 = (bf16[512]{0:T(512)(128)(2,1)S(1)}, bf16[512]{0:T(512)(128)(2,1)}, u32[]{:S(2)}) copy-start(bf16[512]{0:T(512)(128)(2,1)} %param.28) | copy-start | bytes 3076
  10.7 9.2 %copy-start.12 = (bf16[512]{0:T(512)(128)(2,1)S(1)}, bf16[512]{0:T(512)(128)(2,1)}, u32[]{:S(2)}) copy-start(bf16[512]{0:T(512)(128)(2,1)} %param.27) | copy-start | bytes 3076
  10.7 9.8 %copy-start.13 = (bf16[512]{0:T(512)(128)(2,1)S(1)}, bf16[512]{0:T(512)(128)(2,1)}, u32[]{:S(2)}) copy-start(bf16[512]{0:T(512)(128)(2,1)} %param.29) | copy-start | bytes 3076
  10.7 10.4 %copy-start.14 = (bf16[512]{0:T(512)(128)(2,1)S(1)}, bf16[512]{0:T(512)(128)(2,1)}, u32[]{:S(2)}) copy-start(bf16[512]{0:T(512)(128)(2,1)} %param.31) | copy-start | bytes 3076
  10.7 11.0 %copy-start.15 = (bf16[512]{0:T(512)(128)(2,1)S(1)}, bf16[512]{0:T(512)(128)(2,1)}, u32[]{:S(2)}) copy-start(bf16[512]{0:T(512)(128)(2,1)} %param.32) | copy-start | bytes 3076
  10.7 11.5 %copy-start.10 = (bf16[2048]{0:T(1024)(128)(2,1)S(1)}, bf16[2048]{0:T(1024)(128)(2,1)}, u32[]{:S(2)}) copy-start(bf16[2048]{0:T(1024)(128)(2,1)} %param.38) | copy-start | bytes 12292
  10.8 12.1 %copy-start.16 = (bf16[512]{0:T(512)(128)(2,1)S(1)}, bf16[512]{0:T(512)(128)(2,1)}, u32[]{:S(2)}) copy-start(bf16[512]{0:T(512)(128)(2,1)} %param.34) | copy-start | bytes 3076
  10.8 12.7 %copy-start.17 = (bf16[512]{0:T(512)(128)(2,1)S(1)}, bf16[512]{0:T(512)(128)(2,1)}, u32[]{:S(2)}) copy-start(bf16[512]{0:T(512)(128)(2,1)} %param.35) | copy-start | bytes 3076
  10.8 13.3 %copy-start.18 = (bf16[512]{0:T(512)(128)(2,1)S(1)}, bf16[512]{0:T(512)(128)(2,1)}, u32[]{:S(2)}) copy-start(bf16[512]{0:T(512)(128)(2,1)} %param.36) | copy-start | bytes 3076
  10.8 13.8 %copy-start.19 = (bf16[512]{0:T(512)(128)(2,1)S(1)}, bf16[512]{0:T(512)(128)(2,1)}, u32[]{:S(2)}) copy-start(bf16[512]{0:T(512)(128)(2,1)} %param.40) | copy-start | bytes 3076
  10.8 169.9 %all-to-all-start = ((bf16[8,256,512]{2,1,0:T(8,128)(2,1)}), bf16[8,256,512]{2,1,0:T(8,128)(2,1)S(1)}, u32[]{:S(2)}, u32[]{:S(2)}) async-start(bf16[8,256,512]{2,1,0:T(8,128)(2,1)} %param.41), calls=%async_computation | async-start | bytes 4194304 | tf_op jit(solution)/shard_map/all_to_all | solution.py:1025
  16.1 427.4 %reduce-scatter.2.cloned.1.call-start = ((), (), s32[]{:S(2)}) async-start(), calls=%async_computation.3 | async-start | bytes 3760128 | tf_op jit(solution)/shard_map/reduce_scatter | solution.py:1112
  180.7 1.3 copy-start.2
  398.0 1.4 copy-start.4
  398.0 45.5 %copy-start.5 = (bf16[408,768]{1,0:T(8,128)(2,1)S(1)}, bf16[408,768]{1,0:T(8,128)(2,1)}, u32[]{:S(2)}) copy-start(bf16[408,768]{1,0:T(8,128)(2,1)} %param.21) | copy-start | bytes 1880068
  398.0 197.1 %all-reduce.2.cloned.1.call-start = ((), (), s32[]{:S(2)}) async-start(), calls=%async_computation.4 | async-start | bytes 9535488 | tf_op jit(solution)/shard_map/psum | solution.py:1126
  399.4 47.0 %copy-start.6 = (f32[8,512]{1,0:T(8,128)S(1)}, f32[8,512]{1,0:T(8,128)}, u32[]{:S(2)}) copy-start(f32[8,512]{1,0:T(8,128)} %get-tuple-element.65) | copy-start | bytes 49156
  399.4 47.6 %copy-start.7 = (f32[8,512]{1,0:T(8,128)S(1)}, f32[8,512]{1,0:T(8,128)}, u32[]{:S(2)}) copy-start(f32[8,512]{1,0:T(8,128)} %get-tuple-element.66) | copy-start | bytes 49156
  455.5 4.4 copy-start.1
  600.4 4.4 copy-start.3
Sparse Core Ops, SparseCore 0:
  10.9 46.9 all-gather.1
  398.1 45.3 reduce-scatter.1
  450.2 144.8 all-reduce.1

commit v3 on v2

--- a/solution.py
+++ b/solution.py
@@ -345,9 +345,12 @@
 
 
 def enter_kernel(
-    embedded_ref,
+    latents_ref,
+    embed_ref,
+    embed_bias_ref,
     slot_ref,
-    table_ref,
+    coarse_ref,
+    fine_ref,
     mask_ref,
     gain_ref,
     shift_ref,
@@ -362,13 +365,65 @@
     key_t_ref,
     value_ref,
     value_t_ref,
+    embedded_ref,
+    sems,
 ):
     block, width = stream_ref.shape
+    spot = Spot()
+    capacity = embedded_ref.shape[0] // spot.splits
+
+    @pl.when(pl.program_id(0) == 0)
+    def _():
+        count = spot.meet(spot.tree(False))
+        embedded = plain_dot(latents_ref[...], embed_ref[...]) + embed_bias_ref[...].astype(
+            jnp.float32
+        )
+        if capacity > latents_ref.shape[0]:
+            rest = jnp.zeros((capacity - latents_ref.shape[0], width), jnp.float32)
+            embedded = jnp.concatenate([embedded, rest], axis=0)
+
+        def held(core, chip):
+            return embedded_ref.at[span_of((chip * 2 + core) * capacity, capacity)]
+
+        def share(at, core, chip, device):
+            return send(held(core, chip), held(core, chip), sems, at, device)
+
+        embedded_ref[span_of(spot.index * capacity, capacity), :] = embedded.astype(jnp.bfloat16)
+        pl.semaphore_wait(pltpu.get_barrier_semaphore(), count)
+        for step in range(1, spot.half):
+            share(step, spot.core, spot.chip, spot.peer(step)).start()
+        share(0, spot.core, spot.chip, spot.sibling()).start()
+        for step in range(1, spot.half):
+            share(step, spot.core, spot.chip_at(-step), spot.peer(step)).wait_recv()
+            share(
+                spot.half + step, spot.core, spot.chip_at(-step), spot.sibling()
+            ).start()
+        for step in range(1, spot.half):
+            share(step, spot.core, spot.chip, spot.peer(step)).wait_send()
+        share(0, spot.core, spot.chip, spot.sibling()).wait_send()
+        share(0, 1 - spot.core, spot.chip, spot.sibling()).wait_recv()
+        for step in range(1, spot.half):
+            at = spot.half + step
+            share(at, spot.core, spot.chip_at(-step), spot.sibling()).wait_send()
+            share(at, 1 - spot.core, spot.chip_at(-step), spot.sibling()).wait_recv()
+
     place = lax.broadcasted_iota(jnp.int32, (block, 1), 0) + pl.program_id(0) * block
     fills = (place == slot_ref[...]).astype(jnp.float32)
     empty = 1.0 - jnp.sum(fills, axis=1, keepdims=True)
     placed = plain_dot(fills.astype(jnp.bfloat16), embedded_ref[...])
-    stream = placed + empty * mask_ref[...].astype(jnp.float32) + table_ref[...]
+    fine_rows = fine_ref.shape[0]
+    half = width // 2
+    fine_sin, fine_cos = fine_ref[:, :half], fine_ref[:, half:]
+    tables = []
+    for at in range(block // fine_rows):
+        row = coarse_ref[0, at : at + 1, :]
+        sin, cos = row[:, :half], row[:, half:]
+        tables.append(
+            jnp.concatenate(
+                [sin * fine_cos + cos * fine_sin, cos * fine_cos - sin * fine_sin], axis=1
+            )
+        )
+    stream = placed + empty * mask_ref[...].astype(jnp.float32) + jnp.concatenate(tables, axis=0)
     stream_ref[...] = stream
     empty_ref[...] = empty
     normed, _ = normalize(stream)
@@ -386,10 +441,27 @@
     value_t_ref[...] = values.T.astype(jnp.bfloat16)
 
 
-def enter(embedded_all, slot_place, table, mask_token, gain, shift, joint_weight, query_bias, value_bias):
-    rows, width = table.shape
-    slots = embedded_all.shape[0]
+def enter(
+    latents,
+    embed_weight,
+    embed_bias,
+    slot_place,
+    first_place,
+    rows,
+    mask_token,
+    gain,
+    shift,
+    joint_weight,
+    query_bias,
+    value_bias,
+):
+    splits = lax.axis_size("seq")
+    width = embed_weight.shape[1]
+    slots = slot_place.shape[0]
     block = min(256, rows)
+    fine_rows = min(32, block)
+    fine = sinusoid(jnp.arange(fine_rows, dtype=jnp.int32), width)
+    coarse = sinusoid(first_place + fine_rows * jnp.arange(rows // fine_rows, dtype=jnp.int32), width)
     row_block = pl.BlockSpec((block, width), lambda i: (i, 0))
     lane_block = pl.BlockSpec((width, block), lambda i: (0, i))
     vector = whole((1, width))
@@ -399,9 +471,12 @@
         enter_kernel,
         grid=(rows // block,),
         in_specs=[
-            whole((slots, width)),
+            whole(latents.shape),
+            whole(embed_weight.shape),
+            vector,
             whole((1, slots)),
-            row_block,
+            pl.BlockSpec((1, block // fine_rows, width), lambda i: (i, 0, 0)),
+            whole(fine.shape),
             vector,
             vector,
             vector,
@@ -429,7 +504,13 @@
             low,
             low_t,
         ],
-        compiler_params=pltpu.CompilerParams(vmem_limit_bytes=VMEM_LIMIT),
+        scratch_shapes=[
+            pltpu.VMEM((slots, width), jnp.bfloat16),
+            pltpu.SemaphoreType.DMA((2, splits)),
+        ],
+        compiler_params=pltpu.CompilerParams(
+            vmem_limit_bytes=VMEM_LIMIT, collective_id=0, has_side_effects=True
+        ),
         cost_estimate=pl.CostEstimate(
             flops=2 * rows * width * (slots + 3 * width),
             bytes_accessed=20 * rows * width,
@@ -437,9 +518,12 @@
         ),
         name="enter",
     )(
-        embedded_all,
+        latents,
+        embed_weight,
+        embed_bias[None, :],
         slot_place[None, :],
-        table,
+        coarse.reshape(rows // block, block // fine_rows, width),
+        fine,
         mask_token[None, :],
         gain[None, :],
         shift[None, :],
@@ -890,18 +974,33 @@
     gain_ref,
     joint_ref,
     slot_ref,
-    back_ref,
-    grad_joint_ref,
-    small_ref,
+    latents_ref,
+    embed_ref,
+    early_ref,
+    latent_grad_ref,
+    joint_total_ref,
+    embed_total_ref,
     joint_sum,
     small_sum,
     grad_all,
+    joint_flat,
+    embed_flat,
+    near_out,
+    near_in,
+    far_out,
+    far_in,
+    sems,
+    *sum_refs,
 ):
     block, width = stream_ref.shape
-    step = pl.program_id(0)
-
-    @pl.when(step == 0)
+    step_now = pl.program_id(0)
+    spot = Spot()
+    capacity = near_out.shape[0] // spot.half
+    others = spot.tree()
+
+    @pl.when(step_now == 0)
     def _():
+        spot.meet(others)
         joint_sum[...] = jnp.zeros_like(joint_sum)
         small_sum[...] = jnp.zeros_like(small_sum)
 
@@ -915,31 +1014,111 @@
     grad_stream = grad_middle_ref[...] + normalize_back(
         grad_normed * gain_ref[...].astype(jnp.float32), normed, scale
     )
-    grad_all[pl.ds(pl.multiple_of(step * block, block), block), :] = grad_stream.astype(jnp.bfloat16)
+    grad_all[pl.ds(pl.multiple_of(step_now * block, block), block), :] = grad_stream.astype(
+        jnp.bfloat16
+    )
     small_sum[0:1, :] += column_sum(empty_ref[...] * grad_stream)
     small_sum[1:2, :] += column_sum(grad_normed * normed)
     small_sum[2:3, :] += column_sum(grad_normed)
     small_sum[3:4, :] += column_sum(sides[0])
     small_sum[4:5, :] += column_sum(sides[2])
 
-    @pl.when(step == pl.num_programs(0) - 1)
+    @pl.when(step_now == pl.num_programs(0) - 1)
     def _():
-        grad_joint_ref[...] = joint_sum[...].astype(grad_joint_ref.dtype)
-        small_ref[...] = small_sum[...]
-        slots = back_ref.shape[0]
+        count = len(sum_refs) // 2
+        joint_tree = TreeSum(spot, joint_flat, joint_total_ref, sum_refs[:count], False)
+        embed_tree = TreeSum(spot, embed_flat, embed_total_ref, sum_refs[count:], False)
+        joint_flat[...] = joint_sum[...].astype(jnp.bfloat16)
+        pl.semaphore_wait(pltpu.get_barrier_semaphore(), len(others))
+        joint_tree.start()
         place = lax.broadcasted_iota(jnp.int32, (1, grad_all.shape[0]), 1)
-        part = slots // 8
-        for at in range(0, slots, part):
-            takes = (slot_ref[at : at + part, :] == place).astype(jnp.float32).astype(jnp.bfloat16)
-            back_ref[at : at + part, :] = plain_dot(takes, grad_all[...]).astype(jnp.bfloat16)
-
-
-def leave(grad_query_t, grad_key, grad_value, stream, empty, low, grad_middle, gain, joint_weight, slot_place):
+
+        def gathered(owner):
+            slots = slot_ref[pl.ds(pl.multiple_of(owner * capacity, 8), capacity), :]
+            takes = (slots == place).astype(jnp.float32).astype(jnp.bfloat16)
+            return plain_dot(takes, grad_all[...])
+
+        def part(at):
+            return pl.ds(at * capacity, capacity)
+
+        def near_copy(step):
+            return send(
+                near_out.at[part(step)], near_in.at[part(step)], sems, step, spot.sibling()
+            )
+
+        def far_copy(step):
+            return send(
+                far_out.at[part(step - 1)],
+                far_in.at[part(step - 1)],
+                sems,
+                spot.half + step,
+                spot.peer(step),
+            )
+
+        order = list(range(1, spot.half)) + [0]
+        for step in order:
+            near_out[part(step), :] = gathered(spot.chip_at(step) * 2 + 1 - spot.core).astype(
+                jnp.bfloat16
+            )
+            near_copy(step).start()
+        joint_tree.near_to_far()
+        for step in order:
+            near_copy(step).wait()
+            own = gathered(spot.chip_at(step) * 2 + spot.core)
+            own = own + near_in[part(step), :].astype(jnp.float32)
+            if step > 0:
+                far_out[part(step - 1), :] = own.astype(jnp.bfloat16)
+                far_copy(step).start()
+        for step in range(1, spot.half):
+            far_copy(step).wait()
+            own = own + far_in[part(step - 1), :].astype(jnp.float32)
+        grad_embedded = own[: latents_ref.shape[0]].astype(jnp.bfloat16)
+        small_sum[5:6, :] = column_sum(grad_embedded)
+        embed_rows = embed_ref.shape[0]
+        embed_flat[:embed_rows, :] = lead_dot(latents_ref[...], grad_embedded).astype(jnp.bfloat16)
+        small = jnp.concatenate([early_ref[...], small_sum[...]], axis=0)
+        rest = embed_flat.shape[0] - embed_rows - small.shape[0]
+        if rest:
+            small = jnp.concatenate([small, jnp.zeros((rest, width), jnp.float32)], axis=0)
+        embed_flat[embed_rows:, :] = small.astype(jnp.bfloat16)
+        embed_tree.start()
+        latent_grad_ref[...] = trail_dot(grad_embedded, embed_ref[...]).astype(jnp.bfloat16)
+        joint_tree.far_to_deep()
+        embed_tree.near_to_far()
+        joint_tree.deep_to_layer()
+        embed_tree.far_to_deep()
+        joint_tree.part_to_half()
+        embed_tree.deep_to_layer()
+        joint_tree.finish()
+        embed_tree.part_to_half()
+        embed_tree.finish()
+
+
+def leave(
+    grad_query_t,
+    grad_key,
+    grad_value,
+    stream,
+    empty,
+    low,
+    grad_middle,
+    gain,
+    joint_weight,
+    slot_place,
+    latents,
+    embed_weight,
+    early_small,
+):
+    splits, layers = lax.axis_size("seq"), lax.axis_size("dp")
     rows, width = stream.shape
     slots = slot_place.shape[0]
+    capacity = slots // splits
+    half = splits // 2
     block = min(256, rows)
     row_block = pl.BlockSpec((block, width), lambda i: (i, 0))
     lane_block = pl.BlockSpec((width, block), lambda i: (0, i))
+    joint_rows = padded(3 * width, splits * 16)
+    embed_rows = padded(embed_weight.shape[0] + early_small.shape[0] + 8, splits * 16)
     return pl.pallas_call(
         leave_kernel,
         grid=(rows // block,),
@@ -954,19 +1133,37 @@
             whole((1, width)),
             whole((width, 3 * width)),
             whole((slots, 1)),
-        ],
-        out_specs=[whole((slots, width)), whole((3 * width, width)), whole((8, width))],
+            whole(latents.shape),
+            whole(embed_weight.shape),
+            whole(early_small.shape),
+        ],
+        out_specs=[
+            whole(latents.shape),
+            pl.BlockSpec(memory_space=pl.ANY),
+            pl.BlockSpec(memory_space=pl.ANY),
+        ],
         out_shape=[
-            jax.ShapeDtypeStruct((slots, width), jnp.bfloat16),
-            jax.ShapeDtypeStruct((3 * width, width), jnp.bfloat16),
-            jax.ShapeDtypeStruct((8, width), jnp.float32),
+            jax.ShapeDtypeStruct(latents.shape, jnp.bfloat16),
+            jax.ShapeDtypeStruct((joint_rows, width), jnp.bfloat16),
+            jax.ShapeDtypeStruct((embed_rows, width), jnp.bfloat16),
         ],
         scratch_shapes=[
             pltpu.VMEM((3 * width, width), jnp.float32),
             pltpu.VMEM((8, width), jnp.float32),
             pltpu.VMEM((rows, width), jnp.bfloat16),
-        ],
-        compiler_params=pltpu.CompilerParams(vmem_limit_bytes=VMEM_LIMIT),
+            pltpu.VMEM((joint_rows, width), jnp.bfloat16),
+            pltpu.VMEM((embed_rows, width), jnp.bfloat16),
+            pltpu.VMEM((half * capacity, width), jnp.bfloat16),
+            pltpu.VMEM((half * capacity, width), jnp.bfloat16),
+            pltpu.VMEM((max(half - 1, 1) * capacity, width), jnp.bfloat16),
+            pltpu.VMEM((max(half - 1, 1) * capacity, width), jnp.bfloat16),
+            pltpu.SemaphoreType.DMA((2, splits)),
+        ]
+        + TreeSum.scratch(joint_rows, width, False, splits, layers)
+        + TreeSum.scratch(embed_rows, width, False, splits, layers),
+        compiler_params=pltpu.CompilerParams(
+            vmem_limit_bytes=VMEM_LIMIT, collective_id=2, has_side_effects=True
+        ),
         cost_estimate=pl.CostEstimate(
             flops=2 * rows * width * (slots + 6 * width),
             bytes_accessed=20 * rows * width,
@@ -984,6 +1181,9 @@
         gain[None, :],
         joint_weight,
         slot_place[:, None],
+        latents,
+        embed_weight,
+        early_small,
     )
 
 
@@ -1031,22 +1231,20 @@
             axis_index_groups=exchange_groups if sharers > 1 else None,
         )
 
-    slot = jnp.arange(splits * capacity, dtype=jnp.int32)
-    live = (slot % capacity) < jnp.repeat(counts, capacity)
-    mine = live & (clip_ids % clip_count == own_clip)
-    slot_place = jnp.where(mine, restore - first_place, -1)
-    table = sinusoid(first_place + jnp.arange(rows, dtype=jnp.int32), model_width)
-
-    embedded = (plain_dot(latents, embed_weight) + embed_bias.astype(jnp.float32)).astype(
-        jnp.bfloat16
-    )
-    embedded_all = lax.all_gather(embedded, "seq", axis=0, tiled=True)
-    grad_output = to_clips(cotangent).reshape(rows, model_width)
+    live = jnp.arange(capacity, dtype=jnp.int32)[None, :] < counts[:, None]
+    mine = live & ((clip_ids % clip_count).reshape(splits, capacity) == own_clip)
+    slot_place = jnp.where(mine, restore.reshape(splits, capacity) - first_place, -1)
+    slot_place = jnp.pad(
+        slot_place, ((0, 0), (0, padded(capacity, 16) - capacity)), constant_values=-1
+    ).reshape(-1)
 
     stream, empty, first_low, query_t, keys, key_t, values, value_t = enter(
-        embedded_all,
+        latents,
+        embed_weight,
+        embed_bias,
         slot_place,
-        table,
+        first_place,
+        rows,
         mask_token,
         first_gain,
         first_shift,
@@ -1054,6 +1252,8 @@
         query_bias,
         value_bias,
     )
+    cotangent, keys = lax.optimization_barrier((cotangent, keys))
+    grad_output = to_clips(cotangent).reshape(rows, model_width)
     if sharers > 1:
         keys = lax.all_gather(keys, "seq", axis=0, tiled=True, axis_index_groups=clip_groups)
         values = lax.all_gather(values, "seq", axis=0, tiled=True, axis_index_groups=clip_groups)
@@ -1097,7 +1297,7 @@
             )
             for side in (grad_key, grad_value)
         )
-    back_rows, grad_joint, late_small = leave(
+    latent_grad, joint_sum, embed_sum = leave(
         grad_query_t,
         grad_key,
         grad_value,
@@ -1108,22 +1308,10 @@
         first_gain,
         joint_weight,
         slot_place,
-    )
-    grad_embedded = lax.psum_scatter(back_rows, "seq", scatter_dimension=0, tiled=True)
-    latent_grad = trail_dot(grad_embedded, embed_weight).astype(jnp.bfloat16)
-    grad_embed_weight = lead_dot(latents, grad_embedded)
-    grad_embed_bias = column_sum(grad_embedded)
-    late_flat = jnp.concatenate(
-        [
-            grad_joint.astype(jnp.float32),
-            grad_embed_weight,
-            early_small,
-            late_small,
-            grad_embed_bias,
-        ],
-        axis=0,
-    )
-    late_sum = lax.psum(late_flat, ("dp", "seq"))
+        latents,
+        embed_weight,
+        early_small,
+    )
 
     def columns(stack):
         return jnp.concatenate(jnp.split(stack, stack.shape[0] // model_width, axis=0), axis=1)
@@ -1136,21 +1324,22 @@
     grad_expand, grad_contract, grad_output_weight = (
         summed.astype(jnp.float32) for summed in (grad_expand, grad_contract, grad_output_weight)
     )
-    grad_joint_weight = columns(late_sum[: 3 * model_width])
-    at = 3 * model_width + embed_weight.shape[0]
-    grad_embed_weight = late_sum[3 * model_width : at]
-    grad_expand_bias = late_sum[at : at + chunks].reshape(-1)
-    at += chunks
-    grad_contract_bias, grad_output_bias, grad_second_gain, grad_second_shift = late_sum[at : at + 4]
-    at += 4
+    grad_joint_weight = columns(joint_sum.astype(jnp.float32))
+    at = embed_weight.shape[0]
+    grad_embed_weight = embed_sum[:at].astype(jnp.float32)
+    small = embed_sum[at:].astype(jnp.float32)
+    grad_expand_bias = small[:chunks].reshape(-1)
+    grad_contract_bias, grad_output_bias, grad_second_gain, grad_second_shift = small[
+        chunks : chunks + 4
+    ]
     (
         grad_mask,
         grad_first_gain,
         grad_first_shift,
         grad_query_bias,
         grad_value_bias,
-    ) = late_sum[at : at + 5]
-    grad_embed_bias = late_sum[at + 8]
+        grad_embed_bias,
+    ) = small[chunks + 4 : chunks + 10]
     return (
         decoded,
         latent_grad,

time: 622 us -> 469 us (0.75); the launches traced: 613 us -> 468 us
  waiting for transfers between devices: 199 us -> 0.01 us
  Pallas kernels: 339 us -> 428 us
  between operations: 14.4 us -> 0.89 us
  other arithmetic: 25.6 us -> 15.7 us
  matrix products: 6.56 us -> 0 us
    psum x1 -> x0, waiting for transfers between devices: 134 us -> none  [body(): late_sum = lax.psum(late_flat, ('dp', 'seq'))]
    pallas_call x1, Pallas kernels: 24.1 us -> 88.5 us  [leave(): pl.pallas_call(leave_kernel, grid=(rows // block,), in_specs=[lane_block,...]
    reduce_scatter x1 -> x0, waiting for transfers between devices: 42 us -> none  [body(): lax.psum_scatter(back_rows, 'seq', scatter_dimension=0, tiled=True)]
    pallas_call x1, Pallas kernels: 18.8 us -> 43.7 us  [enter(): pl.pallas_call(enter_kernel, grid=(rows // block,), in_specs=[whole(laten...]
    all_gather x1 -> x0, waiting for transfers between devices: 22.7 us -> none  [body(): embedded_all = lax.all_gather(embedded, 'seq', axis=0, tiled=True)]
    sin x1 -> x2, other arithmetic: 7.33 us -> 0.5 us  [sinusoid(): return jnp.concatenate([jnp.sin(angles), jnp.cos(angles)], axis=1)]
    dot_general x3 -> x0, matrix products: 6.56 us -> none  [the longest x1 2.86 us: lead_dot(): lax.dot_general(left, right, (((0,), (0,)), ((), ())), preferred_element_...]
  transfers between devices with their start and end apart: 4 -> 1, of which waited for: 3 -> 0; matrix products, arithmetic and copies ran while one was open for 5% -> 1% of each run, Pallas kernels for 20% -> 22%
where the time goes in v3:
time: 469 us; the launch traced here: 468 us
  Pallas kernels  428 us (91%)
  local copies, waits for them, and re-layouts  19.3 us (4%)
  other arithmetic  15.7 us (3%)
    pallas_call x1, Pallas kernels, attend_back(): pl.pallas_call(partial(attend_back_kernel, groups * (rows // block)), gri...  145 us
    pallas_call x1, Pallas kernels, attend(): pl.pallas_call(attend_kernel, grid=(groups, rows // block), in_specs=[pl....  104 us
    pallas_call x1, Pallas kernels, leave(): pl.pallas_call(leave_kernel, grid=(rows // block,), in_specs=[lane_block,...  88.5 us
    pallas_call x1, Pallas kernels, middle_block(): pl.pallas_call(middle_kernel, grid=(rows // block,), in_specs=[row_block,...  46.3 us
    pallas_call x1, Pallas kernels, enter(): pl.pallas_call(enter_kernel, grid=(rows // block,), in_specs=[whole(laten...  43.7 us
  transfers between devices with their start and end apart: 1, of which 0 were waited for; matrix products, arithmetic and copies ran while one was open for 1% of the time, Pallas kernels for 22%

profile of v3, /device:TPU:0, one launch (start us, length us, event | category | flops | bytes accessed | tf_op | source)
XLA Modules:
  0.0 467.6 jit_solution(3264796185988360517)
XLA Ops:
  0.7 0.7 fusion.1
  1.6 0.7 broadcast_subtract_fusion
  2.4 0.7 fusion.3
  3.1 0.7 broadcast_in_dim_reshape.6.slot_ref
  4.3 1.3 broadcast_in_dim.47.gain_ref
  5.6 1.3 broadcast_in_dim.44.embed_bias_ref
  6.8 1.3 broadcast_in_dim.46.mask_ref
  8.1 1.3 broadcast_in_dim.48.shift_ref
  9.4 1.3 broadcast_in_dim.49.query_bias_ref
  10.6 1.3 broadcast_in_dim.50.value_bias_ref
  11.9 0.7 pad_maximum_fusion.1.coarse_ref
  12.5 0.6 pad_maximum_fusion.2.fine_ref
  13.2 43.7 %enter.1 = (f32[2048,512]{1,0:T(8,128)}, f32[2048,1]{1,0:T(8,128)}, bf16[2048,512]{1,0:T(8,128)(2,1)}, bf16[512,2048]{1,0:T(8,128)(2,1)}, bf16[2048,512]{1,0:T(8...) custom-call(bf16[408,768]{1,0:T(8,128)(2,1)} %latents_ref.3, ...), custom_call_target="tpu_custom_call" | custom-call | flops 10200547328 | bytes 20971520 | tf_op jit(solution)/shard_map/enter/pallas_call | solution.py:470
  57.0 3.7 all-to-all-start
  60.7 2.6 broadcast_in_dim_reshape.8.slot_ref
  63.3 0.6 broadcast_in_dim.54.expand_bias_ref
  64.5 0.6 broadcast_in_dim.52.gain_ref
  66.3 103.9 %attend.1 = (bf16[512,2048]{1,0:T(8,128)(2,1)}, f32[512,2048]{1,0:T(8,128)}, f32[4,8,2048]{2,1,0:T(8,128)}, bf16[16,2048,2048]{2,1,0:T(8,128)(2,1)}) custom-call(bf16[2048,512]{1,0:T(8,128)(2,1)} %get-tuple-element.46.key_ref, bf16[512,2048]{1,0:T(8,128)(2,1)} %get-tuple-element.47.query_ref, bf16[512,2048]{1,0:T(8,128)(2,1)} %get-tuple-element.48.value_ref), custom_call_target="tpu_custom_call" | custom-call | flops 34359738368 | bytes 134217728 | tf_op jit(solution)/shard_map/attend/pallas_call | solution.py:586
  170.2 1.3 copy-done.2
  171.5 46.3 %middle.1 = (bf16[2048,512]{1,0:T(8,128)(2,1)}, f32[2048,512]{1,0:T(8,128)}, bf16[512,2048]{1,0:T(8,128)(2,1)}, bf16[4608,512]{1,0:T(8,128)(2,1)}, f32[8,512]{1,0:T(8,128)}) custom-call(f32[2048,512]{1,0:T(8,128)} %get-tuple-element.54.stream_ref, bf16[512,2048]{1,0:T(8,128)(2,1)} %get-tuple-element.55.mixed_ref, bf16[2048,512]{1,0:T(8,128)(2,1)} %bitcast.16, ...), custom_call_target="tpu_custom_call" | custom-call | flops 28991029248 | bytes 16777216 | tf_op jit(solution)/shard_map/middle/pallas_call | solution.py:717
  217.8 145.5 %attend_back.1 = (bf16[512,2048]{1,0:T(8,128)(2,1)}, bf16[2048,512]{1,0:T(8,128)(2,1)}, bf16[2048,512]{1,0:T(8,128)(2,1)}, bf16[4608,512]{1,0:T(8,128)(2,1)}, bf16[8,256,512]{2,1,0:T(8,128)(2,1)}) custom-call(bf16[16,2048,2048]{2,1,0:T(8,128)(2,1)} %get-tuple-element.49.raised_ref, f32[4,8,2048]{2,1,0:T(8,128)} %get-tuple-element.50.total_ref, ...), custom_call_target="tpu_custom_call" | custom-call | flops 68719476736 | bytes 134217728 | tf_op jit(solution)/shard_map/attend_back/pallas_call | solution.py:919
  363.3 88.5 %leave.1 = (bf16[408,768]{1,0:T(8,128)(2,1)}, bf16[1536,512]{1,0:T(8,128)(2,1)}, bf16[896,512]{1,0:T(8,128)(2,1)}) custom-call(bf16[512,2048]{1,0:T(8,128)(2,1)} %get-tuple-element.61.grad_query_ref, bf16[2048,512]{1,0:T(8,128)(2,1)} %get-tuple-element.62.grad_key_ref, bf16[2048,512]{1,0:T(8,128)(2,1)} %get-tuple-element.63.grad_value_ref, ...), custom_call_target="tpu_custom_call" | custom-call | flops 13421772800 | bytes 20971520 | tf_op jit(solution)/shard_map/leave/pallas_call | solution.py:1122
  451.8 2.5 slice_convert_fusion.1
  454.3 0.9 slice_convert_fusion.3
  455.2 0.6 fusion.6
  455.9 1.3 fusion.4
  457.2 2.6 slice_convert_fusion
  460.2 0.6 copy.40
  460.8 1.9 pad_maximum_fusion
  462.7 2.6 maximum_convert_fusion
  465.3 1.3 copy.43
  466.8 0.8 copy.44
  (36 shorter events, 3.1 us)
Async XLA Ops:
  56.9 6.4 %copy-start.4 = (bf16[2048]{0:T(1024)(128)(2,1)S(1)}, bf16[2048]{0:T(1024)(128)(2,1)}, u32[]{:S(2)}) copy-start(bf16[2048]{0:T(1024)(128)(2,1)} %param.38) | copy-start | bytes 12292
  56.9 7.0 %copy-start.5 = (bf16[512]{0:T(512)(128)(2,1)S(1)}, bf16[512]{0:T(512)(128)(2,1)}, u32[]{:S(2)}) copy-start(bf16[512]{0:T(512)(128)(2,1)} %param.34) | copy-start | bytes 3076
  56.9 7.6 %copy-start.6 = (bf16[512]{0:T(512)(128)(2,1)S(1)}, bf16[512]{0:T(512)(128)(2,1)}, u32[]{:S(2)}) copy-start(bf16[512]{0:T(512)(128)(2,1)} %param.35) | copy-start | bytes 3076
  56.9 8.2 %copy-start.7 = (bf16[512]{0:T(512)(128)(2,1)S(1)}, bf16[512]{0:T(512)(128)(2,1)}, u32[]{:S(2)}) copy-start(bf16[512]{0:T(512)(128)(2,1)} %param.36) | copy-start | bytes 3076
  56.9 8.8 %copy-start.8 = (bf16[512]{0:T(512)(128)(2,1)S(1)}, bf16[512]{0:T(512)(128)(2,1)}, u32[]{:S(2)}) copy-start(bf16[512]{0:T(512)(128)(2,1)} %param.40) | copy-start | bytes 3076
  57.0 113.2 %all-to-all-start = ((bf16[8,256,512]{2,1,0:T(8,128)(2,1)}), bf16[8,256,512]{2,1,0:T(8,128)(2,1)S(1)}, u32[]{:S(2)}, u32[]{:S(2)}) async-start(bf16[8,256,512]{2,1,0:T(8,128)(2,1)} %param.41), calls=%async_computation | async-start | bytes 4194304 | tf_op jit(solution)/shard_map/all_to_all | solution.py:1225
  170.1 1.3 copy-start.2
  363.3 92.6 %slice-start = ((s8[4718592]{0:T(1024)(128)(4,1)}), s8[4194304]{0:T(1024)(128)(4,1)S(1)}, s32[]{:S(2)}) async-start(s8[4718592]{0:T(1024)(128)(4,1)} %bitcast.14), calls=%async_computation.1 | async-start | bytes 8388608
  363.3 92.6 %slice-start.1 = ((s8[4718592]{0:T(1024)(128)(4,1)}), s8[524288]{0:T(1024)(128)(4,1)S(1)}, s32[]{:S(2)}) async-start(s8[4718592]{0:T(1024)(128)(4,1)} %bitcast.14), calls=%async_computation.2 | async-start | bytes 1048576
  457.2 2.6 copy-start
  462.7 2.6 copy-start.1
  465.3 1.5 copy-start.3

commit v4 on v3

--- a/solution.py
+++ b/solution.py
@@ -12,12 +12,17 @@
 HEAD_DIM = 32
 PACK = 128 // HEAD_DIM
 VMEM_LIMIT = 56 * 1024 * 1024
+SAFE_SCORE = 80.0
 MESH = pl.DeviceIdType.MESH
 LOG2E = math.log2(math.e)
 QUERY_SCALE = LOG2E * HEAD_DIM ** (-0.5)
 
 
 epsilon = 1e-06
+
+
+EMBED_BIAS, MASK, FIRST_GAIN, FIRST_SHIFT, QUERY_BIAS, VALUE_BIAS = range(6)
+OUTPUT_BIAS, SECOND_GAIN, SECOND_SHIFT, CONTRACT_BIAS, EXPAND_BIAS = range(6, 11)
 
 
 def whole(shape):
@@ -347,40 +352,53 @@
 def enter_kernel(
     latents_ref,
     embed_ref,
-    embed_bias_ref,
     slot_ref,
     coarse_ref,
     fine_ref,
-    mask_ref,
-    gain_ref,
-    shift_ref,
     joint_ref,
-    query_bias_ref,
-    value_bias_ref,
-    stream_ref,
-    empty_ref,
-    normed_ref,
-    query_t_ref,
-    key_ref,
-    key_t_ref,
-    value_ref,
-    value_t_ref,
-    embedded_ref,
-    sems,
+    *refs,
 ):
+    (
+        stream_ref,
+        empty_ref,
+        normed_ref,
+        query_t_ref,
+        key_ref,
+        key_t_ref,
+        value_ref,
+        value_t_ref,
+        vector_ref,
+        latents_out_ref,
+        embedded_ref,
+        slot_row,
+        sems,
+    ) = refs[-13:]
+    vector_refs = refs[:-13]
     block, width = stream_ref.shape
     spot = Spot()
     capacity = embedded_ref.shape[0] // spot.splits
 
+    def vector(row):
+        return vector_ref[row : row + 1, :]
+
     @pl.when(pl.program_id(0) == 0)
     def _():
         count = spot.meet(spot.tree(False))
-        embedded = plain_dot(latents_ref[...], embed_ref[...]) + embed_bias_ref[...].astype(
-            jnp.float32
-        )
-        if capacity > latents_ref.shape[0]:
-            rest = jnp.zeros((capacity - latents_ref.shape[0], width), jnp.float32)
-            embedded = jnp.concatenate([embedded, rest], axis=0)
+        at = 0
+        for source in vector_refs:
+            for start in range(0, source.shape[0], width):
+                values = source[start : start + width].astype(jnp.float32)
+                vector_ref[at : at + 1, :] = values.reshape(1, width)
+                at += 1
+        latents = latents_ref[...]
+        rest = capacity - latents.shape[0]
+        if rest:
+            latents = jnp.concatenate(
+                [latents.astype(jnp.float32), jnp.zeros((rest, latents.shape[1]), jnp.float32)],
+                axis=0,
+            ).astype(jnp.bfloat16)
+        latents_out_ref[...] = latents
+        embedded = plain_dot(latents, embed_ref[...]) + vector(EMBED_BIAS)
 
         def held(core, chip):
             return embedded_ref.at[span_of((chip * 2 + core) * capacity, capacity)]
@@ -393,11 +411,13 @@
         for step in range(1, spot.half):
             share(step, spot.core, spot.chip, spot.peer(step)).start()
         share(0, spot.core, spot.chip, spot.sibling()).start()
+        for source in range(spot.splits):
+            slot_row[:, source * capacity : (source + 1) * capacity] = slot_ref[
+                source : source + 1, :capacity
+            ]
         for step in range(1, spot.half):
             share(step, spot.core, spot.chip_at(-step), spot.peer(step)).wait_recv()
-            share(
-                spot.half + step, spot.core, spot.chip_at(-step), spot.sibling()
-            ).start()
+            share(spot.half + step, spot.core, spot.chip_at(-step), spot.sibling()).start()
         for step in range(1, spot.half):
             share(step, spot.core, spot.chip, spot.peer(step)).wait_send()
         share(0, spot.core, spot.chip, spot.sibling()).wait_send()
@@ -408,7 +428,7 @@
             share(at, 1 - spot.core, spot.chip_at(-step), spot.sibling()).wait_recv()
 
     place = lax.broadcasted_iota(jnp.int32, (block, 1), 0) + pl.program_id(0) * block
-    fills = (place == slot_ref[...]).astype(jnp.float32)
+    fills = (place == slot_row[...]).astype(jnp.float32)
     empty = 1.0 - jnp.sum(fills, axis=1, keepdims=True)
     placed = plain_dot(fills.astype(jnp.bfloat16), embedded_ref[...])
     fine_rows = fine_ref.shape[0]
@@ -423,20 +443,18 @@
                 [sin * fine_cos + cos * fine_sin, cos * fine_cos - sin * fine_sin], axis=1
             )
         )
-    stream = placed + empty * mask_ref[...].astype(jnp.float32) + jnp.concatenate(tables, axis=0)
+    stream = placed + empty * vector(MASK) + jnp.concatenate(tables, axis=0)
     stream_ref[...] = stream
     empty_ref[...] = empty
     normed, _ = normalize(stream)
-    low = (normed * gain_ref[...].astype(jnp.float32) + shift_ref[...].astype(jnp.float32)).astype(
-        jnp.bfloat16
-    )
+    low = (normed * vector(FIRST_GAIN) + vector(FIRST_SHIFT)).astype(jnp.bfloat16)
     normed_ref[...] = low
-    query = plain_dot(low, joint_ref[:, :width]) + query_bias_ref[...].astype(jnp.float32)
+    query = plain_dot(low, joint_ref[:, :width]) + vector(QUERY_BIAS)
     query_t_ref[...] = (query * QUERY_SCALE).T.astype(jnp.bfloat16)
     keys = plain_dot(low, joint_ref[:, width : 2 * width])
     key_ref[...] = keys.astype(jnp.bfloat16)
     key_t_ref[...] = keys.T.astype(jnp.bfloat16)
-    values = plain_dot(low, joint_ref[:, 2 * width :]) + value_bias_ref[...].astype(jnp.float32)
+    values = plain_dot(low, joint_ref[:, 2 * width :]) + vector(VALUE_BIAS)
     value_ref[...] = values.astype(jnp.bfloat16)
     value_t_ref[...] = values.T.astype(jnp.bfloat16)
 
@@ -444,27 +462,23 @@
 def enter(
     latents,
     embed_weight,
-    embed_bias,
     slot_place,
     first_place,
     rows,
-    mask_token,
-    gain,
-    shift,
+    vectors,
     joint_weight,
-    query_bias,
-    value_bias,
 ):
     splits = lax.axis_size("seq")
     width = embed_weight.shape[1]
-    slots = slot_place.shape[0]
+    capacity = padded(latents.shape[0], 16)
+    slots = splits * capacity
+    vector_rows = sum(vector.shape[0] for vector in vectors) // width
     block = min(256, rows)
     fine_rows = min(32, block)
     fine = sinusoid(jnp.arange(fine_rows, dtype=jnp.int32), width)
     coarse = sinusoid(first_place + fine_rows * jnp.arange(rows // fine_rows, dtype=jnp.int32), width)
     row_block = pl.BlockSpec((block, width), lambda i: (i, 0))
     lane_block = pl.BlockSpec((width, block), lambda i: (0, i))
-    vector = whole((1, width))
     low = jax.ShapeDtypeStruct((rows, width), jnp.bfloat16)
     low_t = jax.ShapeDtypeStruct((width, rows), jnp.bfloat16)
     return pl.pallas_call(
@@ -473,17 +487,12 @@
         in_specs=[
             whole(latents.shape),
             whole(embed_weight.shape),
-            vector,
-            whole((1, slots)),
+            whole(slot_place.shape),
             pl.BlockSpec((1, block // fine_rows, width), lambda i: (i, 0, 0)),
             whole(fine.shape),
-            vector,
-            vector,
-            vector,
             whole((width, 3 * width)),
-            vector,
-            vector,
-        ],
+        ]
+        + [whole(vector.shape) for vector in vectors],
         out_specs=[
             row_block,
             pl.BlockSpec((block, 1), lambda i: (i, 0)),
@@ -493,6 +502,8 @@
             lane_block,
             row_block,
             lane_block,
+            whole((vector_rows, width)),
+            whole((capacity, latents.shape[1])),
         ],
         out_shape=[
             jax.ShapeDtypeStruct((rows, width), jnp.float32),
@@ -503,9 +514,12 @@
             low_t,
             low,
             low_t,
+            jax.ShapeDtypeStruct((vector_rows, width), jnp.float32),
+            jax.ShapeDtypeStruct((capacity, latents.shape[1]), latents.dtype),
         ],
         scratch_shapes=[
             pltpu.VMEM((slots, width), jnp.bfloat16),
+            pltpu.VMEM((1, slots), jnp.int32),
             pltpu.SemaphoreType.DMA((2, splits)),
         ],
         compiler_params=pltpu.CompilerParams(
@@ -520,61 +534,90 @@
     )(
         latents,
         embed_weight,
-        embed_bias[None, :],
-        slot_place[None, :],
+        slot_place,
         coarse.reshape(rows // block, block // fine_rows, width),
         fine,
-        mask_token[None, :],
-        gain[None, :],
-        shift[None, :],
         joint_weight,
-        query_bias[None, :],
-        value_bias[None, :],
+        *vectors,
     )
 
 
 def attend_kernel(
-    key_ref, query_ref, value_ref, mixed_ref, exact_ref, total_ref, raised_ref, scores_ref
+    key_ref, query_ref, value_ref, mixed_ref, exact_ref, total_ref, raised_ref, scores_ref, norm_ref
 ):
     span = key_ref.shape[0]
     block = query_ref.shape[1]
     slice_rows = min(256, span)
+    slices = span // slice_rows
     query = query_ref[...]
     head_row = lax.broadcasted_iota(jnp.int32, query.shape, 0) // HEAD_DIM
     ones = jnp.ones((16, slice_rows), jnp.bfloat16)
-    highest = None
-    for step in range(PACK + 1):
-        if step < PACK:
-            own_query = jnp.where(head_row == step, query, jnp.zeros_like(query))
-            partial_highest = jnp.full((8, block), -jnp.inf, jnp.float32)
-        if step > 0:
-            head = step - 1
-            rows = slice(head * HEAD_DIM, (head + 1) * HEAD_DIM)
-            mixed = jnp.zeros((HEAD_DIM + 16, block), jnp.float32)
-        for at in range(0, span, slice_rows):
-            part = slice(at, at + slice_rows)
-            if step < PACK:
+
+    @pl.when(pl.program_id(1) == 0)
+    def _():
+        keys = key_ref[...].astype(jnp.float32)
+        lane_head = lax.broadcasted_iota(jnp.int32, (128, 128), 0) // HEAD_DIM
+        column = lax.broadcasted_iota(jnp.int32, (128, 128), 1)
+        pick = (lane_head == column).astype(jnp.float32).astype(jnp.bfloat16)
+        norms = plain_dot((keys * keys).astype(jnp.bfloat16), pick)
+        norm_ref[...] = jnp.broadcast_to(jnp.max(norms, axis=0, keepdims=True), norm_ref.shape)
+
+    squares = query.astype(jnp.float32)
+    squares = squares * squares
+    bound = jnp.zeros((1, 1), jnp.float32)
+    for head in range(PACK):
+        rows = slice(head * HEAD_DIM, (head + 1) * HEAD_DIM)
+        longest = jnp.max(
+            jnp.sum(squares[rows], axis=0, keepdims=True), axis=1, keepdims=True
+        )
+        bound = jnp.maximum(bound, longest * norm_ref[0:1, head : head + 1])
+    small = bound[0, 0] * 1.02 < SAFE_SCORE**2
+
+    def run(shifted):
+        lag = slices if shifted else min(2, slices)
+        steps = PACK * slices
+        highest = {}
+        own_query = partial_highest = mixed = None
+        for now in range(steps + lag):
+            if now < steps:
+                head, at = divmod(now, slices)
+                part = slice(at * slice_rows, (at + 1) * slice_rows)
+                if at == 0:
+                    own_query = jnp.where(head_row == head, query, jnp.zeros_like(query))
+                    partial_highest = jnp.full((8, block), -jnp.inf, jnp.float32)
                 scores = plain_dot(key_ref[part, :], own_query)
-                scores_ref[step % 2, part, :] = scores
-                partial_highest = jnp.maximum(
-                    partial_highest, jnp.max(scores.reshape(slice_rows // 8, 8, block), axis=0)
-                )
-            if step > 0:
-                raised = jnp.exp2(scores_ref[(step - 1) % 2, part, :] - highest).astype(
-                    jnp.bfloat16
-                )
+                scores_ref[now % (lag + 1)] = scores
+                if shifted:
+                    partial_highest = jnp.maximum(
+                        partial_highest, jnp.max(scores.reshape(slice_rows // 8, 8, block), axis=0)
+                    )
+                    if at == slices - 1:
+                        highest[head] = jnp.max(partial_highest, axis=0, keepdims=True)
+            if now >= lag:
+                head, at = divmod(now - lag, slices)
+                rows = slice(head * HEAD_DIM, (head + 1) * HEAD_DIM)
+                part = slice(at * slice_rows, (at + 1) * slice_rows)
+                scores = scores_ref[(now - lag) % (lag + 1)]
+                if shifted:
+                    scores = scores - highest[head]
+                raised = jnp.exp2(scores).astype(jnp.bfloat16)
                 raised_ref[head, part, :] = raised
-                mixed = mixed + plain_dot(
-                    jnp.concatenate([value_ref[rows, part], ones], axis=0), raised
-                )
-        if step > 0:
-            total = mixed[HEAD_DIM : HEAD_DIM + 1]
-            total_ref[0, head : head + 1, :] = total
-            mixed = mixed[:HEAD_DIM] / total
-            exact_ref[rows, :] = mixed
-            mixed_ref[rows, :] = mixed.astype(jnp.bfloat16)
-        if step < PACK:
-            highest = jnp.max(partial_highest, axis=0, keepdims=True)
+                term = plain_dot(jnp.concatenate([value_ref[rows, part], ones], axis=0), raised)
+                mixed = term if at == 0 else mixed + term
+                if at == slices - 1:
+                    total = mixed[HEAD_DIM : HEAD_DIM + 1]
+                    total_ref[0, head : head + 1, :] = total
+                    mean = mixed[:HEAD_DIM] / total
+                    exact_ref[rows, :] = mean
+                    mixed_ref[rows, :] = mean.astype(jnp.bfloat16)
+
+    @pl.when(small)
+    def _():
+        run(False)
+
+    @pl.when(jnp.logical_not(small))
+    def _():
+        run(True)
 
 
 def attend(keys, query_t, value_t):
@@ -603,7 +646,10 @@
             jax.ShapeDtypeStruct((groups, 8, rows), jnp.float32),
             jax.ShapeDtypeStruct((HEADS, span, rows), jnp.bfloat16),
         ],
-        scratch_shapes=[pltpu.VMEM((2, span, block), jnp.float32)],
+        scratch_shapes=[
+            pltpu.VMEM((span // min(256, span) + 1, min(256, span), block), jnp.float32),
+            pltpu.VMEM((8, 128), jnp.float32),
+        ],
         compiler_params=pltpu.CompilerParams(vmem_limit_bytes=VMEM_LIMIT),
         cost_estimate=pl.CostEstimate(
             flops=HEADS * span * rows * 512,
@@ -619,13 +665,9 @@
     mixed_ref,
     cotangent_ref,
     output_ref,
-    output_bias_ref,
-    gain_ref,
-    shift_ref,
     expand_ref,
-    expand_bias_ref,
     contract_ref,
-    contract_bias_ref,
+    vector_ref,
     decoded_ref,
     grad_middle_ref,
     grad_attended_ref,
@@ -639,6 +681,9 @@
     width = stream_ref.shape[1]
     chunks = expand_ref.shape[1] // width
 
+    def vector(row):
+        return vector_ref[row : row + 1, :]
+
     @pl.when(pl.program_id(0) == 0)
     def _():
         expand_sum[...] = jnp.zeros_like(expand_sum)
@@ -651,17 +696,17 @@
     middle = (
         stream_ref[...]
         + plain_dot(turned(mixed_t), output_ref[...])
-        + output_bias_ref[...].astype(jnp.float32)
+        + vector(OUTPUT_BIAS)
     )
     normed, scale = normalize(middle)
-    gain = gain_ref[...].astype(jnp.float32)
-    low = (normed * gain + shift_ref[...].astype(jnp.float32)).astype(jnp.bfloat16)
+    gain = vector(SECOND_GAIN)
+    low = (normed * gain + vector(SECOND_SHIFT)).astype(jnp.bfloat16)
     low_t = turned(low)
-    output = middle + contract_bias_ref[...].astype(jnp.float32)
+    output = middle + vector(CONTRACT_BIAS)
     grad_normed = jnp.zeros_like(middle)
     for chunk in range(chunks):
         part = slice(chunk * width, (chunk + 1) * width)
-        hidden = plain_dot(low, expand_ref[:, part]) + expand_bias_ref[:, part].astype(jnp.float32)
+        hidden = plain_dot(low, expand_ref[:, part]) + vector(EXPAND_BIAS + chunk)
         below = 0.5 + 0.5 * lax.erf(hidden * math.sqrt(0.5))
         slope = below + hidden * jnp.exp(-0.5 * hidden * hidden) * (1.0 / math.sqrt(2 * math.pi))
         active = (hidden * below).astype(jnp.bfloat16)
@@ -698,13 +743,9 @@
     mixed_t,
     cotangent,
     output_weight,
-    output_bias,
-    gain,
-    shift,
     expand_weight,
-    expand_bias,
     contract_weight,
-    contract_bias,
+    vectors,
     flat_rows,
 ):
     rows, width = stream.shape
@@ -712,7 +753,6 @@
     block = min(256, rows)
     row_block = pl.BlockSpec((block, width), lambda i: (i, 0))
     lane_block = pl.BlockSpec((width, block), lambda i: (0, i))
-    vector = whole((1, width))
     small_rows = hidden // width + 4
     return pl.pallas_call(
         middle_kernel,
@@ -722,13 +762,9 @@
             lane_block,
             row_block,
             whole((width, width)),
-            vector,
-            vector,
-            vector,
             whole((width, hidden)),
-            whole((1, hidden)),
             whole((hidden, width)),
-            vector,
+            whole(vectors.shape),
         ],
         out_specs=[
             row_block,
@@ -762,13 +798,9 @@
         mixed_t,
         cotangent,
         output_weight,
-        output_bias[None, :],
-        gain[None, :],
-        shift[None, :],
         expand_weight,
-        expand_bias[None, :],
         contract_weight,
-        contract_bias[None, :],
+        vectors,
     )
 
 
@@ -783,15 +815,19 @@
     grad_ref,
     flat_ref,
     rows_ref,
+    latents_ref,
     grad_query_ref,
     grad_key_ref,
     grad_value_ref,
     summed_ref,
     decoded_ref,
+    gathered_ref,
     key_sum,
     value_sum,
     exchange_sems,
     exchange_local,
+    gather_sems,
+    gather_local,
     *sum_refs,
 ):
     spot = Spot()
@@ -816,6 +852,21 @@
             rows_ref.at[span_of(mine * share, share)], decoded_ref.at[mine], exchange_local
         )
 
+    capacity = latents_ref.shape[0]
+
+    def held(core, chip):
+        return gathered_ref.at[span_of((chip * 2 + core) * capacity, capacity)]
+
+    def share_own(at, device):
+        return send(latents_ref, held(spot.core, spot.chip), gather_sems, at, device)
+
+    def pass_on(at, core, step):
+        place = held(core, spot.chip_at(-step))
+        return send(place, place, gather_sems, at, spot.sibling())
+
+    def keep_own():
+        return pltpu.make_async_copy(latents_ref, held(spot.core, spot.chip), gather_local)
+
     step_now = pl.program_id(0) * pl.num_programs(1) + pl.program_id(1)
 
     def at_step(fraction):
@@ -834,22 +885,32 @@
     def _():
         tree.near_to_far()
 
-    @at_step(9)
+    @at_step(8)
     def _():
         tree.far_to_deep()
         own_rows().start()
         for step in range(1, clips):
             exchange(step).start()
-
-    @at_step(13)
+        keep_own().start()
+        for step in range(1, spot.half):
+            share_own(step, spot.peer(step)).start()
+        share_own(0, spot.sibling()).start()
+
+    @at_step(12)
     def _():
         tree.deep_to_layer()
 
-    @at_step(17)
+    @at_step(16)
     def _():
         tree.layer_to_part()
 
-    @at_step(25)
+    @at_step(21)
+    def _():
+        for step in range(1, spot.half):
+            pass_on(step, spot.core, step).wait_recv()
+            pass_on(spot.half + step, spot.core, step).start()
+
+    @at_step(26)
     def _():
         tree.part_to_half()
 
@@ -867,6 +928,14 @@
                 step,
                 (spot.layer, part * clips + member(step)),
             ).wait_recv()
+        keep_own().wait()
+        for step in range(1, spot.half):
+            share_own(step, spot.peer(step)).wait_send()
+        share_own(0, spot.sibling()).wait_send()
+        pass_on(0, 1 - spot.core, 0).wait_recv()
+        for step in range(1, spot.half):
+            pass_on(spot.half + step, spot.core, step).wait_send()
+            pass_on(spot.half + step, 1 - spot.core, step).wait_recv()
 
     @pl.when(pl.program_id(1) == 0)
     def _():
@@ -885,22 +954,34 @@
     inner = grad * exact_ref[...]
     grad_turned = grad.T.astype(jnp.bfloat16)
     query_turned = turned(query_ref[...])
-    for head in range(PACK):
-        rows = slice(head * HEAD_DIM, (head + 1) * HEAD_DIM)
-        own_grad = jnp.where(head_row == head, grad_low, jnp.zeros_like(grad_low))
-        grad_weight = plain_dot(value_ref[...], own_grad)
-        row_inner = jnp.sum(inner[rows], axis=0, keepdims=True)
-        raised = raised_ref[head]
-        grad_scores = raised * (grad_weight - row_inner).astype(jnp.bfloat16)
-        value_sum[...] += plain_dot(
-            raised, jnp.where(head_col == head, grad_turned, jnp.zeros_like(grad_turned))
-        )
-        key_sum[...] += plain_dot(
-            grad_scores, jnp.where(head_col == head, query_turned, jnp.zeros_like(query_turned))
-        )
-        grad_query_ref[rows, :] = (
-            plain_dot(key_ref[rows, :], grad_scores) * HEAD_DIM ** (-0.5)
-        ).astype(jnp.bfloat16)
+    span = value_ref.shape[0]
+    slice_rows = min(256, span)
+    units = [(head, at) for head in range(PACK) for at in range(0, span, slice_rows)]
+    lag = 2
+    weights = {}
+    grad_query = None
+    for now in range(len(units) + lag):
+        if now < len(units):
+            head, at = units[now]
+            own_grad = jnp.where(head_row == head, grad_low, jnp.zeros_like(grad_low))
+            weights[now] = plain_dot(value_ref[at : at + slice_rows, :], own_grad)
+        if now >= lag:
+            head, at = units[now - lag]
+            rows = slice(head * HEAD_DIM, (head + 1) * HEAD_DIM)
+            part = slice(at, at + slice_rows)
+            row_inner = jnp.sum(inner[rows], axis=0, keepdims=True)
+            raised = raised_ref[head, part, :]
+            grad_scores = raised * (weights.pop(now - lag) - row_inner).astype(jnp.bfloat16)
+            value_sum[part, :] += plain_dot(
+                raised, jnp.where(head_col == head, grad_turned, jnp.zeros_like(grad_turned))
+            )
+            key_sum[part, :] += plain_dot(
+                grad_scores, jnp.where(head_col == head, query_turned, jnp.zeros_like(query_turned))
+            )
+            term = plain_dot(key_ref[rows, part], grad_scores)
+            grad_query = term if at == 0 else grad_query + term
+            if at + slice_rows == span:
+                grad_query_ref[rows, :] = (grad_query * HEAD_DIM ** (-0.5)).astype(jnp.bfloat16)
 
     @pl.when(pl.program_id(1) == pl.num_programs(1) - 1)
     def _():
@@ -908,7 +989,7 @@
         grad_value_ref[...] = value_sum[...].astype(jnp.bfloat16)
 
 
-def attend_back(raised, total, values, key_t, query_t, exact_t, grad_t, flat, decoded_rows):
+def attend_back(raised, total, values, key_t, query_t, exact_t, grad_t, flat, decoded_rows, latents):
     splits, layers = lax.axis_size("seq"), lax.axis_size("dp")
     clips, share, _ = decoded_rows.shape
     width, rows = query_t.shape
@@ -929,6 +1010,7 @@
             lane_block,
             pl.BlockSpec(memory_space=pl.ANY),
             pl.BlockSpec(memory_space=pl.ANY),
+            pl.BlockSpec(memory_space=pl.ANY),
         ],
         out_specs=[
             lane_block,
@@ -936,6 +1018,7 @@
             pl.BlockSpec((span, 128), lambda g, i: (0, g)),
             pl.BlockSpec(memory_space=pl.ANY),
             pl.BlockSpec(memory_space=pl.ANY),
+            pl.BlockSpec(memory_space=pl.ANY),
         ],
         out_shape=[
             jax.ShapeDtypeStruct((width, rows), jnp.bfloat16),
@@ -943,11 +1026,14 @@
             jax.ShapeDtypeStruct((span, width), jnp.bfloat16),
             jax.ShapeDtypeStruct(flat.shape, flat.dtype),
             jax.ShapeDtypeStruct(decoded_rows.shape, decoded_rows.dtype),
+            jax.ShapeDtypeStruct((splits * latents.shape[0], latents.shape[1]), latents.dtype),
         ],
         scratch_shapes=[
             pltpu.VMEM((span, 128), jnp.float32),
             pltpu.VMEM((span, 128), jnp.float32),
             pltpu.SemaphoreType.DMA((2, clips)),
+            pltpu.SemaphoreType.DMA,
+            pltpu.SemaphoreType.DMA((2, splits)),
             pltpu.SemaphoreType.DMA,
         ]
         + TreeSum.scratch(flat.shape[0], flat.shape[1], True, splits, layers),
@@ -960,7 +1046,7 @@
             transcendentals=0,
         ),
         name="attend_back",
-    )(raised, total, values, key_t, query_t, exact_t, grad_t, flat, decoded_rows.reshape(clips * share, width))
+    )(raised, total, values, key_t, query_t, exact_t, grad_t, flat, decoded_rows.reshape(clips * share, width), latents)
 
 
 def leave_kernel(
@@ -971,7 +1057,7 @@
     empty_ref,
     low_ref,
     grad_middle_ref,
-    gain_ref,
+    vector_ref,
     joint_ref,
     slot_ref,
     latents_ref,
@@ -985,7 +1071,7 @@
     grad_all,
     joint_flat,
     embed_flat,
-    near_out,
+    back_all,
     near_in,
     far_out,
     far_in,
@@ -995,7 +1081,7 @@
     block, width = stream_ref.shape
     step_now = pl.program_id(0)
     spot = Spot()
-    capacity = near_out.shape[0] // spot.half
+    capacity = back_all.shape[0] // spot.splits
     others = spot.tree()
 
     @pl.when(step_now == 0)
@@ -1012,7 +1098,7 @@
         grad_normed = grad_normed + trail_dot(side, joint_ref[:, at * width : (at + 1) * width])
         joint_sum[at * width : (at + 1) * width, :] += plain_dot(low_t, side)
     grad_stream = grad_middle_ref[...] + normalize_back(
-        grad_normed * gain_ref[...].astype(jnp.float32), normed, scale
+        grad_normed * vector_ref[FIRST_GAIN : FIRST_GAIN + 1, :], normed, scale
     )
     grad_all[pl.ds(pl.multiple_of(step_now * block, block), block), :] = grad_stream.astype(
         jnp.bfloat16
@@ -1034,16 +1120,21 @@
         place = lax.broadcasted_iota(jnp.int32, (1, grad_all.shape[0]), 1)
 
         def gathered(owner):
-            slots = slot_ref[pl.ds(pl.multiple_of(owner * capacity, 8), capacity), :]
-            takes = (slots == place).astype(jnp.float32).astype(jnp.bfloat16)
+            slots = slot_ref[pl.ds(owner, 1), :].astype(jnp.float32)
+            slots = jnp.broadcast_to(slots, (8, slots.shape[1])).T[:capacity, 0:1]
+            takes = (slots.astype(jnp.int32) == place).astype(jnp.float32).astype(jnp.bfloat16)
             return plain_dot(takes, grad_all[...])
+
+        def rows_of(owner):
+            return span_of(owner * capacity, capacity)
 
         def part(at):
             return pl.ds(at * capacity, capacity)
 
         def near_copy(step):
+            owner = spot.chip_at(step) * 2 + 1 - spot.core
             return send(
-                near_out.at[part(step)], near_in.at[part(step)], sems, step, spot.sibling()
+                back_all.at[rows_of(owner)], near_in.at[part(step)], sems, step, spot.sibling()
             )
 
         def far_copy(step):
@@ -1057,34 +1148,35 @@
 
         order = list(range(1, spot.half)) + [0]
         for step in order:
-            near_out[part(step), :] = gathered(spot.chip_at(step) * 2 + 1 - spot.core).astype(
-                jnp.bfloat16
-            )
+            owner = spot.chip_at(step) * 2 + 1 - spot.core
+            back_all[rows_of(owner), :] = gathered(owner).astype(jnp.bfloat16)
             near_copy(step).start()
         joint_tree.near_to_far()
         for step in order:
+            owner = spot.chip_at(step) * 2 + spot.core
+            own = gathered(owner)
+            back_all[rows_of(owner), :] = own.astype(jnp.bfloat16)
             near_copy(step).wait()
-            own = gathered(spot.chip_at(step) * 2 + spot.core)
             own = own + near_in[part(step), :].astype(jnp.float32)
             if step > 0:
                 far_out[part(step - 1), :] = own.astype(jnp.bfloat16)
                 far_copy(step).start()
-        for step in range(1, spot.half):
-            far_copy(step).wait()
-            own = own + far_in[part(step - 1), :].astype(jnp.float32)
-        grad_embedded = own[: latents_ref.shape[0]].astype(jnp.bfloat16)
-        small_sum[5:6, :] = column_sum(grad_embedded)
         embed_rows = embed_ref.shape[0]
-        embed_flat[:embed_rows, :] = lead_dot(latents_ref[...], grad_embedded).astype(jnp.bfloat16)
+        embed_flat[:embed_rows, :] = lead_dot(latents_ref[...], back_all[...]).astype(jnp.bfloat16)
+        small_sum[5:6, :] = column_sum(back_all[...])
         small = jnp.concatenate([early_ref[...], small_sum[...]], axis=0)
         rest = embed_flat.shape[0] - embed_rows - small.shape[0]
         if rest:
             small = jnp.concatenate([small, jnp.zeros((rest, width), jnp.float32)], axis=0)
         embed_flat[embed_rows:, :] = small.astype(jnp.bfloat16)
         embed_tree.start()
-        latent_grad_ref[...] = trail_dot(grad_embedded, embed_ref[...]).astype(jnp.bfloat16)
         joint_tree.far_to_deep()
         embed_tree.near_to_far()
+        for step in range(1, spot.half):
+            far_copy(step).wait()
+            own = own + far_in[part(step - 1), :].astype(jnp.float32)
+        grad_embedded = own[: latent_grad_ref.shape[0]].astype(jnp.bfloat16)
+        latent_grad_ref[...] = trail_dot(grad_embedded, embed_ref[...]).astype(jnp.bfloat16)
         joint_tree.deep_to_layer()
         embed_tree.far_to_deep()
         joint_tree.part_to_half()
@@ -1102,16 +1194,18 @@
     empty,
     low,
     grad_middle,
-    gain,
+    vectors,
     joint_weight,
     slot_place,
-    latents,
+    latents_all,
     embed_weight,
     early_small,
+    own_rows,
 ):
     splits, layers = lax.axis_size("seq"), lax.axis_size("dp")
     rows, width = stream.shape
-    slots = slot_place.shape[0]
+    slots = latents_all.shape[0]
+    latent_shape = (own_rows, latents_all.shape[1])
     capacity = slots // splits
     half = splits // 2
     block = min(256, rows)
@@ -1130,20 +1224,20 @@
             pl.BlockSpec((block, 1), lambda i: (i, 0)),
             row_block,
             row_block,
-            whole((1, width)),
+            whole(vectors.shape),
             whole((width, 3 * width)),
-            whole((slots, 1)),
-            whole(latents.shape),
+            whole(slot_place.shape),
+            pl.BlockSpec(latents_all.shape, lambda i: (0, 0), pipeline_mode=pl.Buffered(1)),
             whole(embed_weight.shape),
             whole(early_small.shape),
         ],
         out_specs=[
-            whole(latents.shape),
+            whole(latent_shape),
             pl.BlockSpec(memory_space=pl.ANY),
             pl.BlockSpec(memory_space=pl.ANY),
         ],
         out_shape=[
-            jax.ShapeDtypeStruct(latents.shape, jnp.bfloat16),
+            jax.ShapeDtypeStruct(latent_shape, jnp.bfloat16),
             jax.ShapeDtypeStruct((joint_rows, width), jnp.bfloat16),
             jax.ShapeDtypeStruct((embed_rows, width), jnp.bfloat16),
         ],
@@ -1153,7 +1247,7 @@
             pltpu.VMEM((rows, width), jnp.bfloat16),
             pltpu.VMEM((joint_rows, width), jnp.bfloat16),
             pltpu.VMEM((embed_rows, width), jnp.bfloat16),
-            pltpu.VMEM((half * capacity, width), jnp.bfloat16),
+            pltpu.VMEM((slots, width), jnp.bfloat16),
             pltpu.VMEM((half * capacity, width), jnp.bfloat16),
             pltpu.VMEM((max(half - 1, 1) * capacity, width), jnp.bfloat16),
             pltpu.VMEM((max(half - 1, 1) * capacity, width), jnp.bfloat16),
@@ -1178,13 +1272,85 @@
         empty,
         low,
         grad_middle,
-        gain[None, :],
+        vectors,
         joint_weight,
-        slot_place[:, None],
-        latents,
+        slot_place,
+        latents_all,
         embed_weight,
         early_small,
     )
+
+
+def finish_kernel(
+    expand_ref,
+    contract_ref,
+    output_ref,
+    joint_ref,
+    embed_ref,
+    small_ref,
+    expand_out,
+    contract_out,
+    output_out,
+    joint_out,
+    embed_out,
+    *small_outs,
+):
+    for source, target in (
+        (expand_ref, expand_out),
+        (contract_ref, contract_out),
+        (output_ref, output_out),
+        (joint_ref, joint_out),
+        (embed_ref, embed_out),
+    ):
+        target[...] = source[...].astype(jnp.float32)
+    small = small_ref[...].astype(jnp.float32)
+    width = small.shape[1]
+    at = 0
+    for target in small_outs:
+        for start in range(0, target.shape[0], width):
+            target[start : start + width] = small[at]
+            at += 1
+
+
+def finish(early_sum, joint_sum, embed_sum, hidden, embed_rows, small_sizes):
+    width = early_sum.shape[1]
+    chunks = hidden // width
+    square = (width, width)
+    embed_block = (embed_rows // chunks, width)
+    sides = joint_sum.shape[0] // width
+    return pl.pallas_call(
+        finish_kernel,
+        grid=(chunks,),
+        in_specs=[
+            pl.BlockSpec(square, lambda i: (i, 0)),
+            pl.BlockSpec(square, lambda i: (chunks + i, 0)),
+            pl.BlockSpec(square, lambda i: (2 * chunks, 0)),
+            pl.BlockSpec(square, lambda i: (jnp.minimum(i, sides - 1), 0)),
+            pl.BlockSpec(embed_block, lambda i: (i, 0)),
+            pl.BlockSpec((16, width), lambda i: (embed_rows // 16, 0)),
+        ],
+        out_specs=[
+            pl.BlockSpec(square, lambda i: (0, i)),
+            pl.BlockSpec(square, lambda i: (i, 0)),
+            pl.BlockSpec(square, lambda i: (0, 0)),
+            pl.BlockSpec(square, lambda i: (0, jnp.minimum(i, sides - 1))),
+            pl.BlockSpec(embed_block, lambda i: (i, 0)),
+        ]
+        + [whole((size,)) for size in small_sizes],
+        out_shape=[
+            jax.ShapeDtypeStruct((width, hidden), jnp.float32),
+            jax.ShapeDtypeStruct((hidden, width), jnp.float32),
+            jax.ShapeDtypeStruct(square, jnp.float32),
+            jax.ShapeDtypeStruct((width, sides * width), jnp.float32),
+            jax.ShapeDtypeStruct((embed_rows, width), jnp.float32),
+        ]
+        + [jax.ShapeDtypeStruct((size,), jnp.float32) for size in small_sizes],
+        compiler_params=pltpu.CompilerParams(vmem_limit_bytes=VMEM_LIMIT),
+        cost_estimate=pl.CostEstimate(
+            flops=0, bytes_accessed=12 * width * (hidden + width), transcendentals=0
+        ),
+        name="finish",
+    )(early_sum, early_sum, early_sum, joint_sum, embed_sum, embed_sum)
 
 
 def body(
@@ -1235,22 +1401,39 @@
     mine = live & ((clip_ids % clip_count).reshape(splits, capacity) == own_clip)
     slot_place = jnp.where(mine, restore.reshape(splits, capacity) - first_place, -1)
     slot_place = jnp.pad(
-        slot_place, ((0, 0), (0, padded(capacity, 16) - capacity)), constant_values=-1
-    ).reshape(-1)
-
-    stream, empty, first_low, query_t, keys, key_t, values, value_t = enter(
+        slot_place, ((0, 0), (0, padded(capacity, 128) - capacity)), constant_values=-1
+    )
+    (
+        stream,
+        empty,
+        first_low,
+        query_t,
+        keys,
+        key_t,
+        values,
+        value_t,
+        vectors,
+        latents,
+    ) = enter(
         latents,
         embed_weight,
-        embed_bias,
         slot_place,
         first_place,
         rows,
-        mask_token,
-        first_gain,
-        first_shift,
+        [
+            embed_bias,
+            mask_token,
+            first_gain,
+            first_shift,
+            query_bias,
+            value_bias,
+            output_bias,
+            second_gain,
+            second_shift,
+            contract_bias,
+            expand_bias,
+        ],
         joint_weight,
-        query_bias,
-        value_bias,
     )
     cotangent, keys = lax.optimization_barrier((cotangent, keys))
     grad_output = to_clips(cotangent).reshape(rows, model_width)
@@ -1270,16 +1453,12 @@
         mixed_t,
         grad_output,
         output_weight,
-        output_bias,
-        second_gain,
-        second_shift,
         expand_weight,
-        expand_bias,
         contract_weight,
-        contract_bias,
+        vectors,
         padded(2 * expand_weight.shape[1] + model_width, splits * lax.axis_size("dp") * 16),
     )
-    grad_query_t, grad_key, grad_value, early_sum, decoded = attend_back(
+    grad_query_t, grad_key, grad_value, early_sum, decoded, latents_all = attend_back(
         raised,
         total,
         values,
@@ -1289,6 +1468,7 @@
         grad_attended_t,
         early_flat,
         decoded_rows.reshape(clip_count, clip_share, model_width),
+        latents,
     )
     if sharers > 1:
         grad_key, grad_value = (
@@ -1305,41 +1485,40 @@
         empty,
         first_low,
         grad_middle,
-        first_gain,
+        vectors,
         joint_weight,
         slot_place,
-        latents,
+        latents_all,
         embed_weight,
         early_small,
-    )
-
-    def columns(stack):
-        return jnp.concatenate(jnp.split(stack, stack.shape[0] // model_width, axis=0), axis=1)
-
+        capacity,
+    )
     hidden_width = expand_weight.shape[1]
-    chunks = hidden_width // model_width
-    grad_expand = columns(early_sum[:hidden_width])
-    grad_contract = early_sum[hidden_width : 2 * hidden_width]
-    grad_output_weight = early_sum[2 * hidden_width : 2 * hidden_width + model_width]
-    grad_expand, grad_contract, grad_output_weight = (
-        summed.astype(jnp.float32) for summed in (grad_expand, grad_contract, grad_output_weight)
-    )
-    grad_joint_weight = columns(joint_sum.astype(jnp.float32))
-    at = embed_weight.shape[0]
-    grad_embed_weight = embed_sum[:at].astype(jnp.float32)
-    small = embed_sum[at:].astype(jnp.float32)
-    grad_expand_bias = small[:chunks].reshape(-1)
-    grad_contract_bias, grad_output_bias, grad_second_gain, grad_second_shift = small[
-        chunks : chunks + 4
-    ]
     (
+        grad_expand,
+        grad_contract,
+        grad_output_weight,
+        grad_joint_weight,
+        grad_embed_weight,
+        grad_expand_bias,
+        grad_contract_bias,
+        grad_output_bias,
+        grad_second_gain,
+        grad_second_shift,
         grad_mask,
         grad_first_gain,
         grad_first_shift,
         grad_query_bias,
         grad_value_bias,
         grad_embed_bias,
-    ) = small[chunks + 4 : chunks + 10]
+    ) = finish(
+        early_sum,
+        joint_sum,
+        embed_sum,
+        hidden_width,
+        embed_weight.shape[0],
+        [hidden_width] + [model_width] * 10,
+    )
     return (
         decoded,
         latent_grad,

time: 469 us -> 407 us (0.87)
  Pallas kernels: 428 us -> 393 us
  local copies, waits for them, and re-layouts: 19.3 us -> 4.4 us
  other arithmetic: 15.7 us -> 4.02 us
    pallas_call x1, Pallas kernels: 104 us -> 73.9 us  [attend(): pl.pallas_call(attend_kernel, grid=(groups, rows // block), in_specs=[pl....]
    pallas_call x1, Pallas kernels: 88.5 us -> 74 us  [leave(): pl.pallas_call(leave_kernel, grid=(rows // block,), in_specs=[lane_block,...]
    broadcast_in_dim x11 -> x0, local copies, waits for them, and re-layouts: 10.5 us -> none  [the longest x1 1.26 us: enter(): gain[None, :]]
    convert_element_type x4 -> x0, other arithmetic: 8.58 us -> none  [the longest x2 5.16 us: body(): summed.astype(jnp.float32)]
    pallas_call x0 -> x1, Pallas kernels: none -> 8.4 us  [finish(): pl.pallas_call(finish_kernel, grid=(chunks,), in_specs=[pl.BlockSpec(squa...]
  transfers between devices with their start and end apart: 1 -> 1, of which waited for: 0 -> 0; matrix products, arithmetic and copies ran while one was open for 1% -> 0% of each run, Pallas kernels for 22% -> 18%
where the time goes in v4:
time: 407 us; the launch traced here: 406 us
  Pallas kernels  393 us (97%)
  local copies, waits for them, and re-layouts  4.4 us (1%)
    pallas_call x1, Pallas kernels, attend_back(): pl.pallas_call(partial(attend_back_kernel, groups * (rows // block)), gri...  146 us
    pallas_call x1, Pallas kernels, leave(): pl.pallas_call(leave_kernel, grid=(rows // block,), in_specs=[lane_block,...  74 us
    pallas_call x1, Pallas kernels, attend(): pl.pallas_call(attend_kernel, grid=(groups, rows // block), in_specs=[pl....  73.9 us
    pallas_call x1, Pallas kernels, middle_block(): pl.pallas_call(middle_kernel, grid=(rows // block,), in_specs=[row_block,...  45.9 us
    pallas_call x1, Pallas kernels, enter(): pl.pallas_call(enter_kernel, grid=(rows // block,), in_specs=[whole(laten...  44.3 us
    pallas_call x1, Pallas kernels, finish(): pl.pallas_call(finish_kernel, grid=(chunks,), in_specs=[pl.BlockSpec(squa...  8.4 us
  transfers between devices with their start and end apart: 1, of which 0 were waited for; matrix products, arithmetic and copies ran while one was open for 0% of the time, Pallas kernels for 18%

profile of v4, /device:TPU:0, one launch (start us, length us, event | category | flops | bytes accessed | tf_op | source)
XLA Modules:
  0.0 405.5 jit_solution(14592126454332147591)
XLA Ops:
  0.7 0.7 fusion.1
  1.4 0.1 eq.15
  1.6 0.7 broadcast_subtract_fusion
  2.3 0.1 sub.16
  2.4 0.7 fusion.3
  3.1 0.6 pad.4.slot_ref
  3.7 0.2 multiply_sine_fusion.1
  3.9 0.3 multiply_sine_fusion
  4.2 0.6 pad_maximum_fusion.1.fine_ref
  4.9 0.7 pad_maximum_fusion.coarse_ref
  5.5 44.3 %enter.1 = (f32[2048,512]{1,0:T(8,128)}, f32[2048,1]{1,0:T(8,128)}, bf16[2048,512]{1,0:T(8,128)(2,1)}, bf16[512,2048]{1,0:T(8,128)(2,1)}, bf16[2048,512]{1,0:T(8...) custom-call(bf16[408,768]{1,0:T(8,128)(2,1)} %latents_ref.1, ...), custom_call_target="tpu_custom_call" | custom-call | flops 10200547328 | bytes 20971520 | tf_op jit(solution)/shard_map/enter/pallas_call | solution.py:484
  49.9 3.6 all-to-all-start
  53.5 73.9 %attend.1 = (bf16[512,2048]{1,0:T(8,128)(2,1)}, f32[512,2048]{1,0:T(8,128)}, f32[4,8,2048]{2,1,0:T(8,128)}, bf16[16,2048,2048]{2,1,0:T(8,128)(2,1)}) custom-call(bf16[2048,512]{1,0:T(8,128)(2,1)} %get-tuple-element.65.key_ref, bf16[512,2048]{1,0:T(8,128)(2,1)} %get-tuple-element.66.query_ref, bf16[512,2048]{1,0:T(8,128)(2,1)} %get-tuple-element.67.value_ref), custom_call_target="tpu_custom_call" | custom-call | flops 34359738368 | bytes 134217728 | tf_op jit(solution)/shard_map/attend/pallas_call | solution.py:629
  127.4 0.0 all-to-all-done
  127.4 0.0 copy-start.1
  127.4 1.3 copy-done.1
  128.7 45.9 %middle.1 = (bf16[2048,512]{1,0:T(8,128)(2,1)}, f32[2048,512]{1,0:T(8,128)}, bf16[512,2048]{1,0:T(8,128)(2,1)}, bf16[4608,512]{1,0:T(8,128)(2,1)}, f32[8,512]{1,0:T(8,128)}) custom-call(f32[2048,512]{1,0:T(8,128)} %get-tuple-element.73.stream_ref, bf16[512,2048]{1,0:T(8,128)(2,1)} %get-tuple-element.74.mixed_ref, bf16[2048,512]{1,0:T(8,128)(2,1)} %bitcast.1, ...), custom_call_target="tpu_custom_call" | custom-call | flops 28991029248 | bytes 16777216 | tf_op jit(solution)/shard_map/middle/pallas_call | solution.py:757
  174.7 146.1 %attend_back.1 = (bf16[512,2048]{1,0:T(8,128)(2,1)}, bf16[2048,512]{1,0:T(8,128)(2,1)}, bf16[2048,512]{1,0:T(8,128)(2,1)}, bf16[4608,512]{1,0:T(8,128)(2,1)}, bf...) custom-call(bf16[16,2048,2048]{2,1,0:T(8,128)(2,1)} %get-tuple-element.68.raised_ref, ...), custom_call_target="tpu_custom_call" | custom-call | flops 68719476736 | bytes 134217728 | tf_op jit(solution)/shard_map/attend_back/pallas_call | solution.py:1000
  320.7 74.0 %leave.1 = (bf16[408,768]{1,0:T(8,128)(2,1)}, bf16[1536,512]{1,0:T(8,128)(2,1)}, bf16[896,512]{1,0:T(8,128)(2,1)}) custom-call(bf16[512,2048]{1,0:T(8,128)(2,1)} %get-tuple-element.82.grad_query_ref, bf16[2048,512]{1,0:T(8,128)(2,1)} %get-tuple-element.83.grad_key_ref, bf16[2048,512]{1,0:T(8,128)(2,1)} %get-tuple-element.84.grad_value_ref, ...), custom_call_target="tpu_custom_call" | custom-call | flops 13421772800 | bytes 20971520 | tf_op jit(solution)/shard_map/leave/pallas_call | solution.py:1216
  394.8 0.0 copy-start
  394.8 8.4 %finish.1 = (f32[512,2048]{1,0:T(8,128)}, f32[2048,512]{1,0:T(8,128)}, f32[512,512]{1,0:T(8,128)}, f32[512,1536]{1,0:T(8,128)}, f32[768,512]{1,0:T(8,128)}, /*in...) custom-call(bf16[4608,512]{1,0:T(8,128)(2,1)} %get-tuple-element.91., ...), custom_call_target="tpu_custom_call" | custom-call | bytes 15728640 | tf_op jit(solution)/shard_map/finish/pallas_call | solution.py:1321
  403.2 0.0 copy-done
  403.2 0.0 copy-start.2
  403.2 1.3 copy.41
  404.5 0.1 copy-done.2
  404.7 0.8 copy.42
  (3 shorter events, 0.0 us)
Async XLA Ops:
  49.9 77.5 %all-to-all-start = ((bf16[8,256,512]{2,1,0:T(8,128)(2,1)}), bf16[8,256,512]{2,1,0:T(8,128)(2,1)S(1)}, u32[]{:S(2)}, u32[]{:S(2)}) async-start(bf16[8,256,512]{2,1,0:T(8,128)(2,1)} %param.41), calls=%async_computation | async-start | bytes 4194304 | tf_op jit(solution)/shard_map/all_to_all | solution.py:1391
  127.4 1.3 copy-start.1
  394.8 8.4 %copy-start = (bf16[8,256,512]{2,1,0:T(8,128)(2,1)S(1)}, bf16[8,256,512]{2,1,0:T(8,128)(2,1)}, u32[]{:S(2)}) copy-start(bf16[8,256,512]{2,1,0:T(8,128)(2,1)} %get-tuple-element.132) | copy-start | bytes 6291460
  403.2 1.5 copy-start.2

commit v5 on v4

--- a/solution.py
+++ b/solution.py
@@ -576,7 +576,7 @@
     def run(shifted):
         lag = slices if shifted else min(2, slices)
         steps = PACK * slices
-        highest = {}
+        highest, held = {}, {}
         own_query = partial_highest = mixed = None
         for now in range(steps + lag):
             if now < steps:
@@ -586,7 +586,7 @@
                     own_query = jnp.where(head_row == head, query, jnp.zeros_like(query))
                     partial_highest = jnp.full((8, block), -jnp.inf, jnp.float32)
                 scores = plain_dot(key_ref[part, :], own_query)
-                scores_ref[now % (lag + 1)] = scores
+                held[now] = scores
                 if shifted:
                     partial_highest = jnp.maximum(
                         partial_highest, jnp.max(scores.reshape(slice_rows // 8, 8, block), axis=0)
@@ -597,7 +597,7 @@
                 head, at = divmod(now - lag, slices)
                 rows = slice(head * HEAD_DIM, (head + 1) * HEAD_DIM)
                 part = slice(at * slice_rows, (at + 1) * slice_rows)
-                scores = scores_ref[(now - lag) % (lag + 1)]
+                scores = held.pop(now - lag)
                 if shifted:
                     scores = scores - highest[head]
                 raised = jnp.exp2(scores).astype(jnp.bfloat16)
@@ -695,7 +695,7 @@
     cotangent = cotangent_ref[...]
     middle = (
         stream_ref[...]
-        + plain_dot(turned(mixed_t), output_ref[...])
+        + lead_dot(mixed_t, output_ref[...])
         + vector(OUTPUT_BIAS)
     )
     normed, scale = normalize(middle)
@@ -713,7 +713,7 @@
         grad_hidden = (trail_dot(cotangent, contract_ref[part, :]) * slope).astype(jnp.bfloat16)
         output = output + plain_dot(active, contract_ref[part, :])
         grad_normed = grad_normed + trail_dot(grad_hidden, expand_ref[:, part])
-        contract_sum[part, :] += plain_dot(turned(active), cotangent)
+        contract_sum[part, :] += lead_dot(active, cotangent)
         expand_sum[part, :] += plain_dot(low_t, grad_hidden)
         small_sum[chunk : chunk + 1, :] += column_sum(grad_hidden)
     decoded_ref[...] = output.astype(jnp.bfloat16)
@@ -881,11 +881,11 @@
         pl.semaphore_wait(pltpu.get_barrier_semaphore(), count)
         tree.start()
 
-    @at_step(2)
+    @at_step(4)
     def _():
         tree.near_to_far()
 
-    @at_step(8)
+    @at_step(11)
     def _():
         tree.far_to_deep()
         own_rows().start()
@@ -896,21 +896,21 @@
             share_own(step, spot.peer(step)).start()
         share_own(0, spot.sibling()).start()
 
-    @at_step(12)
+    @at_step(15)
     def _():
         tree.deep_to_layer()
 
-    @at_step(16)
+    @at_step(19)
     def _():
         tree.layer_to_part()
 
-    @at_step(21)
+    @at_step(24)
     def _():
         for step in range(1, spot.half):
             pass_on(step, spot.core, step).wait_recv()
             pass_on(spot.half + step, spot.core, step).start()
 
-    @at_step(26)
+    @at_step(29)
     def _():
         tree.part_to_half()
 
@@ -1075,7 +1075,9 @@
     near_in,
     far_out,
     far_in,
+    latents_all,
     sems,
+    local,
     *sum_refs,
 ):
     block, width = stream_ref.shape
@@ -1083,40 +1085,66 @@
     spot = Spot()
     capacity = back_all.shape[0] // spot.splits
     others = spot.tree()
+    blocks = pl.num_programs(0) // 2
+    count = len(sum_refs) // 2
+    joint_tree = TreeSum(spot, joint_flat, joint_total_ref, sum_refs[:count], True)
+    embed_tree = TreeSum(spot, embed_flat, embed_total_ref, sum_refs[count:], False)
+
+    def load_latents():
+        return pltpu.make_async_copy(latents_ref, latents_all, local)
 
     @pl.when(step_now == 0)
     def _():
         spot.meet(others)
+        load_latents().start()
         joint_sum[...] = jnp.zeros_like(joint_sum)
         small_sum[...] = jnp.zeros_like(small_sum)
 
-    normed, scale = normalize(stream_ref[...])
-    low_t = turned(low_ref[...])
-    sides = [turned(grad_query_ref[...]), grad_key_ref[...], grad_value_ref[...]]
-    grad_normed = jnp.zeros_like(normed)
-    for at, side in enumerate(sides):
-        grad_normed = grad_normed + trail_dot(side, joint_ref[:, at * width : (at + 1) * width])
-        joint_sum[at * width : (at + 1) * width, :] += plain_dot(low_t, side)
-    grad_stream = grad_middle_ref[...] + normalize_back(
-        grad_normed * vector_ref[FIRST_GAIN : FIRST_GAIN + 1, :], normed, scale
-    )
-    grad_all[pl.ds(pl.multiple_of(step_now * block, block), block), :] = grad_stream.astype(
-        jnp.bfloat16
-    )
-    small_sum[0:1, :] += column_sum(empty_ref[...] * grad_stream)
-    small_sum[1:2, :] += column_sum(grad_normed * normed)
-    small_sum[2:3, :] += column_sum(grad_normed)
-    small_sum[3:4, :] += column_sum(sides[0])
-    small_sum[4:5, :] += column_sum(sides[2])
-
-    @pl.when(step_now == pl.num_programs(0) - 1)
-    def _():
-        count = len(sum_refs) // 2
-        joint_tree = TreeSum(spot, joint_flat, joint_total_ref, sum_refs[:count], False)
-        embed_tree = TreeSum(spot, embed_flat, embed_total_ref, sum_refs[count:], False)
-        joint_flat[...] = joint_sum[...].astype(jnp.bfloat16)
+    @pl.when(step_now < blocks)
+    def _():
+        low_t = turned(low_ref[...])
+        sides = [turned(grad_query_ref[...]), grad_key_ref[...], grad_value_ref[...]]
+        for at, side in enumerate(sides):
+            joint_sum[at * width : (at + 1) * width, :] += plain_dot(low_t, side)
+        small_sum[3:4, :] += column_sum(sides[0])
+        small_sum[4:5, :] += column_sum(sides[2])
+
+    @pl.when(step_now == blocks - 1)
+    def _():
+        rows = joint_sum.shape[0]
+        joint_flat[:rows, :] = joint_sum[...].astype(jnp.bfloat16)
+        if joint_flat.shape[0] > rows:
+            joint_flat[rows:, :] = jnp.zeros(
+                (joint_flat.shape[0] - rows, width), jnp.bfloat16
+            )
         pl.semaphore_wait(pltpu.get_barrier_semaphore(), len(others))
         joint_tree.start()
+
+    @pl.when(step_now == blocks + blocks // 4)
+    def _():
+        joint_tree.near_to_far()
+
+    @pl.when(step_now >= blocks)
+    def _():
+        normed, scale = normalize(stream_ref[...])
+        sides = [turned(grad_query_ref[...]), grad_key_ref[...], grad_value_ref[...]]
+        grad_normed = jnp.zeros_like(normed)
+        for at, side in enumerate(sides):
+            grad_normed = grad_normed + trail_dot(
+                side, joint_ref[:, at * width : (at + 1) * width]
+            )
+        grad_stream = grad_middle_ref[...] + normalize_back(
+            grad_normed * vector_ref[FIRST_GAIN : FIRST_GAIN + 1, :], normed, scale
+        )
+        grad_all[pl.ds(pl.multiple_of((step_now - blocks) * block, block), block), :] = (
+            grad_stream.astype(jnp.bfloat16)
+        )
+        small_sum[0:1, :] += column_sum(empty_ref[...] * grad_stream)
+        small_sum[1:2, :] += column_sum(grad_normed * normed)
+        small_sum[2:3, :] += column_sum(grad_normed)
+
+    @pl.when(step_now == pl.num_programs(0) - 1)
+    def _():
         place = lax.broadcasted_iota(jnp.int32, (1, grad_all.shape[0]), 1)
 
         def gathered(owner):
@@ -1146,13 +1174,10 @@
                 spot.peer(step),
             )
 
-        order = list(range(1, spot.half)) + [0]
-        for step in order:
+        for step in list(range(1, spot.half)) + [0]:
             owner = spot.chip_at(step) * 2 + 1 - spot.core
             back_all[rows_of(owner), :] = gathered(owner).astype(jnp.bfloat16)
             near_copy(step).start()
-        joint_tree.near_to_far()
-        for step in order:
             owner = spot.chip_at(step) * 2 + spot.core
             own = gathered(owner)
             back_all[rows_of(owner), :] = own.astype(jnp.bfloat16)
@@ -1161,8 +1186,11 @@
             if step > 0:
                 far_out[part(step - 1), :] = own.astype(jnp.bfloat16)
                 far_copy(step).start()
+            if step == 1:
+                joint_tree.far_to_deep()
+        load_latents().wait()
         embed_rows = embed_ref.shape[0]
-        embed_flat[:embed_rows, :] = lead_dot(latents_ref[...], back_all[...]).astype(jnp.bfloat16)
+        embed_flat[:embed_rows, :] = lead_dot(latents_all[...], back_all[...]).astype(jnp.bfloat16)
         small_sum[5:6, :] = column_sum(back_all[...])
         small = jnp.concatenate([early_ref[...], small_sum[...]], axis=0)
         rest = embed_flat.shape[0] - embed_rows - small.shape[0]
@@ -1170,15 +1198,15 @@
             small = jnp.concatenate([small, jnp.zeros((rest, width), jnp.float32)], axis=0)
         embed_flat[embed_rows:, :] = small.astype(jnp.bfloat16)
         embed_tree.start()
-        joint_tree.far_to_deep()
+        joint_tree.deep_to_layer()
         embed_tree.near_to_far()
+        joint_tree.layer_to_part()
+        embed_tree.far_to_deep()
         for step in range(1, spot.half):
             far_copy(step).wait()
             own = own + far_in[part(step - 1), :].astype(jnp.float32)
         grad_embedded = own[: latent_grad_ref.shape[0]].astype(jnp.bfloat16)
         latent_grad_ref[...] = trail_dot(grad_embedded, embed_ref[...]).astype(jnp.bfloat16)
-        joint_tree.deep_to_layer()
-        embed_tree.far_to_deep()
         joint_tree.part_to_half()
         embed_tree.deep_to_layer()
         joint_tree.finish()
@@ -1209,25 +1237,28 @@
     capacity = slots // splits
     half = splits // 2
     block = min(256, rows)
-    row_block = pl.BlockSpec((block, width), lambda i: (i, 0))
-    lane_block = pl.BlockSpec((width, block), lambda i: (0, i))
-    joint_rows = padded(3 * width, splits * 16)
+    blocks = rows // block
+    row_block = pl.BlockSpec((block, width), lambda i: (i % blocks, 0))
+    first_block = pl.BlockSpec((block, width), lambda i: (jnp.minimum(i, blocks - 1), 0))
+    later_block = pl.BlockSpec((block, width), lambda i: (jnp.maximum(i - blocks, 0), 0))
+    lane_block = pl.BlockSpec((width, block), lambda i: (0, i % blocks))
+    joint_rows = padded(3 * width, splits * layers * 16)
     embed_rows = padded(embed_weight.shape[0] + early_small.shape[0] + 8, splits * 16)
     return pl.pallas_call(
         leave_kernel,
-        grid=(rows // block,),
+        grid=(2 * blocks,),
         in_specs=[
             lane_block,
             row_block,
             row_block,
-            row_block,
-            pl.BlockSpec((block, 1), lambda i: (i, 0)),
-            row_block,
-            row_block,
+            later_block,
+            pl.BlockSpec((block, 1), lambda i: (jnp.maximum(i - blocks, 0), 0)),
+            first_block,
+            later_block,
             whole(vectors.shape),
             whole((width, 3 * width)),
             whole(slot_place.shape),
-            pl.BlockSpec(latents_all.shape, lambda i: (0, 0), pipeline_mode=pl.Buffered(1)),
+            pl.BlockSpec(memory_space=pl.ANY),
             whole(embed_weight.shape),
             whole(early_small.shape),
         ],
@@ -1251,9 +1282,11 @@
             pltpu.VMEM((half * capacity, width), jnp.bfloat16),
             pltpu.VMEM((max(half - 1, 1) * capacity, width), jnp.bfloat16),
             pltpu.VMEM((max(half - 1, 1) * capacity, width), jnp.bfloat16),
+            pltpu.VMEM(latents_all.shape, latents_all.dtype),
             pltpu.SemaphoreType.DMA((2, splits)),
+            pltpu.SemaphoreType.DMA,
         ]
-        + TreeSum.scratch(joint_rows, width, False, splits, layers)
+        + TreeSum.scratch(joint_rows, width, True, splits, layers)
         + TreeSum.scratch(embed_rows, width, False, splits, layers),
         compiler_params=pltpu.CompilerParams(
             vmem_limit_bytes=VMEM_LIMIT, collective_id=2, has_side_effects=True
@@ -1317,7 +1350,7 @@
     chunks = hidden // width
     square = (width, width)
     embed_block = (embed_rows // chunks, width)
-    sides = joint_sum.shape[0] // width
+    sides = 3
     return pl.pallas_call(
         finish_kernel,
         grid=(chunks,),

time: 407 us -> 387 us (0.951)
  Pallas kernels: 393 us -> 373 us
    pallas_call x1, Pallas kernels: 73.9 us -> 61.3 us  [attend(): pl.pallas_call(attend_kernel, grid=(groups, rows // block), in_specs=[pl....]
  transfers between devices with their start and end apart: 1 -> 1, of which waited for: 0 -> 0; matrix products, arithmetic and copies ran while one was open for 0% -> 0% of each run, Pallas kernels for 18% -> 16%
where the time goes in v5:
time: 387 us
  Pallas kernels  373 us (96%)
  local copies, waits for them, and re-layouts  4.4 us (1%)
  other arithmetic  4.02 us (1%)
    pallas_call x1, Pallas kernels, attend_back(): pl.pallas_call(partial(attend_back_kernel, groups * (rows // block)), gri...  143 us
    pallas_call x1, Pallas kernels, leave(): pl.pallas_call(leave_kernel, grid=(2 * blocks,), in_specs=[lane_block, ro...  71.7 us
    pallas_call x1, Pallas kernels, attend(): pl.pallas_call(attend_kernel, grid=(groups, rows // block), in_specs=[pl....  61.3 us
    pallas_call x1, Pallas kernels, enter(): pl.pallas_call(enter_kernel, grid=(rows // block,), in_specs=[whole(laten...  44.3 us
    pallas_call x1, Pallas kernels, middle_block(): pl.pallas_call(middle_kernel, grid=(rows // block,), in_specs=[row_block,...  44.3 us
    pallas_call x1, Pallas kernels, finish(): pl.pallas_call(finish_kernel, grid=(chunks,), in_specs=[pl.BlockSpec(squa...  8.4 us
  transfers between devices with their start and end apart: 1, of which 0 were waited for; matrix products, arithmetic and copies ran while one was open for 0% of the time, Pallas kernels for 16%

profile of v5, /device:TPU:0, one launch (start us, length us, event | category | flops | bytes accessed | tf_op | source)
XLA Modules:
  0.0 386.5 jit_solution(16553556999330934502)
XLA Ops:
  0.7 0.7 fusion.1
  1.4 0.1 eq.15
  1.6 0.7 broadcast_subtract_fusion
  2.3 0.1 sub.16
  2.4 0.7 fusion.3
  3.1 0.6 pad.4.slot_ref
  3.7 0.2 multiply_sine_fusion.1
  3.9 0.3 multiply_sine_fusion
  4.2 0.6 pad_maximum_fusion.1.fine_ref
  4.9 0.7 pad_maximum_fusion.coarse_ref
  5.5 44.3 %enter.1 = (f32[2048,512]{1,0:T(8,128)}, f32[2048,1]{1,0:T(8,128)}, bf16[2048,512]{1,0:T(8,128)(2,1)}, bf16[512,2048]{1,0:T(8,128)(2,1)}, bf16[2048,512]{1,0:T(8...) custom-call(bf16[408,768]{1,0:T(8,128)(2,1)} %latents_ref.1, ...), custom_call_target="tpu_custom_call" | custom-call | flops 10200547328 | bytes 20971520 | tf_op jit(solution)/shard_map/enter/pallas_call | solution.py:484
  49.9 3.8 all-to-all-start
  53.7 61.3 %attend.1 = (bf16[512,2048]{1,0:T(8,128)(2,1)}, f32[512,2048]{1,0:T(8,128)}, f32[4,8,2048]{2,1,0:T(8,128)}, bf16[16,2048,2048]{2,1,0:T(8,128)(2,1)}) custom-call(bf16[2048,512]{1,0:T(8,128)(2,1)} %get-tuple-element.65.key_ref, bf16[512,2048]{1,0:T(8,128)(2,1)} %get-tuple-element.66.query_ref, bf16[512,2048]{1,0:T(8,128)(2,1)} %get-tuple-element.67.value_ref), custom_call_target="tpu_custom_call" | custom-call | flops 34359738368 | bytes 134217728 | tf_op jit(solution)/shard_map/attend/pallas_call | solution.py:629
  115.0 0.0 all-to-all-done
  115.0 0.0 copy-start.1
  115.0 1.3 copy-done.1
  116.4 44.3 %middle.1 = (bf16[2048,512]{1,0:T(8,128)(2,1)}, f32[2048,512]{1,0:T(8,128)}, bf16[512,2048]{1,0:T(8,128)(2,1)}, bf16[4608,512]{1,0:T(8,128)(2,1)}, f32[8,512]{1,0:T(8,128)}) custom-call(f32[2048,512]{1,0:T(8,128)} %get-tuple-element.73.stream_ref, bf16[512,2048]{1,0:T(8,128)(2,1)} %get-tuple-element.74.mixed_ref, bf16[2048,512]{1,0:T(8,128)(2,1)} %bitcast.1, ...), custom_call_target="tpu_custom_call" | custom-call | flops 28991029248 | bytes 16777216 | tf_op jit(solution)/shard_map/middle/pallas_call | solution.py:757
  160.7 143.4 %attend_back.1 = (bf16[512,2048]{1,0:T(8,128)(2,1)}, bf16[2048,512]{1,0:T(8,128)(2,1)}, bf16[2048,512]{1,0:T(8,128)(2,1)}, bf16[4608,512]{1,0:T(8,128)(2,1)}, bf...) custom-call(bf16[16,2048,2048]{2,1,0:T(8,128)(2,1)} %get-tuple-element.68.raised_ref, ...), custom_call_target="tpu_custom_call" | custom-call | flops 68719476736 | bytes 134217728 | tf_op jit(solution)/shard_map/attend_back/pallas_call | solution.py:1000
  304.1 71.7 %leave.1 = (bf16[408,768]{1,0:T(8,128)(2,1)}, bf16[1536,512]{1,0:T(8,128)(2,1)}, bf16[896,512]{1,0:T(8,128)(2,1)}) custom-call(bf16[512,2048]{1,0:T(8,128)(2,1)} %get-tuple-element.82.grad_query_ref, bf16[2048,512]{1,0:T(8,128)(2,1)} %get-tuple-element.83.grad_key_ref, bf16[2048,512]{1,0:T(8,128)(2,1)} %get-tuple-element.84.grad_value_ref, ...), custom_call_target="tpu_custom_call" | custom-call | flops 13421772800 | bytes 20971520 | tf_op jit(solution)/shard_map/leave/pallas_call | solution.py:1247
  375.8 0.0 copy-start
  375.8 8.4 %finish.1 = (f32[512,2048]{1,0:T(8,128)}, f32[2048,512]{1,0:T(8,128)}, f32[512,512]{1,0:T(8,128)}, f32[512,1536]{1,0:T(8,128)}, f32[768,512]{1,0:T(8,128)}, /*in...) custom-call(bf16[4608,512]{1,0:T(8,128)(2,1)} %get-tuple-element.91., ...), custom_call_target="tpu_custom_call" | custom-call | bytes 15728640 | tf_op jit(solution)/shard_map/finish/pallas_call | solution.py:1354
  384.2 0.0 copy-done
  384.2 0.0 copy-start.2
  384.2 1.3 copy.41
  385.6 0.1 copy-done.2
  385.7 0.8 copy.42
  (3 shorter events, 0.0 us)
Async XLA Ops:
  49.9 65.2 %all-to-all-start = ((bf16[8,256,512]{2,1,0:T(8,128)(2,1)}), bf16[8,256,512]{2,1,0:T(8,128)(2,1)S(1)}, u32[]{:S(2)}, u32[]{:S(2)}) async-start(bf16[8,256,512]{2,1,0:T(8,128)(2,1)} %param.41), calls=%async_computation | async-start | bytes 4194304 | tf_op jit(solution)/shard_map/all_to_all | solution.py:1424
  115.0 1.3 copy-start.1
  375.8 8.4 %copy-start = (bf16[8,256,512]{2,1,0:T(8,128)(2,1)S(1)}, bf16[8,256,512]{2,1,0:T(8,128)(2,1)}, u32[]{:S(2)}) copy-start(bf16[8,256,512]{2,1,0:T(8,128)(2,1)} %get-tuple-element.132) | copy-start | bytes 6291460
  384.2 1.5 copy-start.2

commit v6 on v5

--- a/solution.py
+++ b/solution.py
@@ -95,6 +95,31 @@
 
     def above(self, step):
         return (self.layer_at(step), self.index)
+
+    def routes(self):
+        if self.half != 4:
+            steps = range(1, self.half)
+            return (
+                [self.chip_at(-step) for step in steps],
+                [self.peer(step) for step in steps],
+                [self.chip for _ in steps],
+            )
+        across, up = self.chip % 2, self.chip // 2
+        beside = up * 2 + 1 - across
+        above = (1 - up) * 2 + across
+        first = beside * (1 - self.core) + above * self.core
+        second = above * (1 - self.core) + beside * self.core
+        return (
+            [first, second, 3 - self.chip],
+            [(self.layer, chip * 2 + self.core) for chip in (first, second, second)],
+            [self.chip, self.chip, first],
+        )
+
+    def passed_on(self, at):
+        return self.half == 4 and at == 2
+
+    def sibling_turn(self, at):
+        return [1, 0, 2][at] if self.half == 4 else at
 
     def meet(self, others):
         barrier = pltpu.get_barrier_semaphore()
@@ -408,24 +433,37 @@
 
         embedded_ref[span_of(spot.index * capacity, capacity), :] = embedded.astype(jnp.bfloat16)
         pl.semaphore_wait(pltpu.get_barrier_semaphore(), count)
-        for step in range(1, spot.half):
-            share(step, spot.core, spot.chip, spot.peer(step)).start()
+        sources, targets, sent = spot.routes()
+
+        def far(at):
+            return share(1 + at, spot.core, sent[at], targets[at])
+
+        def near(at, core):
+            return share(spot.half + 1 + at, core, sources[at], spot.sibling())
+
+        turns = range(len(targets))
+        for at in turns:
+            if not spot.passed_on(at):
+                far(at).start()
         share(0, spot.core, spot.chip, spot.sibling()).start()
         for source in range(spot.splits):
             slot_row[:, source * capacity : (source + 1) * capacity] = slot_ref[
                 source : source + 1, :capacity
             ]
-        for step in range(1, spot.half):
-            share(step, spot.core, spot.chip_at(-step), spot.peer(step)).wait_recv()
-            share(spot.half + step, spot.core, spot.chip_at(-step), spot.sibling()).start()
-        for step in range(1, spot.half):
-            share(step, spot.core, spot.chip, spot.peer(step)).wait_send()
+        for at in turns:
+            share(1 + at, spot.core, sources[at], targets[at]).wait_recv()
+            if at == 0 and spot.passed_on(2):
+                far(2).start()
+            near(at, spot.core).start()
+        for at in turns:
+            far(at).wait_send()
         share(0, spot.core, spot.chip, spot.sibling()).wait_send()
         share(0, 1 - spot.core, spot.chip, spot.sibling()).wait_recv()
-        for step in range(1, spot.half):
-            at = spot.half + step
-            share(at, spot.core, spot.chip_at(-step), spot.sibling()).wait_send()
-            share(at, 1 - spot.core, spot.chip_at(-step), spot.sibling()).wait_recv()
+        for at in turns:
+            near(at, spot.core).wait_send()
+            share(
+                spot.half + 1 + at, 1 - spot.core, sources[spot.sibling_turn(at)], spot.sibling()
+            ).wait_recv()
 
     place = lax.broadcasted_iota(jnp.int32, (block, 1), 0) + pl.program_id(0) * block
     fills = (place == slot_row[...]).astype(jnp.float32)

time: 387 us -> 385 us (level)
  no operation moved by 1% of the time
where the time goes in v6:
time: 385 us; the launch traced here: 384 us
  Pallas kernels  371 us (96%)
  local copies, waits for them, and re-layouts  4.4 us (1%)
  other arithmetic  4.02 us (1%)
    pallas_call x1, Pallas kernels, attend_back(): pl.pallas_call(partial(attend_back_kernel, groups * (rows // block)), gri...  143 us
    pallas_call x1, Pallas kernels, leave(): pl.pallas_call(leave_kernel, grid=(2 * blocks,), in_specs=[lane_block, ro...  71.7 us
    pallas_call x1, Pallas kernels, attend(): pl.pallas_call(attend_kernel, grid=(groups, rows // block), in_specs=[pl....  61.4 us
    pallas_call x1, Pallas kernels, middle_block(): pl.pallas_call(middle_kernel, grid=(rows // block,), in_specs=[row_block,...  44.3 us
    pallas_call x1, Pallas kernels, enter(): pl.pallas_call(enter_kernel, grid=(rows // block,), in_specs=[whole(laten...  41.6 us
    pallas_call x1, Pallas kernels, finish(): pl.pallas_call(finish_kernel, grid=(chunks,), in_specs=[pl.BlockSpec(squa...  8.4 us
  transfers between devices with their start and end apart: 1, of which 0 were waited for; matrix products, arithmetic and copies ran while one was open for 0% of the time, Pallas kernels for 16%

profile of v6, /device:TPU:0, one launch (start us, length us, event | category | flops | bytes accessed | tf_op | source)
XLA Modules:
  0.0 383.8 jit_solution(9471944863964863369)
XLA Ops:
  0.7 0.7 fusion.1
  1.4 0.1 eq.15
  1.6 0.7 broadcast_subtract_fusion
  2.3 0.1 sub.16
  2.4 0.7 fusion.3
  3.1 0.6 pad.4.slot_ref
  3.7 0.2 multiply_sine_fusion.1
  3.9 0.3 multiply_sine_fusion
  4.2 0.6 pad_maximum_fusion.1.fine_ref
  4.9 0.7 pad_maximum_fusion.coarse_ref
  5.5 41.6 %enter.1 = (f32[2048,512]{1,0:T(8,128)}, f32[2048,1]{1,0:T(8,128)}, bf16[2048,512]{1,0:T(8,128)(2,1)}, bf16[512,2048]{1,0:T(8,128)(2,1)}, bf16[2048,512]{1,0:T(8...) custom-call(bf16[408,768]{1,0:T(8,128)(2,1)} %latents_ref.1, ...), custom_call_target="tpu_custom_call" | custom-call | flops 10200547328 | bytes 20971520 | tf_op jit(solution)/shard_map/enter/pallas_call | solution.py:522
  47.2 3.8 all-to-all-start
  51.0 61.4 %attend.1 = (bf16[512,2048]{1,0:T(8,128)(2,1)}, f32[512,2048]{1,0:T(8,128)}, f32[4,8,2048]{2,1,0:T(8,128)}, bf16[16,2048,2048]{2,1,0:T(8,128)(2,1)}) custom-call(bf16[2048,512]{1,0:T(8,128)(2,1)} %get-tuple-element.65.key_ref, bf16[512,2048]{1,0:T(8,128)(2,1)} %get-tuple-element.66.query_ref, bf16[512,2048]{1,0:T(8,128)(2,1)} %get-tuple-element.67.value_ref), custom_call_target="tpu_custom_call" | custom-call | flops 34359738368 | bytes 134217728 | tf_op jit(solution)/shard_map/attend/pallas_call | solution.py:667
  112.3 0.0 all-to-all-done
  112.3 0.0 copy-start.1
  112.3 1.3 copy-done.1
  113.6 44.3 %middle.1 = (bf16[2048,512]{1,0:T(8,128)(2,1)}, f32[2048,512]{1,0:T(8,128)}, bf16[512,2048]{1,0:T(8,128)(2,1)}, bf16[4608,512]{1,0:T(8,128)(2,1)}, f32[8,512]{1,0:T(8,128)}) custom-call(f32[2048,512]{1,0:T(8,128)} %get-tuple-element.73.stream_ref, bf16[512,2048]{1,0:T(8,128)(2,1)} %get-tuple-element.74.mixed_ref, bf16[2048,512]{1,0:T(8,128)(2,1)} %bitcast.1, ...), custom_call_target="tpu_custom_call" | custom-call | flops 28991029248 | bytes 16777216 | tf_op jit(solution)/shard_map/middle/pallas_call | solution.py:795
  158.0 143.4 %attend_back.1 = (bf16[512,2048]{1,0:T(8,128)(2,1)}, bf16[2048,512]{1,0:T(8,128)(2,1)}, bf16[2048,512]{1,0:T(8,128)(2,1)}, bf16[4608,512]{1,0:T(8,128)(2,1)}, bf...) custom-call(bf16[16,2048,2048]{2,1,0:T(8,128)(2,1)} %get-tuple-element.68.raised_ref, ...), custom_call_target="tpu_custom_call" | custom-call | flops 68719476736 | bytes 134217728 | tf_op jit(solution)/shard_map/attend_back/pallas_call | solution.py:1038
  301.4 71.7 %leave.1 = (bf16[408,768]{1,0:T(8,128)(2,1)}, bf16[1536,512]{1,0:T(8,128)(2,1)}, bf16[896,512]{1,0:T(8,128)(2,1)}) custom-call(bf16[512,2048]{1,0:T(8,128)(2,1)} %get-tuple-element.82.grad_query_ref, bf16[2048,512]{1,0:T(8,128)(2,1)} %get-tuple-element.83.grad_key_ref, bf16[2048,512]{1,0:T(8,128)(2,1)} %get-tuple-element.84.grad_value_ref, ...), custom_call_target="tpu_custom_call" | custom-call | flops 13421772800 | bytes 20971520 | tf_op jit(solution)/shard_map/leave/pallas_call | solution.py:1285
  373.1 0.0 copy-start
  373.1 8.4 %finish.1 = (f32[512,2048]{1,0:T(8,128)}, f32[2048,512]{1,0:T(8,128)}, f32[512,512]{1,0:T(8,128)}, f32[512,1536]{1,0:T(8,128)}, f32[768,512]{1,0:T(8,128)}, /*in...) custom-call(bf16[4608,512]{1,0:T(8,128)(2,1)} %get-tuple-element.91., ...), custom_call_target="tpu_custom_call" | custom-call | bytes 15728640 | tf_op jit(solution)/shard_map/finish/pallas_call | solution.py:1392
  381.5 0.0 copy-done
  381.5 0.0 copy-start.2
  381.5 1.3 copy.41
  382.8 0.1 copy-done.2
  383.0 0.8 copy.42
  (3 shorter events, 0.0 us)
Async XLA Ops:
  47.2 65.2 %all-to-all-start = ((bf16[8,256,512]{2,1,0:T(8,128)(2,1)}), bf16[8,256,512]{2,1,0:T(8,128)(2,1)S(1)}, u32[]{:S(2)}, u32[]{:S(2)}) async-start(bf16[8,256,512]{2,1,0:T(8,128)(2,1)} %param.41), calls=%async_computation | async-start | bytes 4194304 | tf_op jit(solution)/shard_map/all_to_all | solution.py:1462
  112.3 1.3 copy-start.1
  373.1 8.4 %copy-start = (bf16[8,256,512]{2,1,0:T(8,128)(2,1)S(1)}, bf16[8,256,512]{2,1,0:T(8,128)(2,1)}, u32[]{:S(2)}) copy-start(bf16[8,256,512]{2,1,0:T(8,128)(2,1)} %get-tuple-element.132) | copy-start | bytes 6291460
  381.5 1.5 copy-start.2

commit v7 on v6

--- a/solution.py
+++ b/solution.py
@@ -511,7 +511,7 @@
     capacity = padded(latents.shape[0], 16)
     slots = splits * capacity
     vector_rows = sum(vector.shape[0] for vector in vectors) // width
-    block = min(256, rows)
+    block = min(512, rows)
     fine_rows = min(32, block)
     fine = sinusoid(jnp.arange(fine_rows, dtype=jnp.int32), width)
     coarse = sinusoid(first_place + fine_rows * jnp.arange(rows // fine_rows, dtype=jnp.int32), width)
@@ -788,7 +788,7 @@
 ):
     rows, width = stream.shape
     hidden = expand_weight.shape[1]
-    block = min(256, rows)
+    block = min(512, rows)
     row_block = pl.BlockSpec((block, width), lambda i: (i, 0))
     lane_block = pl.BlockSpec((width, block), lambda i: (0, i))
     small_rows = hidden // width + 4

time: 385 us -> 386 us (level)
  no operation moved by 1% of the time
where the time goes in v7:
time: 386 us; the launch traced here: 381 us
  Pallas kernels  368 us (95%)
  local copies, waits for them, and re-layouts  4.4 us (1%)
  other arithmetic  4.02 us (1%)
    pallas_call x1, Pallas kernels, attend_back(): pl.pallas_call(partial(attend_back_kernel, groups * (rows // block)), gri...  144 us
    pallas_call x1, Pallas kernels, leave(): pl.pallas_call(leave_kernel, grid=(2 * blocks,), in_specs=[lane_block, ro...  71.8 us
    pallas_call x1, Pallas kernels, attend(): pl.pallas_call(attend_kernel, grid=(groups, rows // block), in_specs=[pl....  61.4 us
    pallas_call x1, Pallas kernels, middle_block(): pl.pallas_call(middle_kernel, grid=(rows // block,), in_specs=[row_block,...  42.8 us
    pallas_call x1, Pallas kernels, enter(): pl.pallas_call(enter_kernel, grid=(rows // block,), in_specs=[whole(laten...  39.8 us
    pallas_call x1, Pallas kernels, finish(): pl.pallas_call(finish_kernel, grid=(chunks,), in_specs=[pl.BlockSpec(squa...  8.4 us
  transfers between devices with their start and end apart: 1, of which 0 were waited for; matrix products, arithmetic and copies ran while one was open for 0% of the time, Pallas kernels for 16%

profile of v7, /device:TPU:0, one launch (start us, length us, event | category | flops | bytes accessed | tf_op | source)
XLA Modules:
  0.0 381.2 jit_solution(10549628053405441524)
XLA Ops:
  0.7 0.7 fusion.1
  1.5 0.1 eq.15
  1.6 0.7 broadcast_subtract_fusion
  2.3 0.1 sub.16
  2.4 0.7 fusion.3
  3.1 0.6 pad.4.slot_ref
  3.7 0.2 multiply_sine_fusion.1
  3.9 0.3 multiply_sine_fusion
  4.2 0.6 pad_maximum_fusion.1.fine_ref
  4.9 0.7 pad_maximum_fusion.coarse_ref
  5.5 39.8 %enter.1 = (f32[2048,512]{1,0:T(8,128)}, f32[2048,1]{1,0:T(8,128)}, bf16[2048,512]{1,0:T(8,128)(2,1)}, bf16[512,2048]{1,0:T(8,128)(2,1)}, bf16[2048,512]{1,0:T(8...) custom-call(bf16[408,768]{1,0:T(8,128)(2,1)} %latents_ref.1, ...), custom_call_target="tpu_custom_call" | custom-call | flops 10200547328 | bytes 20971520 | tf_op jit(solution)/shard_map/enter/pallas_call | solution.py:522
  45.3 3.8 all-to-all-start
  49.1 61.4 %attend.1 = (bf16[512,2048]{1,0:T(8,128)(2,1)}, f32[512,2048]{1,0:T(8,128)}, f32[4,8,2048]{2,1,0:T(8,128)}, bf16[16,2048,2048]{2,1,0:T(8,128)(2,1)}) custom-call(bf16[2048,512]{1,0:T(8,128)(2,1)} %get-tuple-element.65.key_ref, bf16[512,2048]{1,0:T(8,128)(2,1)} %get-tuple-element.66.query_ref, bf16[512,2048]{1,0:T(8,128)(2,1)} %get-tuple-element.67.value_ref), custom_call_target="tpu_custom_call" | custom-call | flops 34359738368 | bytes 134217728 | tf_op jit(solution)/shard_map/attend/pallas_call | solution.py:667
  110.5 0.0 all-to-all-done
  110.5 0.0 copy-start.1
  110.5 1.3 copy-done.1
  111.8 42.8 %middle.1 = (bf16[2048,512]{1,0:T(8,128)(2,1)}, f32[2048,512]{1,0:T(8,128)}, bf16[512,2048]{1,0:T(8,128)(2,1)}, bf16[4608,512]{1,0:T(8,128)(2,1)}, f32[8,512]{1,0:T(8,128)}) custom-call(f32[2048,512]{1,0:T(8,128)} %get-tuple-element.73.stream_ref, bf16[512,2048]{1,0:T(8,128)(2,1)} %get-tuple-element.74.mixed_ref, bf16[2048,512]{1,0:T(8,128)(2,1)} %bitcast.1, ...), custom_call_target="tpu_custom_call" | custom-call | flops 28991029248 | bytes 16777216 | tf_op jit(solution)/shard_map/middle/pallas_call | solution.py:795
  154.6 143.6 %attend_back.1 = (bf16[512,2048]{1,0:T(8,128)(2,1)}, bf16[2048,512]{1,0:T(8,128)(2,1)}, bf16[2048,512]{1,0:T(8,128)(2,1)}, bf16[4608,512]{1,0:T(8,128)(2,1)}, bf...) custom-call(bf16[16,2048,2048]{2,1,0:T(8,128)(2,1)} %get-tuple-element.68.raised_ref, ...), custom_call_target="tpu_custom_call" | custom-call | flops 68719476736 | bytes 134217728 | tf_op jit(solution)/shard_map/attend_back/pallas_call | solution.py:1038
  298.3 71.8 %leave.1 = (bf16[408,768]{1,0:T(8,128)(2,1)}, bf16[1536,512]{1,0:T(8,128)(2,1)}, bf16[896,512]{1,0:T(8,128)(2,1)}) custom-call(bf16[512,2048]{1,0:T(8,128)(2,1)} %get-tuple-element.82.grad_query_ref, bf16[2048,512]{1,0:T(8,128)(2,1)} %get-tuple-element.83.grad_key_ref, bf16[2048,512]{1,0:T(8,128)(2,1)} %get-tuple-element.84.grad_value_ref, ...), custom_call_target="tpu_custom_call" | custom-call | flops 13421772800 | bytes 20971520 | tf_op jit(solution)/shard_map/leave/pallas_call | solution.py:1285
  370.0 0.0 copy-start
  370.0 8.4 %finish.1 = (f32[512,2048]{1,0:T(8,128)}, f32[2048,512]{1,0:T(8,128)}, f32[512,512]{1,0:T(8,128)}, f32[512,1536]{1,0:T(8,128)}, f32[768,512]{1,0:T(8,128)}, /*in...) custom-call(bf16[4608,512]{1,0:T(8,128)(2,1)} %get-tuple-element.91., ...), custom_call_target="tpu_custom_call" | custom-call | bytes 15728640 | tf_op jit(solution)/shard_map/finish/pallas_call | solution.py:1392
  378.5 0.0 copy-done
  378.5 0.0 copy-start.2
  378.5 1.3 copy.41
  379.8 0.1 copy-done.2
  379.9 0.8 copy.42
  (3 shorter events, 0.0 us)
Async XLA Ops:
  45.3 65.2 %all-to-all-start = ((bf16[8,256,512]{2,1,0:T(8,128)(2,1)}), bf16[8,256,512]{2,1,0:T(8,128)(2,1)S(1)}, u32[]{:S(2)}, u32[]{:S(2)}) async-start(bf16[8,256,512]{2,1,0:T(8,128)(2,1)} %param.41), calls=%async_computation | async-start | bytes 4194304 | tf_op jit(solution)/shard_map/all_to_all | solution.py:1462
  110.5 1.3 copy-start.1
  370.0 8.4 %copy-start = (bf16[8,256,512]{2,1,0:T(8,128)(2,1)S(1)}, bf16[8,256,512]{2,1,0:T(8,128)(2,1)}, u32[]{:S(2)}) copy-start(bf16[8,256,512]{2,1,0:T(8,128)(2,1)} %get-tuple-element.132) | copy-start | bytes 6291460
  378.5 1.5 copy-start.2
